TPU v7x, 32 devices: a whole 2x2x4 slice. The times are simulated.
32 devices in a mesh: wide: 8 (over y, x, core), narrow: 4 (over z).
Axes of the slice: x: 2, y: 2, z: 4, core: 2. Of those that a mesh axis runs over, the one named last changes fastest.
Arguments:
- patches: bfloat16 [6400, 4, 512], P(('wide', 'narrow')), may hold values from -6 to 6
- window_extent: int32 [64, 2], P('wide'), may hold values from 1 to 10, as said below
- merge_gain: float32 [2048], replicated, may hold values from 0.5 to 1.5
- merge_shift: float32 [2048], replicated, may hold values from -2 to 2
- merge_weight: bfloat16 [2048, 1024], replicated, may hold values from -0.125 to 0.125
- norm1_gain: float32 [1024], replicated, may hold values from 0.5 to 1.5
- norm1_shift: float32 [1024], replicated, may hold values from -2 to 2
- qkv_weight: bfloat16 [1024, 3072], replicated, may hold values from -0.25 to 0.25
- qkv_bias: float32 [3072], replicated, may hold values from -2 to 2
- rel_table: float32 [361, 32], P(None, 'narrow'), may hold values from -4 to 4
- proj_weight: bfloat16 [1024, 1024], P('narrow'), may hold values from -0.5 to 0.5
- proj_bias: float32 [1024], replicated, may hold values from -2 to 2
- norm2_gain: float32 [1024], replicated, may hold values from 0.5 to 1.5
- norm2_shift: float32 [1024], replicated, may hold values from -2 to 2
- fc1_weight: bfloat16 [1024, 4096], P(None, 'narrow'), may hold values from -0.1875 to 0.1875
- fc1_bias: float32 [4096], P('narrow'), may hold values from -2 to 2
- fc2_weight: bfloat16 [4096, 1024], P('narrow'), may hold values from -0.125 to 0.125
- fc2_bias: float32 [1024], replicated, may hold values from -2 to 2
- out_grad: bfloat16 [6400, 1024], P('wide'), may hold values from -6 to 6
Outputs:
- output: bfloat16 [6400, 1024], P(('wide', 'narrow'))
- patches_grad: bfloat16 [6400, 4, 512], P(('wide', 'narrow'))
- merge_gain_grad: float32 [2048], replicated
- merge_shift_grad: float32 [2048], replicated
- merge_weight_grad: float32 [2048, 1024], P(('wide', 'narrow'))
- norm1_gain_grad: float32 [1024], replicated
- norm1_shift_grad: float32 [1024], replicated
- qkv_weight_grad: float32 [1024, 3072], P(('wide', 'narrow'))
- qkv_bias_grad: float32 [3072], replicated
- rel_table_grad: float32 [361, 32], replicated
- proj_weight_grad: float32 [1024, 1024], P(('narrow', 'wide'))
- proj_bias_grad: float32 [1024], replicated
- norm2_gain_grad: float32 [1024], replicated
- norm2_shift_grad: float32 [1024], replicated
- fc1_weight_grad: float32 [1024, 4096], P('wide', 'narrow')
- fc1_bias_grad: float32 [4096], P(('narrow', 'wide'))
- fc2_weight_grad: float32 [4096, 1024], P(('narrow', 'wide'))
- fc2_bias_grad: float32 [1024], replicated
Inputs may be any that keep to these rules, and one draw needn't show every extreme that they name: `window_extent`: each window's rows and columns on its page; many windows are whole, and window 0 is.
All inputs are finite; a program needn't handle non-finite values.
Results may differ from a plain program's by a relative error of at most 0.02.
Values may be sent and summed in bfloat16 or wider, within the bound.
No kernel may reach another device: no remote copies, remote signals or barrier semaphores. Data moves between devices by JAX's collectives and lax.ppermute only.
A program may use at most 128 MiB of HBM per device.

v0:
```python
import jax
import jax.numpy as jnp
from jax import lax
from jax.sharding import PartitionSpec as P

WIN = 10


EPS = 1e-05


def norm_forward(values, gain, shift):
    average = jnp.mean(values, -1, keepdims=True)
    centred = values - average
    inverse = lax.rsqrt(jnp.mean(centred * centred, -1, keepdims=True) + EPS)
    normal = centred * inverse
    return (normal, inverse, normal * gain + shift)


def norm_backward(grad_out, normal, inverse, gain):
    scaled = grad_out * gain
    return inverse * (
        scaled
        - jnp.mean(scaled, -1, keepdims=True)
        - normal * jnp.mean(scaled * normal, -1, keepdims=True)
    )


def matmul(left, right):
    return jnp.dot(left, right, preferred_element_type=jnp.float32)


def contract(left, right, left_dim, right_dim):
    return lax.dot_general(
        left, right, (((left_dim,), (right_dim,)), ((), ())), preferred_element_type=jnp.float32
    )


def exact_gelu(values):
    return jax.nn.gelu(values, approximate=False)


def on_device(
    patches,
    window_extent,
    merge_gain,
    merge_shift,
    merge_weight,
    norm1_gain,
    norm1_shift,
    qkv_weight,
    qkv_bias,
    rel_table,
    proj_weight,
    proj_bias,
    norm2_gain,
    norm2_shift,
    fc1_weight,
    fc1_bias,
    fc2_weight,
    fc2_bias,
    out_grad,
):
    groups = lax.axis_size("narrow")
    my_rank = lax.axis_index("narrow")
    tok_dev = patches.shape[0]
    rows_all = tok_dev * groups
    local_heads = rel_table.shape[1]
    model_width = qkv_weight.shape[0]
    head_dim = model_width // (local_heads * groups)
    width = local_heads * head_dim
    window_tokens = WIN * WIN
    windows = rows_all // window_tokens
    scale = head_dim ** (-0.5)
    flat_in = patches.reshape(tok_dev, -1).astype(jnp.float32)
    merge_hat, merge_inv, merge_out = norm_forward(flat_in, merge_gain, merge_shift)
    merged = merge_out.astype(jnp.bfloat16)
    resid0 = matmul(merged, merge_weight)
    hat1, inv1, out1 = norm_forward(resid0, norm1_gain, norm1_shift)
    normed1 = out1.astype(jnp.bfloat16)
    qkv_local = (matmul(normed1, qkv_weight) + qkv_bias).astype(jnp.bfloat16)
    packed = qkv_local.reshape(tok_dev, 3, groups, width)
    regrouped = lax.all_to_all(packed, "narrow", split_axis=2, concat_axis=0, tiled=True)
    qkv_win = regrouped.reshape(windows, window_tokens, 3, local_heads, head_dim)
    query = qkv_win[:, :, 0]
    keys = qkv_win[:, :, 1]
    values_win = qkv_win[:, :, 2]
    positions = jnp.arange(window_tokens)
    pos_row = positions // WIN
    pos_col = positions % WIN
    offsets = (
        (pos_row[:, None] - pos_row[None, :] + WIN - 1) * (2 * WIN - 1)
        + pos_col[:, None]
        - pos_col[None, :]
        + WIN
        - 1
    ).reshape(-1)
    onehot = (offsets[:, None] == jnp.arange(rel_table.shape[0])[None, :]).astype(jnp.float32)
    bias_flat = jnp.dot(onehot, rel_table, precision=lax.Precision.HIGHEST)
    bias_heads = jnp.transpose(
        bias_flat.reshape(window_tokens, window_tokens, local_heads), (2, 0, 1)
    )
    valid = (pos_row[None, :] < window_extent[:, 0:1]) & (pos_col[None, :] < window_extent[:, 1:2])

    def masked_scores():
        raw = (
            jnp.einsum("wqhd,wkhd->whqk", query, keys, preferred_element_type=jnp.float32) * scale
            + bias_heads[None]
        )
        return jnp.where(valid[:, None, None, :], raw, -1e30)

    scores = masked_scores()
    peak = jnp.max(scores, -1, keepdims=True)
    expo = jnp.exp(scores - peak)
    total = jnp.sum(expo, -1, keepdims=True)
    log_total = peak + jnp.log(total)
    probs_low = (expo / total).astype(jnp.bfloat16)
    heads_out = (
        jnp.einsum("whqk,wkhd->wqhd", probs_low, values_win, preferred_element_type=jnp.float32)
        .astype(jnp.bfloat16)
        .reshape(rows_all, width)
    )
    attn_part = matmul(heads_out, proj_weight)
    attn_own = lax.psum_scatter(
        attn_part.astype(jnp.bfloat16), "narrow", scatter_dimension=0, tiled=True
    ).astype(jnp.float32)
    resid1 = resid0 + attn_own + proj_bias
    grad_own = lax.dynamic_slice_in_dim(out_grad, my_rank * tok_dev, tok_dev, 0).astype(jnp.float32)
    hat2, inv2, out2 = norm_forward(resid1, norm2_gain, norm2_shift)
    normed2_all = lax.all_gather(out2.astype(jnp.bfloat16), "narrow", axis=0, tiled=True)
    pre = matmul(normed2_all, fc1_weight) + fc1_bias
    act = exact_gelu(pre).astype(jnp.bfloat16)
    pre, act, fc2_part = (pre, act, matmul(act, fc2_weight))
    fc2_own = lax.psum_scatter(
        fc2_part.astype(jnp.bfloat16), "narrow", scatter_dimension=0, tiled=True
    ).astype(jnp.float32)
    output = (resid1 + fc2_own + fc2_bias).astype(jnp.bfloat16)
    d_act = contract(out_grad, fc2_weight, 1, 1)
    d_pre = jax.vjp(exact_gelu, pre)[1](d_act)[0].astype(jnp.bfloat16)
    fc1_w_grad = contract(normed2_all, d_pre, 0, 0)
    fc1_b_grad = jnp.sum(d_pre.astype(jnp.float32), 0)
    fc2_w_grad = contract(act, out_grad, 0, 0)
    d_norm2_part = contract(d_pre, fc1_weight, 1, 1)
    d_norm2 = lax.psum_scatter(
        d_norm2_part.astype(jnp.bfloat16), "narrow", scatter_dimension=0, tiled=True
    ).astype(jnp.float32)
    d_resid1 = grad_own + norm_backward(d_norm2, hat2, inv2, norm2_gain)
    d_branch = lax.all_gather(d_resid1.astype(jnp.bfloat16), "narrow", axis=0, tiled=True)
    proj_w_grad = contract(heads_out, d_branch, 0, 0)
    d_heads = (
        contract(d_branch, proj_weight, 1, 1)
        .astype(jnp.bfloat16)
        .reshape(windows, window_tokens, local_heads, head_dim)
    )
    probs = jnp.exp(masked_scores() - log_total)
    probs_again = probs.astype(jnp.bfloat16)
    d_probs = jnp.einsum("wqhd,wkhd->whqk", d_heads, values_win, preferred_element_type=jnp.float32)
    row_dot = jnp.sum(d_probs * probs, -1, keepdims=True)
    d_scores = (probs * (d_probs - row_dot)).astype(jnp.bfloat16)
    d_bias = jnp.sum(d_scores.astype(jnp.float32), 0)
    d_bias_flat = jnp.transpose(d_bias, (1, 2, 0)).reshape(
        window_tokens * window_tokens, local_heads
    )
    rel_part = lax.dot_general(
        onehot, d_bias_flat, (((0,), (0,)), ((), ())), precision=lax.Precision.HIGHEST
    )
    d_query = (
        jnp.einsum("whqk,wkhd->wqhd", d_scores, keys, preferred_element_type=jnp.float32) * scale
    )
    d_keys = (
        jnp.einsum("whqk,wqhd->wkhd", d_scores, query, preferred_element_type=jnp.float32) * scale
    )
    d_values = jnp.einsum(
        "whqk,wqhd->wkhd", probs_again, d_heads, preferred_element_type=jnp.float32
    )
    d_packed = (
        jnp.stack([d_query, d_keys, d_values], 2)
        .astype(jnp.bfloat16)
        .reshape(rows_all, 3, 1, width)
    )
    returned = lax.all_to_all(d_packed, "narrow", split_axis=0, concat_axis=2, tiled=True).reshape(
        tok_dev, -1
    )
    qkv_b_grad = jnp.sum(returned.astype(jnp.float32), 0)
    d_norm1 = contract(returned, qkv_weight, 1, 1)
    d_resid0 = (d_resid1 + norm_backward(d_norm1, hat1, inv1, norm1_gain)).astype(jnp.bfloat16)
    merge_w_grad = contract(merged, d_resid0, 0, 0)
    d_merged = contract(d_resid0, merge_weight, 1, 1)
    d_flat = norm_backward(d_merged, merge_hat, merge_inv, merge_gain)
    patches_grad = d_flat.astype(jnp.bfloat16).reshape(patches.shape)
    rel_full = lax.dynamic_update_slice(
        jnp.zeros((rel_table.shape[0], local_heads * groups), jnp.float32),
        rel_part,
        (jnp.int32(0), my_rank * local_heads),
    )
    qkv_w_grad = contract(normed1, returned, 0, 0)
    tensor = (
        lax.psum_scatter(proj_w_grad, "wide", scatter_dimension=0, tiled=True),
        lax.psum_scatter(fc1_w_grad, "wide", scatter_dimension=0, tiled=True),
        lax.psum_scatter(fc2_w_grad, "wide", scatter_dimension=0, tiled=True),
        lax.psum_scatter(fc1_b_grad, "wide", scatter_dimension=0, tiled=True),
    )
    shared = (
        lax.psum_scatter(merge_w_grad, ("wide", "narrow"), scatter_dimension=0, tiled=True),
        lax.psum_scatter(qkv_w_grad, ("wide", "narrow"), scatter_dimension=0, tiled=True),
    )
    merge_out_grad = shared[0]
    qkv_out_grad = shared[1]
    vectors = lax.psum(
        (
            jnp.sum(d_merged * merge_hat, 0),
            jnp.sum(d_merged, 0),
            jnp.sum(d_norm1 * hat1, 0),
            jnp.sum(d_norm1, 0),
            qkv_b_grad,
            rel_full,
            jnp.sum(d_resid1, 0),
            jnp.sum(d_norm2 * hat2, 0),
            jnp.sum(d_norm2, 0),
            jnp.sum(grad_own, 0),
        ),
        ("wide", "narrow"),
    )
    return (
        output,
        patches_grad,
        vectors[0],
        vectors[1],
        merge_out_grad,
        vectors[2],
        vectors[3],
        qkv_out_grad,
        vectors[4],
        vectors[5],
        tensor[0],
        vectors[6],
        vectors[7],
        vectors[8],
        tensor[1],
        tensor[3],
        tensor[2],
        vectors[9],
    )


def solution(mesh):
    in_specs = (
        P(("wide", "narrow"), None, None),
        P("wide", None),
        P(),
        P(),
        P(),
        P(),
        P(),
        P(),
        P(),
        P(None, "narrow"),
        P("narrow", None),
        P(),
        P(),
        P(),
        P(None, "narrow"),
        P("narrow"),
        P("narrow", None),
        P(),
        P("wide", None),
    )
    out_specs = (
        P(("wide", "narrow"), None),
        P(("wide", "narrow"), None, None),
        P(),
        P(),
        P(("wide", "narrow"), None),
        P(),
        P(),
        P(("wide", "narrow"), None),
        P(),
        P(),
        P(("narrow", "wide"), None),
        P(),
        P(),
        P(),
        P("wide", "narrow"),
        P(("narrow", "wide")),
        P(("narrow", "wide"), None),
        P(),
    )
    return jax.shard_map(
        on_device, mesh=mesh, in_specs=in_specs, out_specs=out_specs, check_vma=False
    )
```

profile of v0, /device:TPU:0, one launch (start us, length us, event | category | flops | bytes accessed | tf_op | source)
XLA Modules:
  0.0 942.2 jit_solution(10738546722964309004)
XLA Ops:
  26.8 6.3 all-to-all-start
  33.9 7.6 fusion.1
  45.5 17.2 %all-to-all-done = bf16[200,3,4,256]{3,0,1,2:T(8,128)(2,1)S(1)} async-done(((bf16[200,3,4,256]{3,0,1,2:T(8,128)(2,1)}), bf16[200,3,4,256]{3,0,1,2:T(8,128)(2,1)S(1)}, u32[]{:S(2)}, u32[]{:S(2)}) %all-to-all-start) | async-done | bytes 1228832 | tf_op jit(solution)/shard_map/all_to_all | solution.py:83
  64.9 3.9 reshape.328
  78.2 35.5 %reduce-scatter.9.cloned.1.call-done = bf16[200,1024]{1,0:T(8,128)(2,1)} async-done(((bf16[800,1024]{1,0:T(8,128)(2,1)}), bf16[200,1024]{1,0:T(8,128)(2,1)}) %reduce-scatter.9.cloned.1.call-update) | async-done | bytes 409616 | tf_op jit(solution)/shard_map/reduce_scatter | solution.py:124
  116.6 37.1 %all-gather.3.cloned.1.call-done = bf16[800,1024]{1,0:T(8,128)(2,1)} async-done(((bf16[200,1024]{1,0:T(8,128)(2,1)}), bf16[800,1024]{1,0:T(8,128)(2,1)}) %all-gather.3.cloned.1.call-update) | async-done | bytes 1638416 | tf_op jit(solution)/shard_map/all_gather | solution.py:130
  153.7 4.1 fusion.49
  157.9 10.4 %convert_reduce_fusion.1 = (f32[1024]{0:T(1024)S(1)}, bf16[800,1024]{1,0:T(8,128)(2,1)S(1)}, f32[800,1024]{1,0:T(8,128)}) fusion(f32[800,1024]{1,0:T(8,128)S(1)} %fusion.49, f32[1024]{0:T(1024)S(1)} %copy-done.34, bf16[800,1024]{1,0:T(8,128)(2,1)S(1)} %copy-done.27, bf16[1024,1024]{1,0:T(8,128)(2,1)S(1)} %copy-done), kind=kOutput, calls=%fused_computation.16 | convolution fusion | flops 1739160576 | bytes 11935744 | tf_op jit(solution)/shard_map/dot_general | solution.py:34
  172.7 3.8 multiply_convert_fusion.1
  180.8 27.2 %reduce-scatter.13.cloned.1.call-done = bf16[200,1024]{1,0:T(8,128)(2,1)} async-done(((bf16[800,1024]{1,0:T(8,128)(2,1)}), bf16[200,1024]{1,0:T(8,128)(2,1)}) %reduce-scatter.13.cloned.1.call-update) | async-done | bytes 409616 | tf_op jit(solution)/shard_map/reduce_scatter | solution.py:144
  210.0 35.5 %reduce-scatter.11.cloned.1.call-done = bf16[200,1024]{1,0:T(8,128)(2,1)} async-done(((bf16[800,1024]{1,0:T(8,128)(2,1)}), bf16[200,1024]{1,0:T(8,128)(2,1)}) %reduce-scatter.11.cloned.1.call-update) | async-done | bytes 409616 | tf_op jit(solution)/shard_map/reduce_scatter | solution.py:134
  250.4 5.8 fusion.51
  258.2 4.4 fusion.52
  262.6 25.0 %all-gather.5.cloned.1.call-done = bf16[800,1024]{1,0:T(8,128)(2,1)} async-done(((bf16[200,1024]{1,0:T(8,128)(2,1)}), bf16[800,1024]{1,0:T(8,128)(2,1)}) %all-gather.5.cloned.1.call-update) | async-done | bytes 1638416 | tf_op jit(solution)/shard_map/all_gather | solution.py:148
  322.7 5.1 fusion.32
  327.8 29.3 %all-to-all-done.1 = bf16[800,3,1,256]{3,1,2,0:T(4,128)(2,1)S(1)} async-done(((bf16[800,3,1,256]{3,1,2,0:T(4,128)(2,1)}), bf16[800,3,1,256]{3,1,2,0:T(4,128)(2,1)S(1)}, u32[]{:S(2)}, u32[]{:S(2)}) %all-to-all-start.1) | async-done | bytes 1228832 | tf_op jit(solution)/shard_map/all_to_all | solution.py:181
  360.5 6.3 multiply_reduce_fusion.5
  370.8 4.6 fusion.41
  376.8 6.6 fusion.40
  385.3 13.2 %all-reduce = f32[1024]{0:T(1024)S(1)} all-reduce(f32[1024]{0:T(1024)S(1)} %get-tuple-element.40), channel_id=9, replica_groups=mesh['wide'=8,'narrow'=4] {'wide'}, use_global_device_ids=true, to_apply=%region_41.42.clone | all-reduce | flops 1024 | bytes 8192
  403.1 34.5 %reduce-scatter.19.cloned.1.call-done = f32[32,1024]{1,0:T(8,128)} async-done(((f32[256,1024]{1,0:T(8,128)}), f32[32,1024]{1,0:T(8,128)}) %reduce-scatter.19.cloned.1.call-update) | async-done | bytes 131088 | tf_op jit(solution)/shard_map/reduce_scatter | solution.py:198
  437.6 135.4 %all-reduce.4.cloned.1.call-done = (f32[2048]{0:T(1024)}, f32[2048]{0:T(1024)}, f32[1024]{0:T(1024)}, f32[1024]{0:T(1024)}, f32[3072]{0:T(1024)}, /*index=5*/f32...) async-done(((f32[2048]{0:T(1024)}, f32[2048]{0:T(1024)}, f32[1024]{0:T(1024)}, f32[1024]{0:T(1024)}, f32[3072]{0:T(1024)}, ...) | async-done | bytes 99472 | tf_op jit(solution)/shard_map/psum | solution.py:209
  573.0 189.5 %reduce-scatter.15.cloned.1.call-done = f32[64,1024]{1,0:T(8,128)} async-done(((f32[2048,1024]{1,0:T(8,128)}), f32[64,1024]{1,0:T(8,128)}) %reduce-scatter.15.cloned.1.call-update) | async-done | bytes 262160 | tf_op jit(solution)/shard_map/reduce_scatter | solution.py:204
  762.5 160.0 %reduce-scatter.17.cloned.1.call-done = f32[32,3072]{1,0:T(8,128)} async-done(((f32[1024,3072]{1,0:T(8,128)}), f32[32,3072]{1,0:T(8,128)}) %reduce-scatter.17.cloned.1.call-update) | async-done | bytes 393232 | tf_op jit(solution)/shard_map/reduce_scatter | solution.py:205
  (207 shorter events, 118.6 us)
Async XLA Ops:
  7.2 150.6 %copy-start = (bf16[1024,1024]{1,0:T(8,128)(2,1)S(1)}, bf16[1024,1024]{1,0:T(8,128)(2,1)}, u32[]{:S(2)}) copy-start(bf16[1024,1024]{1,0:T(8,128)(2,1)} %param.35) | copy-start | bytes 6291460
  26.8 35.9 %all-to-all-start = ((bf16[200,3,4,256]{3,0,1,2:T(8,128)(2,1)}), bf16[200,3,4,256]{3,0,1,2:T(8,128)(2,1)S(1)}, u32[]{:S(2)}, u32[]{:S(2)}) async-start(bf16[200,3,4,256]{3,0,1,2:T(8,128)(2,1)} %copy.83), calls=%async_computation | async-start | bytes 2457600 | tf_op jit(solution)/shard_map/all_to_all | solution.py:83
  33.1 80.6 %reduce-scatter.9.cloned.1.call-start = ((), (), s32[]{:S(2)}) async-start(), calls=%async_computation.10 | async-start | bytes 2048000 | tf_op jit(solution)/shard_map/reduce_scatter | solution.py:124
  74.3 39.4 %copy-start.35 = (f32[1024]{0:T(1024)S(1)}, f32[1024]{0:T(1024)}, u32[]{:S(2)}) copy-start(f32[1024]{0:T(1024)} %param.30) | copy-start | bytes 12292
  75.0 40.3 %copy-start.33 = (f32[1024]{0:T(1024)S(1)}, f32[1024]{0:T(1024)}, u32[]{:S(2)}) copy-start(f32[1024]{0:T(1024)} %param.31) | copy-start | bytes 12292
  75.0 40.3 %copy-start.36 = (f32[1024]{0:T(1024)S(1)}, f32[1024]{0:T(1024)}, u32[]{:S(2)}) copy-start(f32[1024]{0:T(1024)} %param.32) | copy-start | bytes 12292
  78.1 75.6 %all-gather.3.cloned.1.call-start = ((), (), s32[]{:S(2)}) async-start(), calls=%async_computation.11 | async-start | bytes 2048000 | tf_op jit(solution)/shard_map/all_gather | solution.py:130
  116.4 41.4 %copy-start.34 = (f32[1024]{0:T(1024)S(1)}, f32[1024]{0:T(1024)}, u32[]{:S(2)}) copy-start(f32[1024]{0:T(1024)} %param.34) | copy-start | bytes 12292
  116.4 91.6 %reduce-scatter.13.cloned.1.call-start = ((), (), s32[]{:S(2)}) async-start(), calls=%async_computation.13 | async-start | bytes 2048000 | tf_op jit(solution)/shard_map/reduce_scatter | solution.py:144
  157.8 11.7 %copy-start.40 = (bf16[1024,1024]{1,0:T(8,128)(2,1)S(1)}, bf16[1024,1024]{1,0:T(8,128)(2,1)}, u32[]{:S(2)}) copy-start(bf16[1024,1024]{1,0:T(8,128)(2,1)} %param.33) | copy-start | bytes 6291460
  172.7 72.8 %reduce-scatter.11.cloned.1.call-start = ((), (), s32[]{:S(2)}) async-start(), calls=%async_computation.12 | async-start | bytes 2048000 | tf_op jit(solution)/shard_map/reduce_scatter | solution.py:134
  177.7 67.8 %copy-start.37 = (f32[1024]{0:T(1024)S(1)}, f32[1024]{0:T(1024)}, u32[]{:S(2)}) copy-start(f32[1024]{0:T(1024)} %param.36) | copy-start | bytes 12292
  180.8 69.6 %copy-start.41 = (bf16[800,1024]{1,0:T(8,128)(2,1)S(1)}, bf16[800,1024]{1,0:T(8,128)(2,1)}, u32[]{:S(2)}) copy-start(bf16[800,1024]{1,0:T(8,128)(2,1)} %all-gather.3.cloned.1.call-done) | copy-start | bytes 4915204
  180.8 106.9 %all-gather.5.cloned.1.call-start = ((), (), s32[]{:S(2)}) async-start(), calls=%async_computation.14 | async-start | bytes 2048000 | tf_op jit(solution)/shard_map/all_gather | solution.py:148
  250.3 152.8 %reduce-scatter.21.cloned.1.call-start = ((), (), s32[]{:S(2)}) async-start(), calls=%async_computation.18 | async-start | bytes 4718592 | tf_op jit(solution)/shard_map/reduce_scatter | solution.py:199
  256.2 146.9 %reduce-scatter.23.cloned.1.call-start = ((), (), s32[]{:S(2)}) async-start(), calls=%async_computation.19 | async-start | bytes 4718592 | tf_op jit(solution)/shard_map/reduce_scatter | solution.py:200
  262.6 32.4 %copy-start.3 = (f32[8,8,100,100]{2,3,1,0:T(8,128)S(1)}, f32[8,8,100,100]{2,3,1,0:T(8,128)}, u32[]{:S(2)}) copy-start(f32[8,8,100,100]{2,3,1,0:T(8,128)} %copy-done.2) | copy-start | bytes 7680004
  315.0 42.1 %all-to-all-start.1 = ((bf16[800,3,1,256]{3,1,2,0:T(4,128)(2,1)}), bf16[800,3,1,256]{3,1,2,0:T(4,128)(2,1)S(1)}, u32[]{:S(2)}, u32[]{:S(2)}) async-start(bf16[800,3,1,256]{3,1,2,0:T(4,128)(2,1)} %copy.100), calls=%async_computation.4 | async-start | bytes 3276800 | tf_op jit(solution)/shard_map/all_to_all | solution.py:181
  318.6 119.0 %reduce-scatter.19.cloned.1.call-start = ((), (), s32[]{:S(2)}) async-start(), calls=%async_computation.17 | async-start | bytes 1179648 | tf_op jit(solution)/shard_map/reduce_scatter | solution.py:198
  322.2 250.8 %all-reduce.4.cloned.1.call-start = ((), (), s32[]{:S(2)}) async-start(), calls=%async_computation.20 | async-start | bytes 204800 | tf_op jit(solution)/shard_map/psum | solution.py:209
  327.8 30.1 %copy-start.24 = (f32[361,32]{0,1:T(8,128)}, f32[361,32]{0,1:T(8,128)S(1)}, u32[]{:S(2)}) copy-start(f32[361,32]{0,1:T(8,128)S(1)} %fusion.32) | copy-start | bytes 138628
  370.8 391.7 %reduce-scatter.15.cloned.1.call-start = ((), (), s32[]{:S(2)}) async-start(), calls=%async_computation.15 | async-start | bytes 8650752 | tf_op jit(solution)/shard_map/reduce_scatter | solution.py:204
  375.5 547.0 %reduce-scatter.17.cloned.1.call-start = ((), (), s32[]{:S(2)}) async-start(), calls=%async_computation.16 | async-start | bytes 12976128 | tf_op jit(solution)/shard_map/reduce_scatter | solution.py:205
  383.4 552.0 %copy-start.1 = (bf16[1024,1024]{1,0:T(8,128)(2,1)S(1)}, bf16[1024,1024]{1,0:T(8,128)(2,1)}, u32[]{:S(2)}) copy-start(bf16[1024,1024]{1,0:T(8,128)(2,1)} %param.35) | copy-start | bytes 6291460
  (37 other events, 169.9 us)
Sparse Core Ops, SparseCore 0:
  78.2 35.3 reduce-scatter.8
  116.5 37.1 all-gather.2
  172.8 35.1 reduce-scatter.12
  210.1 35.3 reduce-scatter.10
  250.5 37.1 all-gather.4
  291.8 50.1 reduce-scatter.20
  346.0 51.3 reduce-scatter.22
  401.5 36.0 reduce-scatter.18
  446.9 126.0 all-reduce.3
  575.7 186.7 reduce-scatter.14
  769.1 153.3 reduce-scatter.16
where the time goes:
time: 948 us; the launch traced here: 942 us
  waiting for transfers between devices  726 us (77%)
  matrix products  91.3 us (10%)
  local copies, waits for them, and re-layouts  58.5 us (6%)
  other arithmetic  25.7 us (3%)
  between operations  15.4 us (2%)
  blocking collectives  13.2 us (1%)
  starting transfers between devices  11.8 us (1%)
    reduce_scatter x1, waiting for transfers between devices, on_device(): lax.psum_scatter(merge_w_grad, ('wide', 'narrow'), scatter_dimension=0, t...  189 us
    reduce_scatter x1, waiting for transfers between devices, on_device(): lax.psum_scatter(qkv_w_grad, ('wide', 'narrow'), scatter_dimension=0, til...  160 us
    psum x1, waiting for transfers between devices, on_device(): lax.psum((jnp.sum(d_merged * merge_hat, 0), jnp.sum(d_merged, 0), jnp.sum...  135 us
    dot_general x10, matrix products, contract(): lax.dot_general(left, right, (((left_dim,), (right_dim,)), ((), ())), pre...  50.9 us
    all_gather x1, waiting for transfers between devices, on_device(): lax.all_gather(out2.astype(jnp.bfloat16), 'narrow', axis=0, tiled=True)  37.1 us
    reduce_scatter x1, waiting for transfers between devices, on_device(): lax.psum_scatter(attn_part.astype(jnp.bfloat16), 'narrow', scatter_dimens...  35.5 us
    reduce_scatter x1, waiting for transfers between devices, on_device(): lax.psum_scatter(fc2_part.astype(jnp.bfloat16), 'narrow', scatter_dimensi...  35.5 us
    reduce_scatter x1, waiting for transfers between devices, on_device(): lax.psum_scatter(proj_w_grad, 'wide', scatter_dimension=0, tiled=True)  34.5 us
  transfers between devices with their start and end apart: 13, of which 11 were waited for; matrix products, arithmetic and copies ran while one was open for 10% of the time, Pallas kernels for 0%

commit v1 on v0

v1 whole, which is shorter than its diff:
```python
import functools

import jax
import jax.numpy as jnp
from jax import lax
from jax.experimental import pallas as pl
from jax.experimental.pallas import tpu as pltpu
from jax.sharding import PartitionSpec as P

WIN = 10
WINDOW_TOKENS = WIN * WIN
QUERY_ROWS = 112
KEY_ROWS = 128
EPS = 1e-05
MEBI = 1024 * 1024
PROBS_ROOM = 52
WAIT_US = 100.0
WEIGHT_US = {
    "attend_back": 7.2, "back1": 4.1, "proj_grad": 3.1, "back0": 3.3, "qkv_grad": 5.0, "merge_grad": 4.2,
    "second_join": 2.0, "qkv_join": 1.5,
}
WEIGHT_US |= dict.fromkeys(
    ("pack", "front", "cut", "pieces", "spread", "attend", "mine", "after", "slope", "feed", "second", "fc1_grad",
     "fc2_grad", "fc1_join", "fc2_join", "fc1_join2", "fc2_join2", "back2"), WAIT_US
)
FLOPS_PER_US = 10**9
BF = jnp.bfloat16
F32 = jnp.float32


def normalise(values):
    average = jnp.mean(values, -1, keepdims=True)
    centred = values - average
    inverse = lax.rsqrt(jnp.mean(centred * centred, -1, keepdims=True) + EPS)
    return centred * inverse, inverse


def norm_backward(grad_out, normal, inverse, gain):
    scaled = grad_out * gain
    return inverse * (
        scaled
        - jnp.mean(scaled, -1, keepdims=True)
        - normal * jnp.mean(scaled * normal, -1, keepdims=True)
    )


def matmul(left, right):
    return jnp.dot(left, right, preferred_element_type=jnp.float32)


def contract(left, right, left_dim, right_dim):
    return lax.dot_general(
        left, right, (((left_dim,), (right_dim,)), ((), ())), preferred_element_type=jnp.float32
    )


def low(array):
    return array.astype(BF)


def row(vector):
    return vector.reshape(1, -1)


def stays():
    return pl.BlockSpec(memory_space=pl.ANY)


def outside():
    return pl.BlockSpec(memory_space=pltpu.HBM)


def held():
    return pl.BlockSpec(memory_space=pltpu.VMEM)


def shape_of(shape, dtype):
    return jax.ShapeDtypeStruct(shape, dtype)


def whole(kernel, place, outs, *operands, leave=(), scratch=(), after=(), room=20, name=None):
    arrays = [a for a, _ in operands]
    count, skip = len(arrays), len(after)

    def body(place_ref, *refs):
        kernel(place_ref, *refs[:count], *refs[count + skip :])

    return pl.pallas_call(
        body,
        in_specs=[pl.BlockSpec(memory_space=pltpu.SMEM)]
        + [{True: held, False: outside, None: stays}[inside]() for _, inside in operands]
        + [stays()] * skip,
        out_specs=[outside() if k in leave else held() for k in range(len(outs))],
        out_shape=list(outs),
        scratch_shapes=list(scratch),
        compiler_params=pltpu.CompilerParams(vmem_limit_bytes=room * MEBI),
        cost_estimate=pl.CostEstimate(
            flops=int(WEIGHT_US.get(name, 0.7) * FLOPS_PER_US), bytes_accessed=0, transcendentals=0
        ),
        name=name,
    )(place, *arrays, *after)


def tie(array, *after):
    def body(*refs):
        del refs

    return pl.pallas_call(
        body,
        in_specs=[stays()] * (1 + len(after)),
        out_specs=stays(),
        out_shape=shape_of(array.shape, array.dtype),
        input_output_aliases={0: 0},
        name="tie",
    )(array, *after)


def swap(array, axis, mask):
    size = lax.axis_size(axis)
    return lax.ppermute(array, axis, [(i, i ^ mask) for i in range(size)])


def turn(array, axis, step):
    size = lax.axis_size(axis)
    return lax.ppermute(array, axis, [(i, (i + step) % size) for i in range(size)])


def sum_all(vector):
    mask = 1
    while mask < lax.axis_size("wide"):
        vector = vector + swap(vector, "wide", mask)
        mask *= 2
    mask = 1
    while mask < lax.axis_size("narrow"):
        vector = vector + swap(vector, "narrow", mask)
        mask *= 2
    return vector


def sum_high(parts, high):
    take = lambda index: lax.dynamic_index_in_dim(parts, index, 0, keepdims=False)
    total = take(high).astype(F32)
    for j in range(1, parts.shape[0]):
        total = total + swap(low(take(high ^ j)), "wide", 8 * j).astype(F32)
    return total


def grad_kernel(place_ref, *refs, lefts, rights, block, rows, riding):
    left_refs, right_refs = refs[: len(lefts)], refs[len(lefts) : len(lefts) + len(rights)]
    kept_ref, sent_ref, total_ref = refs[-3:]
    core = place_ref[1]
    if riding:
        give_sums(sent_ref, kept_ref.shape[0], refs[-4][...])

    @pl.loop(0, kept_ref.shape[0])
    def _(step):
        at = pl.ds(pl.multiple_of(step * block, block), block)
        total = None
        for l_ref, l_at, r_ref, r_at in zip(left_refs, lefts, right_refs, rights):
            left = l_ref[:, at] if l_at is None else l_ref[l_at, :, at]
            right = r_ref[: left.shape[0]] if r_at is None else r_ref[r_at]
            right = low(right)
            part = contract(left, right, 0, 0)
            total = part if total is None else total + part
        total_ref[...] = total
        for s in range(block // (2 * rows)):
            mine = pl.multiple_of((2 * s + core) * rows, rows)
            theirs = pl.multiple_of((2 * s + 1 - core) * rows, rows)
            kept_ref[step, s * rows : (s + 1) * rows] = total_ref[pl.ds(mine, rows)]
            sent_ref[step, s * rows : (s + 1) * rows] = low(total_ref[pl.ds(theirs, rows)])


def grad_call(place, lefts, rights, block, rows, name, after=(), sums=None):
    split = lambda item: item if isinstance(item, tuple) else (item, None)
    left_arrays, left_at = zip(*map(split, lefts))
    right_arrays, right_at = zip(*map(split, rights))
    deep, width = left_arrays[0].shape[-1], right_arrays[0].shape[-1]
    shape = (deep // block, block // 2, width)
    return whole(
        functools.partial(
            grad_kernel, lefts=left_at, rights=right_at, block=block, rows=rows,
            riding=sums is not None,
        ),
        place,
        [shape_of(shape, F32), shape_of((shape[0] + (sums is not None), *shape[1:]), BF)],
        *((a, True) for a in left_arrays + right_arrays + (() if sums is None else (sums,))),
        scratch=[pltpu.VMEM((block, width), F32)],
        after=after,
        name=name,
    )


def add_up(refs, lead, rows):
    total = None
    for ref in refs:
        part = ref[lead, rows, :].astype(F32)
        total = part if total is None else total + part
    return total


def join_call(place, groups, outs, name, after=(), sums=None):
    width = groups[0][0].shape[2]
    counts = [len(sources) for sources in groups]
    count = sum(counts)
    rows_of = [pieces[0]((0, 0, 0))[3] for _, pieces in outs]
    more = 2 * sums[0].shape[0] // rows_of[1] if sums else 0
    shapes = [
        shape_of((len(pieces) + (more if k else 0), rows, width), dtype)
        for k, ((dtype, pieces), rows) in enumerate(zip(outs, rows_of))
    ]
    if sums:
        shapes = [shape_of(sums[0].shape, F32)] + shapes

    def kernel(place_ref, *refs):
        place_now = (place_ref[0], place_ref[1], place_ref[2])
        ins, out_refs = refs[:count], refs[count:]
        if sums:
            own_ref, total_ref, out_refs = refs[count], refs[count + 1], refs[count + 2 :]
            total = own_ref[...] + take_sums(ins[counts[0] - 1], sums[1], own_ref.shape[0])
            total_ref[...] = total
        at = [sum(counts[:g]) for g in range(len(counts))]
        for k, (out_ref, (dtype, pieces)) in enumerate(zip(out_refs, outs)):
            for n, piece in enumerate(pieces):
                group, lead, start, rows = piece(place_now)
                if not isinstance(start, int):
                    start = pl.multiple_of(start, rows)
                part = add_up(ins[at[group] : at[group] + counts[group]], lead, pl.ds(start, rows))
                out_ref[n] = part.astype(dtype)
            if sums and k:
                give_sums(out_ref, len(pieces), total)

    arrays = [s for sources in groups for s in sources] + ([sums[0]] if sums else [])
    return whole(
        kernel, place, shapes, *((s, True) for s in arrays), after=after, name=name
    )


def give_sums(ref, first, values):
    high = low(values)
    parts = jnp.concatenate([high, low(values - high.astype(F32))], 0)
    size = ref.shape[1]
    for k in range(parts.shape[0] // size):
        ref[first + k] = parts[k * size : (k + 1) * size]
    rest = parts.shape[0] % size
    if rest:
        ref[first + parts.shape[0] // size, :rest] = parts[parts.shape[0] - rest :]


def take_sums(ref, first, rows):
    size = ref.shape[1]
    blocks = [ref[first + k].astype(F32) for k in range(-(-2 * rows // size))]
    parts = jnp.concatenate(blocks, 0) if len(blocks) > 1 else blocks[0]
    return parts[:rows] + parts[rows : 2 * rows]


def cut_kernel(place_ref, merged_ref, own_ref, sent_ref, onward_ref):
    quad = place_ref[2]
    lanes = own_ref.shape[1]
    take = lambda j: merged_ref[:, pl.ds(pl.multiple_of((quad ^ j) * lanes, lanes), lanes)]
    own_ref[...] = take(0)
    sent_ref[0] = take(2)
    sent_ref[1] = take(3)
    onward_ref[...] = take(1)


def pack_kernel(
    place_ref, proj_ref, table_ref, message_ref
):
    part = proj_ref.shape[0] // 8
    own_heads = table_ref.shape[1]
    room = message_ref.shape[1] // 2
    eighth = place_ref[2] * 2 + place_ref[1]
    message_ref[:part] = proj_ref[pl.ds(pl.multiple_of(eighth * part, part), part), :]
    offsets = table_ref.shape[0]
    table = jnp.concatenate(
        [table_ref[...], jnp.zeros((offsets, 128 - own_heads), F32)], 1
    )
    table = jnp.concatenate([table, jnp.zeros((room - offsets, 128), F32)], 0)
    table = jnp.transpose(table)[:own_heads]
    high = low(table).astype(F32)
    rows = jnp.concatenate([high, table - high], 1)
    spare = message_ref.shape[0] - part - own_heads
    message_ref[part:] = low(jnp.concatenate([rows, jnp.zeros((spare, 2 * room), F32)], 0))


def pieces_kernel(place_ref, *refs, part):
    del place_ref
    for j, ref in enumerate(refs[:-1]):
        refs[-1][j * part : (j + 1) * part] = ref[:part]


def front_kernel(
    place_ref, flat_ref, mg_ref, ms_ref, n1g_ref, n1s_ref, qb_ref, mw_any, qw_any,
    merged_ref, resid0_ref, normed1_ref, qkv_ref, mw_ref, qw_ref, sems,
):
    copy_m = pltpu.make_async_copy(mw_any, mw_ref, sems.at[0])
    copy_q = pltpu.make_async_copy(qw_any, qw_ref, sems.at[1])
    copy_m.start()
    copy_q.start()
    hat, _ = normalise(flat_ref[...].astype(F32))
    merged = low(hat * mg_ref[...] + ms_ref[...])
    merged_ref[...] = merged
    copy_m.wait()
    resid0 = matmul(merged, mw_ref[...])
    resid0_ref[...] = resid0
    hat1, _ = normalise(resid0)
    normed1 = low(hat1 * n1g_ref[...] + n1s_ref[...])
    normed1_ref[...] = normed1
    copy_q.wait()
    qkv_ref[...] = low(matmul(normed1, qw_ref[...]) + qb_ref[...])


def front_call(place, flat, mg, ms, n1g, n1s, qb, mw, qw):
    rows, deep = flat.shape
    width = mw.shape[1]
    return whole(
        front_kernel,
        place,
        [
            shape_of((rows, deep), BF),
            shape_of((rows, width), F32),
            shape_of((rows, width), BF),
            shape_of((rows, 3 * width), BF),
        ],
        (flat, True), (row(mg), True), (row(ms), True), (row(n1g), True), (row(n1s), True),
        (row(qb), True), (mw, False), (qw, False),
        scratch=[
            pltpu.VMEM(mw.shape, BF), pltpu.VMEM(qw.shape, BF), pltpu.SemaphoreType.DMA((2,)),
        ],
        room=28,
        name="front",
    )


def mine_kernel(place_ref, *refs):
    del place_ref
    rows = refs[0].shape[0]
    for q, ref in enumerate(refs[:-1]):
        refs[-1][q * rows : (q + 1) * rows] = ref[...]


def bring_proj(place_ref, own_any, mine_any, theirs_any, proj_ref, sems, groups):
    rank, core, quad = place_ref[0], place_ref[1], place_ref[2]
    shard = own_any.shape[0]
    part = shard // 8

    def bring(source, start, rows, sem):
        at = pl.ds(pl.multiple_of(start, rows), rows)
        copy = pltpu.make_async_copy(source, proj_ref.at[at], sems.at[sem])
        copy.start()
        return copy

    copies = [bring(own_any, rank * shard, shard, 0)]
    for k in range(4 * (groups - 1)):
        q, j = k // (groups - 1), k % (groups - 1)
        base = lax.rem(rank + groups - 1 - j, groups) * shard + (quad ^ q) * 2 * part
        rows = pl.ds(k * part, part)
        copies.append(bring(mine_any.at[rows], base + core * part, part, 1 + 2 * k))
        copies.append(bring(theirs_any.at[rows], base + (1 - core) * part, part, 2 + 2 * k))
    return copies


def after_kernel(
    place_ref, heads_ref, resid0_ref, pb_ref, n2g_ref, n2s_ref, own_any, mine_any, theirs_any,
    resid1_ref, normed2_ref, proj_ref, sems, *, groups,
):
    for copy in bring_proj(place_ref, own_any, mine_any, theirs_any, proj_ref, sems, groups):
        copy.wait()
    resid1 = resid0_ref[...] + matmul(heads_ref[...], proj_ref[...]) + pb_ref[...]
    resid1_ref[...] = resid1
    hat2, _ = normalise(resid1)
    normed2_ref[...] = low(hat2 * n2g_ref[...] + n2s_ref[...])


SQRT_HALF = 0.5**0.5
DENSITY = 0.3989422804014327


def gelu_pair(values):
    below = 0.5 * (1.0 + lax.erf(values * SQRT_HALF))
    density = jnp.exp(-0.5 * values * values) * DENSITY
    return values * below, below + values * density


def slope_kernel(
    place_ref, dy_ref, fc2_ref, rows_ref, own_ref, out_ref, wide_ref, *, groups, pad, chunk
):
    tokens, width = own_ref.shape
    wide_ref[...] = dy_ref[...].astype(F32)
    fill = jnp.zeros((pad - tokens, width), F32)
    for j in range(groups):
        at = lax.rem(place_ref[0] + groups - j, groups) * tokens
        block = wide_ref[pl.ds(pl.multiple_of(at, 8), tokens), :]
        rows_ref[j * pad : (j + 1) * pad] = low(jnp.concatenate([block, fill], 0))
        if j == 0:
            own_ref[...] = low(block)

    @pl.loop(0, fc2_ref.shape[0] // chunk)
    def _(step):
        at = pl.ds(pl.multiple_of(step * chunk, chunk), chunk)
        out_ref[:, at] = contract(rows_ref[...], fc2_ref[at, :], 1, 1)


def feed_kernel(
    place_ref, n0_ref, n1_ref, n2_ref, n3_ref, d_act_ref, fc1_ref, fc1b_ref,
    act_ref, dpre_ref, all_ref, db_ref, o0_ref, o1_ref, o2_ref, o3_ref, *, pad, chunk,
):
    del place_ref
    rows, width = n0_ref.shape
    for j, ref in enumerate((n0_ref, n1_ref, n2_ref, n3_ref)):
        all_ref[j * pad : j * pad + rows, :] = ref[...]
        all_ref[j * pad + rows : (j + 1) * pad, :] = jnp.zeros((pad - rows, width), BF)

    @pl.loop(0, fc1_ref.shape[1] // chunk)
    def _(step):
        at = pl.ds(pl.multiple_of(step * chunk, chunk), chunk)
        pre = matmul(all_ref[...], fc1_ref[:, at]) + fc1b_ref[:, at]
        act, slope = gelu_pair(pre)
        act_ref[:, at] = low(act)
        d_low = low(d_act_ref[:, at] * slope)
        dpre_ref[:, at] = d_low
        db_ref[:, at] = jnp.sum(d_low.astype(F32), 0, keepdims=True)

    for j, ref in enumerate((o0_ref, o1_ref, o2_ref, o3_ref)):
        part = contract(dpre_ref[j * pad : (j + 1) * pad, :], fc1_ref[...], 1, 1)
        ref[...] = low(part[:rows])


def second_kernel(place_ref, act_ref, fc2_ref, kept_ref, sent_ref, *, pad, groups):
    rank = place_ref[0]
    rows = kept_ref.shape[1]
    for ref, k, flip in ((sent_ref, 0, 1), (sent_ref, 1, 3), (kept_ref, 0, 0), (kept_ref, 1, 2)):
        block = lax.rem(rank + groups - (rank ^ flip), groups)
        at = pl.ds(pl.multiple_of(block * pad, pad), pad)
        ref[k] = low(matmul(act_ref[at, :], fc2_ref[...])[:rows])


def back2_kernel(
    place_ref, c0_ref, c1_ref, c2_ref, c3_ref, resid1_ref, dy_ref, n2g_ref, own_any, mine_any, theirs_any,
    dresid1_ref, dheads_ref, proj_ref, sems, *, groups,
):
    copies = bring_proj(place_ref, own_any, mine_any, theirs_any, proj_ref, sems, groups)
    rows = dheads_ref.shape[0]
    d_norm2 = (
        c0_ref[...].astype(F32) + c1_ref[...].astype(F32)
        + c2_ref[...].astype(F32) + c3_ref[...].astype(F32)
    )
    hat2, inv2 = normalise(resid1_ref[...])
    dy = dy_ref[...].astype(F32)
    d_resid1 = dy + norm_backward(d_norm2, hat2, inv2, n2g_ref[...])
    dresid1_ref[:rows] = d_resid1
    sums = (d_resid1, d_norm2 * hat2, d_norm2, dy)
    for k, part in enumerate(sums):
        dresid1_ref[rows + k : rows + k + 1] = jnp.sum(part, 0, keepdims=True)
    for copy in copies:
        copy.wait()
    dheads_ref[...] = low(contract(low(d_resid1), proj_ref[...], 1, 1))


def back1_kernel(
    place_ref, even_ref, odd_ref, dresid1_ref, resid0_ref, n1g_ref, qw_any,
    dresid0_ref, sums_ref, qw_ref, sems,
):
    rows, width = resid0_ref.shape
    quad = place_ref[2]
    lanes = width // 4
    copies = [
        pltpu.make_async_copy(qw_any.at[:, pl.ds(i * width, width)], qw_ref.at[i], sems.at[i])
        for i in range(3)
    ]
    for copy in copies:
        copy.start()
    hat1, inv1 = normalise(resid0_ref[...])
    d_norm1 = jnp.zeros((rows, width), F32)
    for i in range(3):
        copies[i].wait()
        for j in range(4):
            part = (odd_ref if j % 2 else even_ref)[j // 2, :, i * lanes : (i + 1) * lanes]
            at = pl.ds(pl.multiple_of((quad ^ j) * lanes, lanes), lanes)
            d_norm1 = d_norm1 + contract(part, qw_ref[i, :, at], 1, 1)
            sums_ref[2 + i : 3 + i, at] = jnp.sum(part.astype(F32), 0, keepdims=True)
    dresid0_ref[...] = low(
        dresid1_ref[:rows] + norm_backward(d_norm1, hat1, inv1, n1g_ref[...])
    )
    sums_ref[0:1] = jnp.sum(d_norm1 * hat1, 0, keepdims=True)
    sums_ref[1:2] = jnp.sum(d_norm1, 0, keepdims=True)


def back0_kernel(
    place_ref, dresid0_ref, flat_ref, mg_ref, mw_any, grad_ref, sums_ref, mw_ref, sems
):
    del place_ref
    copy = pltpu.make_async_copy(mw_any, mw_ref, sems.at[0])
    copy.start()
    hat, inv = normalise(flat_ref[...].astype(F32))
    copy.wait()
    d_merged = contract(dresid0_ref[...], mw_ref[...], 1, 1)
    grad_ref[...] = low(norm_backward(d_merged, hat, inv, mg_ref[...]))
    width = dresid0_ref.shape[1]
    gain = jnp.sum(d_merged * hat, 0, keepdims=True)
    shift = jnp.sum(d_merged, 0, keepdims=True)
    for i in range(gain.shape[1] // width):
        sums_ref[i : i + 1] = gain[:, i * width : (i + 1) * width]
        sums_ref[2 + i : 3 + i] = shift[:, i * width : (i + 1) * width]


SPAN = 2 * WIN - 1
OFFSETS = 384
STRIP = 256


def strip_picks(column, offsets_first):
    shape, o_dim = ((OFFSETS, STRIP), 0) if offsets_first else ((STRIP, OFFSETS), 1)
    offset = lax.broadcasted_iota(jnp.int32, shape, o_dim)
    lane = lax.broadcasted_iota(jnp.int32, shape, 1 - o_dim)
    wanted = (SPAN - 1 - lane // WIN) * SPAN + column - lane % WIN + WIN - 1
    hit = (offset == wanted) & (lane < SPAN * WIN)
    return jnp.where(hit, 1.0, 0.0).astype(BF)


def split3(values):
    first = low(values)
    rest = values - first.astype(F32)
    second = low(rest)
    third = low(rest - second.astype(F32))
    return first, second, third


def spread_kernel(place_ref, m0_ref, m1_ref, m2_ref, m3_ref, bias_ref, table_ref, *, part, groups):
    heads = table_ref.shape[0]
    own_heads = heads // groups
    room = m0_ref.shape[1] // 2
    for j, ref in enumerate((m0_ref, m1_ref, m2_ref, m3_ref)):
        both = ref[part : part + 2 * own_heads, :].astype(F32)[:own_heads]
        at = pl.multiple_of(lax.rem(place_ref[0] + groups - j, groups) * own_heads, own_heads)
        table_ref[pl.ds(at, own_heads), :] = both[:, :OFFSETS] + both[:, room : room + OFFSETS]
    table = table_ref[...]
    high = low(table)
    table = jnp.concatenate([high, low(table - high.astype(F32))], 0)
    for column in range(WIN):
        parts = matmul(table, strip_picks(column, True))
        strip = parts[:heads] + parts[heads:]
        for r in range(WIN):
            start = (WIN - 1 - r) * WIN
            at = (r * WIN + column) * heads
            bias_ref[at : at + heads, :] = strip[:, start : start + KEY_ROWS]
    bias_ref[WINDOW_TOKENS * heads :, :] = jnp.zeros(
        ((QUERY_ROWS - WINDOW_TOKENS) * heads, KEY_ROWS), F32
    )


def fold(grad_ref, heads):
    total = jnp.zeros((3 * heads, OFFSETS), F32)
    for column in range(WIN):
        strip = jnp.zeros((heads, STRIP), F32)
        for r in range(WIN):
            start = (WIN - 1 - r) * WIN
            at = (r * WIN + column) * heads
            part = grad_ref[at : at + heads, :]
            wide = jnp.concatenate([part, jnp.zeros((heads, STRIP - KEY_ROWS), F32)], 1)
            strip = strip + (pltpu.roll(wide, start, 1) if start else wide)
        total = total + matmul(jnp.concatenate(split3(strip), 0), strip_picks(column, False))
    return total[:heads] + total[heads : 2 * heads] + total[2 * heads :]


def window_rows(values, window, rows):
    part = values.astype(F32)[window * WINDOW_TOKENS : (window + 1) * WINDOW_TOKENS]
    zeros = jnp.zeros((rows - WINDOW_TOKENS, part.shape[1]), F32)
    return low(jnp.concatenate([part, zeros], 0))


def stack_heads(part, heads, head_dim):
    lane = lax.broadcasted_iota(jnp.int32, part.shape, 1) // head_dim
    zero = jnp.zeros_like(part)
    return jnp.concatenate([jnp.where(lane == h, part, zero) for h in range(heads)], 0)


def attend_kernel(
    place_ref, qkv_ref, bias_ref, mask_ref, out_ref, probs_any, probs_ref, sems, *, windows, head_dim
):
    del place_ref
    width = out_ref.shape[1]
    lanes = width // 4

    def keep(step):
        return pltpu.make_async_copy(probs_ref.at[step], probs_any.at[step], sems.at[step])

    @pl.loop(0, 4)
    def _(step):
        attend_group(
            step, qkv_ref, bias_ref, mask_ref, out_ref, probs_ref, windows, head_dim, width, lanes
        )
        keep(step).start()

    for step in range(4):
        keep(step).wait()


def attend_group(
    step, qkv_ref, bias_ref, mask_ref, out_ref, probs_ref, windows, head_dim, width, lanes
):
    heads, all_heads = lanes // head_dim, width // head_dim
    first = step * heads
    scale = head_dim ** (-0.5)
    at = lambda kind: pl.ds(pl.multiple_of(kind * width + step * lanes, lanes), lanes)
    q_all, k_all, v_all = (qkv_ref[:, at(kind)] for kind in range(3))
    outs = []
    for w in range(windows):
        query = window_rows(q_all, w, QUERY_ROWS)
        keys = stack_heads(window_rows(k_all, w, KEY_ROWS), heads, head_dim)
        values = stack_heads(window_rows(v_all, w, KEY_ROWS), heads, head_dim)
        scores = contract(query, keys, 1, 1) * scale
        mask = mask_ref[w]
        rounded = []
        for h in range(heads):
            bias = bias_ref[pl.ds(first + h, QUERY_ROWS, stride=all_heads), :]
            raw = scores[:, h * KEY_ROWS : (h + 1) * KEY_ROWS] + bias + mask
            expo = jnp.exp(raw - jnp.max(raw, -1, keepdims=True))
            probs = expo / jnp.sum(expo, -1, keepdims=True)
            probs_ref[step, w, h] = probs
            rounded.append(low(probs))
        mixed = matmul(jnp.concatenate(rounded, 1), values)
        outs.append(mixed[:WINDOW_TOKENS])
    out_ref[:, at(0)] = low(jnp.concatenate(outs, 0))


def attend_back_kernel(
    place_ref, qkv_ref, grad_ref, probs_any, even_ref, odd_ref, table_ref, dbias_ref, probs_ref, sems,
    *, windows, head_dim
):
    width = grad_ref.shape[1]

    def fetch(step):
        return pltpu.make_async_copy(
            probs_any.at[place_ref[2] ^ step], probs_ref.at[step], sems.at[step]
        )

    for step in range(4):
        fetch(step).start()

    @pl.loop(0, 4)
    def _(step):
        fetch(step).wait()
        attend_back_group(
            place_ref[2] ^ step, step, qkv_ref, grad_ref, probs_ref, even_ref, odd_ref, dbias_ref,
            windows, head_dim, width, width // 4,
        )

    table_ref[...] = fold(dbias_ref, table_ref.shape[0])


def attend_back_group(
    group, step, qkv_ref, grad_ref, probs_ref, even_ref, odd_ref, dbias_ref,
    windows, head_dim, width, lanes,
):
    heads, all_heads = lanes // head_dim, width // head_dim
    first = group * heads
    scale = head_dim ** (-0.5)
    at = lambda kind: pl.ds(pl.multiple_of(kind * width + group * lanes, lanes), lanes)
    q_all, k_all, v_all = (qkv_ref[:, at(kind)] for kind in range(3))
    g_all = grad_ref[:, at(0)]
    all_q, all_k, all_v = [], [], []
    d_first = []
    for w in range(windows):
        query = stack_heads(window_rows(q_all, w, QUERY_ROWS), heads, head_dim)
        keys = stack_heads(window_rows(k_all, w, KEY_ROWS), heads, head_dim)
        values = stack_heads(window_rows(v_all, w, KEY_ROWS), heads, head_dim)
        plain = window_rows(g_all, w, QUERY_ROWS)
        grad = stack_heads(plain, heads, head_dim)
        d_probs = contract(plain, values, 1, 1)
        d_list, p_list = [], []
        for h in range(heads):
            probs = probs_ref[step, w, h]
            part = d_probs[:, h * KEY_ROWS : (h + 1) * KEY_ROWS]
            total = jnp.sum(part * probs, -1, keepdims=True)
            d_scores = low(probs * (part - total))
            d_list.append(d_scores)
            p_list.append(low(probs))
            if w == 0:
                d_first.append(d_scores.astype(F32))
            else:
                d_first[h] = d_first[h] + d_scores.astype(F32)
            if w == windows - 1:
                dbias_ref[pl.ds(first + h, QUERY_ROWS, stride=all_heads), :] = d_first[h]
        d_query = matmul(jnp.concatenate(d_list, 1), keys) * scale
        d_keys = contract(jnp.concatenate(d_list, 0), query, 0, 0) * scale
        d_values = contract(jnp.concatenate(p_list, 0), grad, 0, 0)
        all_q.append(d_query[:WINDOW_TOKENS])
        all_k.append(d_keys[:WINDOW_TOKENS])
        all_v.append(d_values[:WINDOW_TOKENS])
    result = jnp.concatenate(
        [low(jnp.concatenate(parts, 0)) for parts in (all_q, all_k, all_v)], 1
    )

    @pl.when(step % 2 == 0)
    def _():
        even_ref[step // 2] = result

    @pl.when(step % 2 == 1)
    def _():
        odd_ref[step // 2] = result


def spots(heads, lines, vectors):
    columns = 3
    return [(k // columns, OFFSETS + 128 * (k % columns)) for k in range(vectors * lines)]


def collect_kernel(place_ref, s0_ref, s1_ref, d_ref, rel_ref, b_ref, out_ref):
    heads = rel_ref.shape[0]
    lines = s0_ref.shape[1] // 128
    out_ref[...] = jnp.zeros(out_ref.shape, F32)
    out_ref[:heads, :OFFSETS] = rel_ref[...]
    vectors = [ref[r : r + 1, :] for ref in (s0_ref, s1_ref) for r in range(ref.shape[0])]
    after = d_ref.shape[0] - 8
    vectors += [d_ref[after + r : after + r + 1, :] for r in range(4)]
    for k, (at, lane) in enumerate(spots(heads, lines, len(vectors))):
        piece = vectors[k // lines][:, 128 * (k % lines) : 128 * (k % lines + 1)]
        out_ref[at : at + 1, lane : lane + 128] = piece
    own = b_ref.shape[1] // 128
    first = heads + pl.multiple_of((place_ref[0] // 2) * own, own)
    block = jnp.concatenate([b_ref[:, k * 128 : (k + 1) * 128] for k in range(own)], 0)
    side = place_ref[0] % 2

    @pl.when(side == 0)
    def _():
        out_ref[pl.ds(first, own), 0:128] = block

    @pl.when(side == 1)
    def _():
        out_ref[pl.ds(first, own), 128:256] = block


def deliver_kernel(place_ref, all_ref, sums_ref, rel_ref, b_ref):
    heads = rel_ref.shape[0]
    vectors, width = sums_ref.shape
    lines = width // 128
    rel_ref[...] = all_ref[:heads, :OFFSETS]
    for k, (at, lane) in enumerate(spots(heads, lines, vectors)):
        sums_ref[k // lines : k // lines + 1, 128 * (k % lines) : 128 * (k % lines + 1)] = all_ref[
            at : at + 1, lane : lane + 128
        ]
    own = b_ref.shape[0]
    first = heads + pl.multiple_of((place_ref[0] // 2) * own, own)
    side = place_ref[0] % 2

    @pl.when(side == 0)
    def _():
        b_ref[...] = all_ref[pl.ds(first, own), 0:128]

    @pl.when(side == 1)
    def _():
        b_ref[...] = all_ref[pl.ds(first, own), 128:256]


def columns_kernel(place_ref, b0_ref, b1_ref, b2_ref, b3_ref, own_ref, out_ref, sums_ref):
    rows = out_ref.shape[0]
    lanes = b0_ref.shape[2] // 3
    total = own_ref[...]
    for j, ref in enumerate((b0_ref, b1_ref, b2_ref, b3_ref)):
        for part in range(3):
            at = pl.multiple_of((part * 4 + (place_ref[2] ^ j)) * lanes, lanes)
            out_ref[:, pl.ds(at, lanes)] = ref[0, :rows, part * lanes : (part + 1) * lanes].astype(F32)
        if j:
            total = total + take_sums(ref, 1, own_ref.shape[0])
    sums_ref[...] = total


def on_device(
    patches,
    window_extent,
    merge_gain,
    merge_shift,
    merge_weight,
    norm1_gain,
    norm1_shift,
    qkv_weight,
    qkv_bias,
    rel_table,
    proj_weight,
    proj_bias,
    norm2_gain,
    norm2_shift,
    fc1_weight,
    fc1_bias,
    fc2_weight,
    fc2_bias,
    out_grad,
):
    groups, wide = lax.axis_size("narrow"), lax.axis_size("wide")
    devices = wide * groups
    highs = wide // 8
    wide_at, rank = lax.axis_index("wide"), lax.axis_index("narrow")
    core, quad, high = wide_at % 2, (wide_at // 2) % 4, wide_at // 8
    place = jnp.stack([rank, core, quad]).astype(jnp.int32)
    tokens = patches.shape[0]
    width = qkv_weight.shape[0]
    own_heads = rel_table.shape[1]
    heads = own_heads * groups
    head_dim = width // heads
    windows = tokens // WINDOW_TOKENS
    pad = tokens + (-tokens) % 16

    def arrange(array, order):
        if highs == 1:
            return array
        sizes = {"h": highs, "q": 4, "c": 2, "n": groups}
        cut = [sizes[k] for k in order]
        rest = array.shape[1]
        for size in cut:
            rest //= size
        at = order.index("h") + 1
        moved = [i + 1 for i in range(len(order)) if i + 1 != at] + [at, len(order) + 1]
        return jnp.transpose(array.reshape(-1, *cut, rest), [0] + moved).reshape(array.shape)

    def settle(array):
        if highs == 1:
            return array[0]
        return sum_high(array[0].reshape(highs, -1, array.shape[2]), high)

    part = proj_weight.shape[0] // 8
    message = whole(
        pack_kernel,
        place,
        [shape_of((part + own_heads + (-(part + own_heads)) % 16, width), BF)],
        (proj_weight, True),
        (rel_table, True),
        name="pack",
    )[0]
    messages = [turn(message, "narrow", step) for step in range(1, groups)]

    flat = patches.reshape(tokens, -1)
    merged, resid0, normed1, qkv = front_call(
        place, flat, merge_gain, merge_shift, norm1_gain, norm1_shift, qkv_bias,
        merge_weight, qkv_weight,
    )
    mine = whole(
        functools.partial(pieces_kernel, part=part),
        place,
        [shape_of(((groups - 1) * part, width), BF)],
        *((m, True) for m in messages),
        name="pieces",
    )
    mine = list(mine) + [swap(mine[0], "wide", 2 * j) for j in (1, 2, 3)]

    merged_own, merged_sent, merged_onward = whole(
        cut_kernel,
        place,
        [
            shape_of((tokens, merged.shape[1] // 4), BF),
            shape_of((2, tokens, merged.shape[1] // 4), BF),
            shape_of((tokens, merged.shape[1] // 4), BF),
        ],
        (arrange(merged, "hqcn"), True),
        name="cut",
    )
    merged_near = swap(merged_sent, "wide", 4)
    normed1_cut = arrange(normed1, "hqcn")
    normed1_near = swap(normed1_cut, "wide", 2)

    positions = jnp.arange(KEY_ROWS)
    extent = lax.dynamic_slice_in_dim(window_extent, rank * windows, windows, 0)
    valid = (
        (positions[None, :] // WIN < extent[:, 0:1])
        & (positions[None, :] % WIN < extent[:, 1:2])
        & (positions[None, :] < WINDOW_TOKENS)
    )
    mask = jnp.where(valid, 0.0, -1e30).astype(F32)[:, None, :]
    bias = whole(
        functools.partial(spread_kernel, part=part, groups=groups),
        place,
        [shape_of((QUERY_ROWS * heads, KEY_ROWS), F32)],
        (message, True),
        *((m, True) for m in messages),
        scratch=[pltpu.VMEM((heads, OFFSETS), F32)],
        name="spread",
    )[0]
    heads_out, probs = whole(
        functools.partial(attend_kernel, windows=windows, head_dim=head_dim),
        place,
        [
            shape_of((tokens, width), BF),
            shape_of((PROBS_ROOM, windows, heads // 4, QUERY_ROWS, KEY_ROWS), F32),
        ],
        (qkv, True), (bias, True), (mask, True),
        leave=(1,),
        scratch=[
            pltpu.VMEM((4, windows, heads // 4, QUERY_ROWS, KEY_ROWS), F32),
            pltpu.SemaphoreType.DMA((4,)),
        ],
        name="attend",
    )

    mine = whole(
        mine_kernel,
        place,
        [shape_of((4 * mine[0].shape[0], width), BF)],
        *((m, True) for m in mine),
        after=(heads_out, merged_near, normed1_near),
        name="mine",
    )[0]
    theirs = swap(mine, "wide", 1)
    resid1, normed2 = whole(
        functools.partial(after_kernel, groups=groups),
        place,
        [shape_of((tokens, width), F32), shape_of((tokens, width), BF)],
        (heads_out, True), (resid0, True),
        (row(proj_bias), True), (row(norm2_gain), True), (row(norm2_shift), True),
        (proj_weight, None), (mine, None), (theirs, None),
        scratch=[pltpu.VMEM((width, width), BF), pltpu.SemaphoreType.DMA((1 + 8 * (groups - 1),))],
        name="after",
    )
    blocks = [normed2] + [turn(normed2, "narrow", step) for step in range(1, groups)]

    merged_onward = jnp.stack([tie(merged_onward, normed2), merged_near[1]])
    merged_far = swap(merged_onward, "wide", 2)
    normed1_both = jnp.stack([normed1_cut, tie(normed1_near, normed2)])
    normed1_far = swap(normed1_both, "wide", 4)

    total, units = groups * pad, fc1_weight.shape[1]
    dy_rows, dy_own, d_act = whole(
        functools.partial(slope_kernel, groups=groups, pad=pad, chunk=256),
        place,
        [
            shape_of((total, width), BF),
            shape_of((tokens, width), BF),
            shape_of((total, units), F32),
        ],
        (out_grad, True), (fc2_weight, True),
        scratch=[pltpu.VMEM(out_grad.shape, F32)],
        after=(normed2,),
        name="slope",
    )
    act, d_pre, rows_all, fc1_b_grad, *chunks = whole(
        functools.partial(feed_kernel, pad=pad, chunk=256),
        place,
        [
            shape_of((total, units), BF),
            shape_of((total, units), BF),
            shape_of((total, width), BF),
            shape_of((1, units), F32),
        ]
        + [shape_of((tokens, width), BF)] * 4,
        *((b, True) for b in blocks), (d_act, True), (fc1_weight, True), (row(fc1_bias), True),
        after=(normed1_far, merged_far),
        name="feed",
    )
    arrived = [chunks[0]] + [turn(chunks[j], "narrow", -j) for j in range(1, groups)]

    fc1_kept, fc1_sent = grad_call(place, [arrange(rows_all, "hqc")], [d_pre], 256, 128, "fc1_grad")
    fc2_kept, fc2_sent = grad_call(place, [arrange(act, "hqc")], [dy_rows], 256, 128, "fc2_grad")
    fc1_come, fc2_come = swap(fc1_sent, "wide", 1), swap(fc2_sent, "wide", 1)
    fc1_kept, fc1_sent = join_call(
        place, [(fc1_kept, fc1_come)],
        [
            (F32, [lambda p, y=y: (0, 2 * y + p[2] % 2, 0, 128) for y in range(2)]),
            (BF, [lambda p, y=y: (0, 2 * y + 1 - p[2] % 2, 0, 128) for y in range(2)]),
        ],
        "fc1_join",
    )
    fc2_kept, fc2_sent = join_call(
        place, [(fc2_kept, fc2_come)],
        [
            (F32, [lambda p, x=x: (0, 2 * (p[2] // 2) + x, 0, 128) for x in range(2)]),
            (BF, [lambda p, x=x: (0, 2 * (1 - p[2] // 2) + x, 0, 128) for x in range(2)]),
        ],
        "fc2_join",
    )
    fc1_come, fc2_come = swap(fc1_sent, "wide", 2), swap(fc2_sent, "wide", 4)
    fc1_kept, fc1_sent = join_call(
        place, [(fc1_kept, fc1_come)],
        [
            (F32, [lambda p: (0, p[2] // 2, 0, 128)]),
            (BF, [lambda p: (0, 1 - p[2] // 2, 0, 128)]),
        ],
        "fc1_join2",
    )
    fc2_kept, fc2_sent = join_call(
        place, [(fc2_kept, fc2_come)],
        [
            (F32, [lambda p: (0, p[2] % 2, 0, 128)]),
            (BF, [lambda p: (0, 1 - p[2] % 2, 0, 128)]),
        ],
        "fc2_join2",
    )
    fc1_come, fc2_come = swap(fc1_sent, "wide", 4), swap(fc2_sent, "wide", 2)
    fc1_out = settle(fc1_kept + fc1_come.astype(F32))
    fc2_out = settle(fc2_kept + fc2_come.astype(F32))

    second_kept, second_sent = whole(
        functools.partial(second_kernel, pad=pad, groups=groups),
        place,
        [shape_of((2, tokens, width), BF)] * 2,
        (act, True),
        (fc2_weight, True),
        name="second",
    )
    d_resid1, d_heads = whole(
        functools.partial(back2_kernel, groups=groups),
        place,
        [shape_of((tokens + 8, width), F32), shape_of((tokens, width), BF)],
        *((a, True) for a in arrived),
        (resid1, True), (dy_own, True), (row(norm2_gain), True),
        (proj_weight, None), (mine, None), (theirs, None),
        scratch=[pltpu.VMEM((width, width), BF), pltpu.SemaphoreType.DMA((1 + 8 * (groups - 1),))],
        after=(fc1_sent, fc2_sent, second_sent),
        name="back2",
    )
    second_come = swap(tie(second_sent, d_heads), "narrow", 1)
    d_even, d_odd, rel_part = whole(
        functools.partial(attend_back_kernel, windows=windows, head_dim=head_dim),
        place,
        [shape_of((2, tokens, 3 * width // 4), BF)] * 2 + [shape_of((heads, OFFSETS), F32)],
        (qkv, True), (d_heads, True), (probs, False),
        scratch=[
            pltpu.VMEM((QUERY_ROWS * heads, KEY_ROWS), F32),
            pltpu.VMEM((4, *probs.shape[1:]), F32),
            pltpu.SemaphoreType.DMA((4,)),
        ],
        name="attend_back",
    )
    d_near = swap(d_odd, "wide", 2)

    d_resid0, sums1 = whole(
        back1_kernel,
        place,
        [shape_of((tokens, width), BF), shape_of((5, width), F32)],
        (d_even, True), (d_odd, True), (d_resid1, True), (resid0, True),
        (row(norm1_gain), True), (qkv_weight, False),
        room=56,
        scratch=[pltpu.VMEM((3, width, width), BF), pltpu.SemaphoreType.DMA((3,))],
        after=(fc1_come, fc2_come),
        name="back1",
    )
    r_near = swap(d_resid0, "wide", 4)
    proj_kept, proj_sent = grad_call(
        place, [arrange(heads_out, "nhqc")], [d_resid1], 256, 32, "proj_grad", after=(d_resid0,)
    )
    proj_come = swap(proj_sent, "wide", 1)
    d_onward = jnp.stack([d_even[1], d_near[1]])
    d_far = swap(d_onward, "wide", 4)
    r_both = jnp.stack([d_resid0, r_near])
    r_far = swap(r_both, "wide", 2)

    d_flat, sums0 = whole(
        back0_kernel,
        place,
        [shape_of(flat.shape, BF), shape_of((2 * flat.shape[1] // width, width), F32)],
        (d_resid0, True), (flat, True), (row(merge_gain), True), (merge_weight, False),
        scratch=[pltpu.VMEM(merge_weight.shape, BF), pltpu.SemaphoreType.DMA((1,))],
        after=(d_onward, r_both),
        name="back0",
    )
    patches_grad = d_flat.reshape(patches.shape)

    second_own, second_sent = join_call(
        place, [(second_kept, second_come)],
        [(F32, [lambda p: (0, 0, 0, tokens)]), (BF, [lambda p: (0, 1, 0, tokens)])],
        "second_join",
        after=(d_onward, r_both),
    )
    second_come = swap(second_sent, "narrow", 2)

    own_sums = whole(
        collect_kernel,
        place,
        [shape_of((48, 3 * width // 4), F32)],
        (sums0, True), (sums1, True), (d_resid1, True), (rel_part, True), (fc1_b_grad, True),
        name="collect",
    )[0]
    qkv_kept, qkv_sent = grad_call(
        place,
        [normed1_cut, (normed1_both, 1), (normed1_far, 0), (normed1_far, 1)],
        [(d_even, 0), (d_near, 0), (d_far, 0), (d_far, 1)],
        256, 128, "qkv_grad", sums=own_sums, after=(second_sent,),
    )
    qkv_come = swap(qkv_sent, "wide", 1)
    merge_kept, merge_sent = grad_call(
        place,
        [merged_own, (merged_near, 0), (merged_far, 0), (merged_far, 1)],
        [d_resid0, (r_both, 1), (r_far, 0), (r_far, 1)],
        merged_own.shape[1], merged_own.shape[1] // 2, "merge_grad", after=(qkv_sent,),
    )
    merge_come = swap(merge_sent, "wide", 1)

    side = lambda pick_x: [
        lambda p, n=n, y=y: (0, n, (2 * y + pick_x(p[2] % 2)) * 32, 32)
        for n in range(groups) for y in range(2)
    ]
    proj_kept, proj_sent = join_call(
        place, [(proj_kept, proj_come)],
        [(F32, side(lambda x: x)), (BF, side(lambda x: 1 - x))],
        "proj_join",
        after=(qkv_sent,),
    )
    proj_come = swap(proj_sent, "wide", 2)

    rows = 128 // groups
    qkv_pieces = lambda flip: [
        lambda p, g=g, k=k: (0, g, (2 * k + (p[0] + flip) % 2) * rows, rows)
        for k in range(2) for g in range(4)
    ]
    own_sums, qkv_kept, qkv_sent = join_call(
        place, [(qkv_kept, qkv_come)], [(F32, qkv_pieces(0)), (BF, qkv_pieces(1))], "qkv_join",
        sums=(own_sums, 4),
    )
    qkv_come = swap(qkv_sent, "narrow", 1)

    merge_rows = merged_own.shape[1] // 2 // groups
    merge_pieces = lambda flip: [
        lambda p, k=k: (0, 0, (2 * k + (p[0] + flip) % 2) * merge_rows, merge_rows)
        for k in range(2)
    ]
    merge_kept, merge_sent = join_call(
        place, [(merge_kept, merge_come)],
        [(F32, merge_pieces(0)), (BF, merge_pieces(1))],
        "merge_join",
        after=(qkv_sent,),
    )
    merge_come = swap(merge_sent, "narrow", 1)

    second_pieces = lambda flip: [
        lambda p, g=g: (0, ((p[0] // 2 + flip) % 2) * 4 + g, 0, rows) for g in range(4)
    ]
    own_sums, qkv_kept, qkv_sent = join_call(
        place, [(qkv_kept, qkv_come)],
        [(F32, second_pieces(0)), (BF, second_pieces(1))],
        "qkv_join2",
        sums=(own_sums, 8),
    )
    qkv_come = swap(qkv_sent, "narrow", 2)
    last_pieces = lambda flip, size: [lambda p: (0, (p[0] // 2 + flip) % 2, 0, size)]
    merge_kept, merge_sent = join_call(
        place, [(merge_kept, merge_come)],
        [(F32, last_pieces(0, merge_rows)), (BF, last_pieces(1, merge_rows))],
        "merge_join2",
        after=(qkv_sent,),
    )
    merge_come = swap(merge_sent, "narrow", 2)

    proj_kept, proj_sent = join_call(
        place, [(proj_kept, proj_come)],
        [
            (F32, [lambda p, n=n: (0, 2 * n + p[2] // 2, 0, 32) for n in range(groups)]),
            (BF, [lambda p, n=n: (0, 2 * n + 1 - p[2] // 2, 0, 32) for n in range(groups)]),
        ],
        "proj_join2",
        after=(qkv_sent,),
    )
    proj_come = swap(proj_sent, "wide", 4)
    proj_pieces = lambda flip: [
        lambda p, k=k: (0, 2 * k + (p[0] + flip) % 2, 0, 32) for k in range(2)
    ]
    proj_kept, proj_sent = join_call(
        place, [(proj_kept, proj_come)], [(F32, proj_pieces(0)), (BF, proj_pieces(1))],
        "proj_join3",
    )
    proj_come = swap(proj_sent, "narrow", 1)
    proj_kept, proj_sent = join_call(
        place, [(proj_kept, proj_come)],
        [(F32, last_pieces(0, 32)), (BF, last_pieces(1, 32))],
        "proj_join4",
    )
    proj_come = swap(proj_sent, "narrow", 2)

    own_sums, *cuts = join_call(
        place, [(qkv_kept, qkv_come)],
        [(BF, [lambda p, j=j: (0, p[2] ^ j, 0, rows)]) for j in range(4)],
        "qkv_join3",
        sums=(own_sums, 4),
    )
    cuts = [cuts[0]] + [swap(cuts[j], "wide", 2 * j) for j in (1, 2, 3)]
    qkv_out, all_sums = whole(
        columns_kernel,
        place,
        [shape_of((rows, 3 * width), F32), shape_of(own_sums.shape, F32)],
        *((c, True) for c in cuts), (own_sums, True),
        name="columns",
    )
    qkv_out = settle(qkv_out[None])
    mask = 8
    while mask < wide:
        all_sums = all_sums + swap(all_sums, "wide", mask)
        mask *= 2
    merge_out = settle(merge_kept + merge_come.astype(F32))
    proj_out = settle(proj_kept + proj_come.astype(F32))

    output = low(resid1 + row(fc2_bias) + second_own[0] + second_come[0].astype(F32))

    sums, rel_sum, fc1_b_mine = whole(
        deliver_kernel,
        place,
        [
            shape_of((13, width), F32),
            shape_of((heads, OFFSETS), F32),
            shape_of((units // 128, 128), F32),
        ],
        (all_sums, True),
        name="deliver",
    )
    rel_grad = jnp.transpose(rel_sum[:, : rel_table.shape[0]])
    fc1_b_out = lax.dynamic_index_in_dim(
        fc1_b_mine.reshape(wide, -1), wide_at, 0, keepdims=False
    )

    return (
        output,
        patches_grad,
        sums[0:2].reshape(-1),
        sums[2:4].reshape(-1),
        merge_out,
        sums[4],
        sums[5],
        qkv_out,
        sums[6:9].reshape(-1),
        rel_grad,
        proj_out,
        sums[9],
        sums[10],
        sums[11],
        fc1_out,
        fc1_b_out,
        fc2_out,
        sums[12],
    )


def solution(mesh):
    in_specs = (
        P(("wide", "narrow"), None, None),
        P("wide", None),
        P(),
        P(),
        P(),
        P(),
        P(),
        P(),
        P(),
        P(None, "narrow"),
        P("narrow", None),
        P(),
        P(),
        P(),
        P(None, "narrow"),
        P("narrow"),
        P("narrow", None),
        P(),
        P("wide", None),
    )
    out_specs = (
        P(("wide", "narrow"), None),
        P(("wide", "narrow"), None, None),
        P(),
        P(),
        P(("wide", "narrow"), None),
        P(),
        P(),
        P(("wide", "narrow"), None),
        P(),
        P(),
        P(("narrow", "wide"), None),
        P(),
        P(),
        P(),
        P("wide", "narrow"),
        P(("narrow", "wide")),
        P(("narrow", "wide"), None),
        P(),
    )
    return jax.shard_map(
        on_device, mesh=mesh, in_specs=in_specs, out_specs=out_specs, check_vma=False
    )
```

time: 948 us -> 269 us (0.28)
  waiting for transfers between devices: 726 us -> 88.1 us
  Pallas kernels: 0 us -> 98 us
  matrix products: 91.3 us -> 0 us
  local copies, waits for them, and re-layouts: 58.5 us -> 22.7 us
  starting transfers between devices: 11.8 us -> 47.4 us
  other arithmetic: 25.7 us -> 10.3 us
  between operations: 15.4 us -> 1.65 us
  blocking collectives: 13.2 us -> 0 us
    reduce_scatter x8 -> x0, waiting for transfers between devices: 482 us -> none  [the longest x1 189 us: on_device(): lax.psum_scatter(merge_w_grad, ('wide', 'narrow'), scatter_dimension=0, t...]
    psum x1 -> x0, waiting for transfers between devices: 135 us -> none  [on_device(): lax.psum((jnp.sum(d_merged * merge_hat, 0), jnp.sum(d_merged, 0), jnp.sum...]
    pallas_call x0 -> x40, Pallas kernels: none -> 98 us  [the longest x37 98 us: whole(): pl.pallas_call(body, in_specs=[pl.BlockSpec(memory_space=pltpu.SMEM)] + [...]
    dot_general x23 -> x0, matrix products: 91.3 us -> none  [the longest x10 50.9 us: contract(): lax.dot_general(left, right, (((left_dim,), (right_dim,)), ((), ())), pre...]
    ppermute x0 -> x43, waiting for transfers between devices: none -> 88.1 us  [the longest x34 62.7 us: swap(): return lax.ppermute(array, axis, [(i, i ^ mask) for i in range(size)])]
    all_gather x2 -> x0, waiting for transfers between devices: 62.2 us -> none  [the longest x1 37.1 us: on_device(): lax.all_gather(out2.astype(jnp.bfloat16), 'narrow', axis=0, tiled=True)]
    ppermute x0 -> x43, starting transfers between devices: none -> 47.4 us  [the longest x34 33.5 us: swap(): return lax.ppermute(array, axis, [(i, i ^ mask) for i in range(size)])]
    all_to_all x2 -> x0, waiting for transfers between devices: 46.4 us -> none  [the longest x1 29.3 us: on_device(): lax.all_to_all(d_packed, 'narrow', split_axis=0, concat_axis=2, tiled=True)]
  transfers between devices with their start and end apart: 13 -> 43, of which waited for: 11 -> 19; matrix products, arithmetic and copies ran while one was open for 10% -> 5% of each run, Pallas kernels for 0% -> 30%
where the time goes in v1:
time: 269 us; the launch traced here: 268 us
  Pallas kernels  98 us (36%)
  waiting for transfers between devices  88.1 us (33%)
  starting transfers between devices  47.4 us (18%)
  local copies, waits for them, and re-layouts  22.7 us (8%)
  other arithmetic  10.3 us (4%)
    pallas_call x37, Pallas kernels, whole(): pl.pallas_call(body, in_specs=[pl.BlockSpec(memory_space=pltpu.SMEM)] + [...  98 us
    ppermute x34, waiting for transfers between devices, swap(): return lax.ppermute(array, axis, [(i, i ^ mask) for i in range(size)])  62.7 us
    ppermute x34, starting transfers between devices, swap(): return lax.ppermute(array, axis, [(i, i ^ mask) for i in range(size)])  33.5 us
    ppermute x9, waiting for transfers between devices, turn(): lax.ppermute(array, axis, [(i, (i + step) % size) for i in range(size)])  25.5 us
    unnamed x165, local copies, waits for them, and re-layouts  17.5 us
    ppermute x9, starting transfers between devices, turn(): lax.ppermute(array, axis, [(i, (i + step) % size) for i in range(size)])  13.9 us
  transfers between devices with their start and end apart: 43, of which 19 were waited for; matrix products, arithmetic and copies ran while one was open for 5% of the time, Pallas kernels for 30%

profile of v1, /device:TPU:0, one launch (start us, length us, event | category | flops | bytes accessed | tf_op | source)
XLA Modules:
  0.0 268.2 jit_solution(1361241195769333031)
XLA Ops:
  4.0 5.0 %collective-permute-start.2 = (bf16[48,1024]{1,0:T(8,128)(2,1)}, bf16[48,1024]{1,0:T(8,128)(2,1)}, u32[]{:S(2)}, u32[]{:S(2)}) collective-permute-start(bf16[48,1024]{1,0:T(8,128)(2,1)} %pack.1.refs_0_), channel_id=1, source_target_pairs={{0,3},{1,0},{2,1},{3,2},{4,7},{5,4},{6,5},{7,6},{8,11},{9,8},{10,9... | collective-permute-start | bytes 294920 | tf_op jit(solution)/shard_map/ppermute | solution.py:125
  10.4 4.8 %front.1 = (bf16[200,2048]{1,0:T(8,128)(2,1)S(1)}, f32[200,1024]{1,0:T(8,128)S(1)}, bf16[200,1024]{1,0:T(8,128)(2,1)}, bf16[200,3072]{1,0:T(8,128)(2,1)S(1)}) custom-call(s32[3]{0:T(128)S(1)} %pad_add_fusion.place_ref, bf16[200,2048]{1,0:T(8,128)(2,1)S(1)} %bitcast.58, f32[1,2048]{1,0:T(1,128)S(1)} %bitcast.64, f32[1,2048]{1,0:T(1,128)S(1)} %bitcast.63, ...), custom_call_target="tpu_custom_call" | custom-call | flops 99999997952 | tf_op jit(solution)/shard_map/front/pallas_call | solution.py:88
  27.8 6.7 %attend.1 = (bf16[200,1024]{1,0:T(8,128)(2,1)S(1)}, f32[52,2,8,112,128]{4,3,2,1,0:T(8,128)}) custom-call(s32[3]{0:T(128)S(1)} %pad_add_fusion.place_ref, bf16[200,3072]{1,0:T(8,128)(2,1)S(1)} %get-tuple-element.99.refs_0_, f32[3584,128]{1,0:T(8,128)S(1)} %spread.1.refs_1_, f32[2,1,128]{2,1,0:T(1,128)S(1)} %and_select_fusion.refs_2_), custom_call_target="tpu_custom_call" | custom-call | flops 99999997952 | tf_op jit(solution)/shard_map/attend/pallas_call | solution.py:88
  41.4 4.6 %after.1 = (f32[200,1024]{1,0:T(8,128)S(1)}, bf16[200,1024]{1,0:T(8,128)(2,1)}) custom-call(s32[3]{0:T(128)S(1)} %pad_add_fusion.place_ref, bf16[200,1024]{1,0:T(8,128)(2,1)S(1)} %get-tuple-element.100.refs_4_.refs_0_, f32[200,1024]{1,0:T(8,128)S(1)} %get-tuple-element.101.refs_1_.refs_3_, f32[1,1024]{1,0:T(1,128)S(1)} %bitcast.67, f32[1,1024]{1,0:T(1,128)S(1)} %bitcast.70, ...), custom_call_target="tpu_custom_call" | custom-call | flops 99999997952 | tf_op jit(solution)/shard_map/after/pallas_call | solution.py:88
  57.3 3.5 %slope.1 = (bf16[832,1024]{1,0:T(8,128)(2,1)S(1)}, bf16[200,1024]{1,0:T(8,128)(2,1)S(1)}, f32[832,1024]{1,0:T(8,128)S(1)}) custom-call(s32[3]{0:T(128)S(1)} %pad_add_fusion.place_ref, bf16[800,1024]{1,0:T(8,128)(2,1)S(1)} %copy-done.33, bf16[1024,1024]{1,0:T(8,128)(2,1)S(1)} %copy-done.31, bf16[200,1024]{1,0:T(8,128)(2,1)} %get-tuple-element.106.refs_2_.refs_1_.refs_0_), custom_call_target="tpu_custom_call" | custom-call | flops 99999997952 | tf_op jit(solution)/shard_map/slope/pallas_call | solution.py:88
  63.0 23.1 %collective-permute-done.10.refs_2_ = bf16[200,1024]{1,0:T(8,128)(2,1)} collective-permute-done((bf16[200,1024]{1,0:T(8,128)(2,1)}, bf16[200,1024]{1,0:T(8,128)(2,1)}, u32[]{:S(2)}, u32[]{:S(2)}) %collective-permute-start.10) | collective-permute-done | bytes 409632 | tf_op jit(solution)/shard_map/ppermute | solution.py:125
  86.2 9.2 %feed.1 = (bf16[832,1024]{1,0:T(8,128)(2,1)S(1)}, bf16[832,1024]{1,0:T(8,128)(2,1)S(1)}, bf16[832,1024]{1,0:T(8,128)(2,1)S(1)}, f32[1,1024]{1,0:T(1,128)S(1)}, b...) custom-call(s32[3]{0:T(128)S(1)} %pad_add_fusion.place_ref, ...), custom_call_target="tpu_custom_call" | custom-call | flops 99999997952 | tf_op jit(solution)/shard_map/feed/pallas_call | solution.py:88
  101.5 4.0 %fc2_grad.1 = (f32[4,128,1024]{2,1,0:T(8,128)S(1)}, bf16[4,128,1024]{2,1,0:T(8,128)(2,1)S(1)}) custom-call(s32[3]{0:T(128)S(1)} %pad_add_fusion.place_ref, bf16[832,1024]{1,0:T(8,128)(2,1)S(1)} %get-tuple-element.109.refs_0_, bf16[832,1024]{1,0:T(8,128)(2,1)S(1)} %get-tuple-element.124.refs_1_), custom_call_target="tpu_custom_call" | custom-call | flops 99999997952 | tf_op jit(solution)/shard_map/fc2_grad/pallas_call | solution.py:88
  105.6 3.8 %fc1_grad.1 = (f32[4,128,1024]{2,1,0:T(8,128)S(1)}, bf16[4,128,1024]{2,1,0:T(8,128)(2,1)S(1)}) custom-call(s32[3]{0:T(128)S(1)} %pad_add_fusion.place_ref, bf16[832,1024]{1,0:T(8,128)(2,1)S(1)} %get-tuple-element.117.refs_0_, bf16[832,1024]{1,0:T(8,128)(2,1)S(1)} %get-tuple-element.118.refs_1_), custom_call_target="tpu_custom_call" | custom-call | flops 99999997952 | tf_op jit(solution)/shard_map/fc1_grad/pallas_call | solution.py:88
  114.7 10.0 %collective-permute-done.20.refs_1_ = bf16[2,128,1024]{2,1,0:T(8,128)(2,1)S(1)} collective-permute-done((bf16[2,128,1024]{2,1,0:T(8,128)(2,1)S(1)}, bf16[2,128,1024]{2,1,0:T(8,128)(2,1)S(1)}, u32[]{:S(2)}, u32[]{:S(2)}) %collective-permute-start.20) | collective-permute-done | bytes 524320 | tf_op jit(solution)/shard_map/ppermute | solution.py:120
  132.7 5.5 %back2.1 = (f32[208,1024]{1,0:T(8,128)S(1)}, bf16[200,1024]{1,0:T(8,128)(2,1)S(1)}) custom-call(s32[3]{0:T(128)S(1)} %pad_add_fusion.place_ref, bf16[200,1024]{1,0:T(8,128)(2,1)S(1)} %get-tuple-element.112.refs_0_, bf16[200,1024]{1,0:T(8,128)(2,1)} %collective-permute-done.14.refs_1_, bf16[200,1024]{1,0:T(8,128)(2,1)} %collective-permute-done.15.refs_2_, ...), custom_call_target="tpu_custom_call" | custom-call | flops 99999997952 | tf_op jit(solution)/shard_map/back2/pallas_call | solution.py:88
  139.1 9.4 %attend_back.1 = (bf16[2,200,768]{2,1,0:T(8,128)(2,1)S(1)}, bf16[2,200,768]{2,1,0:T(8,128)(2,1)}, f32[32,384]{1,0:T(8,128)S(1)}) custom-call(s32[3]{0:T(128)S(1)} %pad_add_fusion.place_ref, bf16[200,3072]{1,0:T(8,128)(2,1)S(1)} %copy-done.4, bf16[200,1024]{1,0:T(8,128)(2,1)S(1)} %get-tuple-element.130.refs_1_, f32[52,2,8,112,128]{4,3,2,1,0:T(8,128)} %get-tuple-element.131.refs_2_), custom_call_target="tpu_custom_call" | custom-call | flops 7200000000 | tf_op jit(solution)/shard_map/attend_back/pallas_call | solution.py:88
  150.2 6.7 %back1.1 = (bf16[200,1024]{1,0:T(8,128)(2,1)}, f32[5,1024]{1,0:T(8,128)}) custom-call(s32[3]{0:T(128)} %copy-done.25, bf16[2,200,768]{2,1,0:T(8,128)(2,1)} %copy-done.23, bf16[2,200,768]{2,1,0:T(8,128)(2,1)} %get-tuple-element.133.refs_1_, f32[208,1024]{1,0:T(8,128)} %copy-done.66, f32[200,1024]{1,0:T(8,128)} %copy-done.74, f32[1,1024]{1,0:T(1,128)} %bitcast.72, ...), custom_call_target="tpu_custom_call" | custom-call | flops 4100000000 | tf_op jit(solution)/shard_map/back1/pallas_call | solution.py:88
  164.0 5.6 %collective-permute-done.25 = bf16[200,1024]{1,0:T(8,128)(2,1)S(1)} collective-permute-done((bf16[200,1024]{1,0:T(8,128)(2,1)}, bf16[200,1024]{1,0:T(8,128)(2,1)S(1)}, u32[]{:S(2)}, u32[]{:S(2)}) %collective-permute-start.25) | collective-permute-done | bytes 409632 | tf_op jit(solution)/shard_map/ppermute | solution.py:120
  170.4 3.4 %back0.1 = (bf16[200,2048]{1,0:T(8,128)(2,1)S(1)}, f32[4,1024]{1,0:T(4,128)S(1)}) custom-call(s32[3]{0:T(128)S(1)} %copy-done.26, bf16[200,1024]{1,0:T(8,128)(2,1)S(1)} %copy-done.22, bf16[200,2048]{1,0:T(8,128)(2,1)S(1)} %bitcast.59, f32[1,2048]{1,0:T(1,128)S(1)} %bitcast.65, bf16[2048,1024]{1,0:T(8,128)(2,1)S(1)} %copy-done.29, ...), custom_call_target="tpu_custom_call" | custom-call | flops 3300000000 | tf_op jit(solution)/shard_map/back0/pallas_call | solution.py:88
  176.9 3.8 %collective-permute-done.27.refs_6_.refs_7_ = bf16[2,200,768]{2,1,0:T(8,128)(2,1)S(1)} collective-permute-done((bf16[2,200,768]{2,1,0:T(8,128)(2,1)S(1)}, bf16[2,200,768]{2,1,0:T(8,128)(2,1)S(1)}, u32[]{:S(2)}, u32[]{:S(2)}) %collective-permute-start.27) | collective-permute-done | bytes 614432 | tf_op jit(solution)/shard_map/ppermute | solution.py:120
  180.6 5.0 %qkv_grad.1 = (f32[4,128,768]{2,1,0:T(8,128)S(1)}, bf16[5,128,768]{2,1,0:T(8,128)(2,1)}) custom-call(s32[3]{0:T(128)S(1)} %copy-done.26, bf16[200,1024]{1,0:T(8,128)(2,1)} %get-tuple-element.104.refs_0_, bf16[2,200,1024]{2,1,0:T(8,128)(2,1)S(1)} %copy-done.10, bf16[2,200,1024]{2,1,0:T(8,128)(2,1)S(1)} %copy-done.37, bf16[2,200,1024]{2,1,0:T(8,128)(2,1)S(1)} %copy-done.37, ...), custom_call_target="tpu_custom_call" | custom-call | flops 5000000000 | tf_op jit(solution)/shard_map/qkv_grad/pallas_call | solution.py:88
  186.8 3.2 %merge_grad.1 = (f32[1,256,1024]{2,1,0:T(8,128)S(1)}, bf16[1,256,1024]{2,1,0:T(8,128)(2,1)}) custom-call(s32[3]{0:T(128)S(1)} %copy-done.26, bf16[200,512]{1,0:T(8,128)(2,1)S(1)} %get-tuple-element.158.refs_0_, bf16[2,200,512]{2,1,0:T(8,128)(2,1)} %collective-permute-done.6.refs_5_.refs_1_, bf16[2,200,512]{2,1,0:T(8,128)(2,1)S(1)} %copy-done.46, ...), custom_call_target="tpu_custom_call" | custom-call | flops 4200000000 | tf_op jit(solution)/shard_map/merge_grad/pallas_call | solution.py:88
  208.2 12.9 %collective-permute-done.29.refs_1_ = bf16[11,32,768]{2,1,0:T(8,128)(2,1)S(1)} collective-permute-done((bf16[11,32,768]{2,1,0:T(8,128)(2,1)S(1)}, bf16[11,32,768]{2,1,0:T(8,128)(2,1)S(1)}, u32[]{:S(2)}, u32[]{:S(2)}) %collective-permute-start.29) | collective-permute-done | bytes 540704 | tf_op jit(solution)/shard_map/ppermute | solution.py:120
  232.3 4.2 %collective-permute-done.40.refs_1_ = bf16[4,32,1024]{2,1,0:T(8,128)(2,1)S(1)} collective-permute-done((bf16[4,32,1024]{2,1,0:T(8,128)(2,1)S(1)}, bf16[4,32,1024]{2,1,0:T(8,128)(2,1)S(1)}, u32[]{:S(2)}, u32[]{:S(2)}) %collective-permute-start.40) | collective-permute-done | bytes 262176 | tf_op jit(solution)/shard_map/ppermute | solution.py:120
  239.0 3.8 %collective-permute-done.41.refs_1_ = bf16[2,32,1024]{2,1,0:T(8,128)(2,1)S(1)} collective-permute-done((bf16[2,32,1024]{2,1,0:T(8,128)(2,1)S(1)}, bf16[2,32,1024]{2,1,0:T(8,128)(2,1)S(1)}, u32[]{:S(2)}, u32[]{:S(2)}) %collective-permute-start.41) | collective-permute-done | bytes 131104 | tf_op jit(solution)/shard_map/ppermute | solution.py:120
  246.0 4.9 %collective-permute-done.30.refs_1_ = bf16[7,32,768]{2,1,0:T(8,128)(2,1)S(1)} collective-permute-done((bf16[7,32,768]{2,1,0:T(8,128)(2,1)S(1)}, bf16[7,32,768]{2,1,0:T(8,128)(2,1)S(1)}, u32[]{:S(2)}, u32[]{:S(2)}) %collective-permute-start.30) | collective-permute-done | bytes 344096 | tf_op jit(solution)/shard_map/ppermute | solution.py:120
  255.7 3.7 %collective-permute-done.31.refs_1_ = bf16[4,32,768]{2,1,0:T(8,128)(2,1)S(1)} collective-permute-done((bf16[4,32,768]{2,1,0:T(8,128)(2,1)S(1)}, bf16[4,32,768]{2,1,0:T(8,128)(2,1)S(1)}, u32[]{:S(2)}, u32[]{:S(2)}) %collective-permute-start.31) | collective-permute-done | bytes 196640 | tf_op jit(solution)/shard_map/ppermute | solution.py:120
  259.4 3.3 %collective-permute-done.32.refs_2_ = bf16[4,32,768]{2,1,0:T(8,128)(2,1)S(1)} collective-permute-done((bf16[4,32,768]{2,1,0:T(8,128)(2,1)S(1)}, bf16[4,32,768]{2,1,0:T(8,128)(2,1)S(1)}, u32[]{:S(2)}, u32[]{:S(2)}) %collective-permute-start.32) | collective-permute-done | bytes 196640 | tf_op jit(solution)/shard_map/ppermute | solution.py:120
  (291 shorter events, 116.5 us)
Async XLA Ops:
  4.0 16.4 %collective-permute-start.2 = (bf16[48,1024]{1,0:T(8,128)(2,1)}, bf16[48,1024]{1,0:T(8,128)(2,1)}, u32[]{:S(2)}, u32[]{:S(2)}) collective-permute-start(bf16[48,1024]{1,0:T(8,128)(2,1)} %pack.1.refs_0_), channel_id=1, source_target_pairs={{0,3},{1,0},{2,1},{3,2},{4,7},{5,4},{6,5},{7,6},{8,11},{9,8},{10,9... | collective-permute-start | bytes 294920 | tf_op jit(solution)/shard_map/ppermute | solution.py:125
  17.3 20.4 %collective-permute-start.6 = (bf16[2,200,512]{2,1,0:T(8,128)(2,1)}, bf16[2,200,512]{2,1,0:T(8,128)(2,1)}, u32[]{:S(2)}, u32[]{:S(2)}) collective-permute-start(bf16[2,200,512]{2,1,0:T(8,128)(2,1)} %get-tuple-element.103), channel_id=1, source_target_pairs={{0,16},{4,20},{8,24},{12,28},{16,0},{20,4},{24,8},{28,12},{1,17},{... | collective-permute-start | bytes 1228808 | tf_op jit(solution)/shard_map/ppermute | solution.py:120
  18.8 18.8 %collective-permute-start.7 = (bf16[200,1024]{1,0:T(8,128)(2,1)}, bf16[200,1024]{1,0:T(8,128)(2,1)}, u32[]{:S(2)}, u32[]{:S(2)}) collective-permute-start(bf16[200,1024]{1,0:T(8,128)(2,1)} %get-tuple-element.104.refs_0_), channel_id=1, source_target_pairs={{0,8},{4,12},{8,0},{12,4},{16,24},{20,28},{24,16},{28,20},{1,9},{5... | collective-permute-start | bytes 1228808 | tf_op jit(solution)/shard_map/ppermute | solution.py:120
  46.0 17.0 %collective-permute-start.11 = (bf16[200,1024]{1,0:T(8,128)(2,1)}, bf16[200,1024]{1,0:T(8,128)(2,1)}, u32[]{:S(2)}, u32[]{:S(2)}) collective-permute-start(bf16[200,1024]{1,0:T(8,128)(2,1)} %get-tuple-element.106.refs_2_.refs_1_.refs_0_), channel_id=1, source_target_pairs={{0,3},{1,0},{2,1},{3,2},{4,7},{5,4},{6,5},{7,6},{8,11},{9,8},{10,9... | collective-permute-start | bytes 1228808 | tf_op jit(solution)/shard_map/ppermute | solution.py:125
  49.1 37.0 %collective-permute-start.10 = (bf16[200,1024]{1,0:T(8,128)(2,1)}, bf16[200,1024]{1,0:T(8,128)(2,1)}, u32[]{:S(2)}, u32[]{:S(2)}) collective-permute-start(bf16[200,1024]{1,0:T(8,128)(2,1)} %get-tuple-element.106.refs_2_.refs_1_.refs_0_), channel_id=1, source_target_pairs={{0,2},{1,3},{2,0},{3,1},{4,6},{5,7},{6,4},{7,5},{8,10},{9,11},{10,... | collective-permute-start | bytes 1228808 | tf_op jit(solution)/shard_map/ppermute | solution.py:125
  50.0 36.1 %collective-permute-start.9 = (bf16[200,1024]{1,0:T(8,128)(2,1)}, bf16[200,1024]{1,0:T(8,128)(2,1)}, u32[]{:S(2)}, u32[]{:S(2)}) collective-permute-start(bf16[200,1024]{1,0:T(8,128)(2,1)} %get-tuple-element.106.refs_2_.refs_1_.refs_0_), channel_id=1, source_target_pairs={{0,1},{1,2},{2,3},{3,0},{4,5},{5,6},{6,7},{7,4},{8,9},{9,10},{10,1... | collective-permute-start | bytes 1228808 | tf_op jit(solution)/shard_map/ppermute | solution.py:125
  54.8 31.3 %collective-permute-start.12 = (bf16[2,200,1024]{2,1,0:T(8,128)(2,1)S(1)}, bf16[2,200,1024]{2,1,0:T(8,128)(2,1)S(1)}, u32[]{:S(2)}, u32[]{:S(2)}) collective-permute-start(bf16[2,200,1024]{2,1,0:T(8,128)(2,1)S(1)} %pad_maximum_fusion.refs_1_), channel_id=1, source_target_pairs={{0,16},{4,20},{8,24},{12,28},{16,0},{20,4},{24,8},{28,12},{1,17},{... | collective-permute-start | bytes 2457608 | tf_op jit(solution)/shard_map/ppermute | solution.py:120
  95.4 34.9 %collective-permute-start.14 = (bf16[200,1024]{1,0:T(8,128)(2,1)}, bf16[200,1024]{1,0:T(8,128)(2,1)}, u32[]{:S(2)}, u32[]{:S(2)}) collective-permute-start(bf16[200,1024]{1,0:T(8,128)(2,1)} %get-tuple-element.113), channel_id=1, source_target_pairs={{0,3},{1,0},{2,1},{3,2},{4,7},{5,4},{6,5},{7,6},{8,11},{9,8},{10,9... | collective-permute-start | bytes 1228808 | tf_op jit(solution)/shard_map/ppermute | solution.py:125
  95.5 37.2 %collective-permute-start.15 = (bf16[200,1024]{1,0:T(8,128)(2,1)}, bf16[200,1024]{1,0:T(8,128)(2,1)}, u32[]{:S(2)}, u32[]{:S(2)}) collective-permute-start(bf16[200,1024]{1,0:T(8,128)(2,1)} %get-tuple-element.114), channel_id=1, source_target_pairs={{0,2},{1,3},{2,0},{3,1},{4,6},{5,7},{6,4},{7,5},{8,10},{9,11},{10,... | collective-permute-start | bytes 1228808 | tf_op jit(solution)/shard_map/ppermute | solution.py:125
  97.0 35.6 %collective-permute-start.16 = (bf16[200,1024]{1,0:T(8,128)(2,1)}, bf16[200,1024]{1,0:T(8,128)(2,1)}, u32[]{:S(2)}, u32[]{:S(2)}) collective-permute-start(bf16[200,1024]{1,0:T(8,128)(2,1)} %get-tuple-element.115), channel_id=1, source_target_pairs={{0,1},{1,2},{2,3},{3,0},{4,5},{5,6},{6,7},{7,4},{8,9},{9,10},{10,1... | collective-permute-start | bytes 1228808 | tf_op jit(solution)/shard_map/ppermute | solution.py:125
  110.8 13.9 %collective-permute-start.20 = (bf16[2,128,1024]{2,1,0:T(8,128)(2,1)S(1)}, bf16[2,128,1024]{2,1,0:T(8,128)(2,1)S(1)}, u32[]{:S(2)}, u32[]{:S(2)}) collective-permute-start(bf16[2,128,1024]{2,1,0:T(8,128)(2,1)S(1)} %get-tuple-element.128), channel_id=1, source_target_pairs={{0,16},{4,20},{8,24},{12,28},{16,0},{20,4},{24,8},{28,12},{1,17},{... | collective-permute-start | bytes 1572872 | tf_op jit(solution)/shard_map/ppermute | solution.py:120
  113.1 15.2 %collective-permute-start.18 = (bf16[2,128,1024]{2,1,0:T(8,128)(2,1)S(1)}, bf16[2,128,1024]{2,1,0:T(8,128)(2,1)S(1)}, u32[]{:S(2)}, u32[]{:S(2)}) collective-permute-start(bf16[2,128,1024]{2,1,0:T(8,128)(2,1)S(1)} %get-tuple-element.122), channel_id=1, source_target_pairs={{0,8},{4,12},{8,0},{12,4},{16,24},{20,28},{24,16},{28,20},{1,9},{5... | collective-permute-start | bytes 1572872 | tf_op jit(solution)/shard_map/ppermute | solution.py:120
  126.8 23.3 %collective-permute-start.24 = (bf16[1,128,1024]{2,1,0:T(8,128)(2,1)}, bf16[1,128,1024]{2,1,0:T(8,128)(2,1)}, u32[]{:S(2)}, u32[]{:S(2)}) collective-permute-start(bf16[1,128,1024]{2,1,0:T(8,128)(2,1)} %get-tuple-element.129.refs_11_), channel_id=1, source_target_pairs={{0,8},{4,12},{8,0},{12,4},{16,24},{20,28},{24,16},{28,20},{1,9},{5... | collective-permute-start | bytes 786440 | tf_op jit(solution)/shard_map/ppermute | solution.py:120
  129.8 20.3 %collective-permute-start.23 = (bf16[1,128,1024]{2,1,0:T(8,128)(2,1)S(1)}, bf16[1,128,1024]{2,1,0:T(8,128)(2,1)}, u32[]{:S(2)}, u32[]{:S(2)}) collective-permute-start(bf16[1,128,1024]{2,1,0:T(8,128)(2,1)S(1)} %get-tuple-element.123.refs_10_), channel_id=1, source_target_pairs={{0,16},{4,20},{8,24},{12,28},{16,0},{20,4},{24,8},{28,12},{1,17},{... | collective-permute-start | bytes 786440 | tf_op jit(solution)/shard_map/ppermute | solution.py:120
  148.6 14.8 %collective-permute-start.22 = (bf16[2,200,768]{2,1,0:T(8,128)(2,1)}, bf16[2,200,768]{2,1,0:T(8,128)(2,1)S(1)}, u32[]{:S(2)}, u32[]{:S(2)}) collective-permute-start(bf16[2,200,768]{2,1,0:T(8,128)(2,1)} %get-tuple-element.133.refs_1_), channel_id=1, source_target_pairs={{0,8},{4,12},{8,0},{12,4},{16,24},{20,28},{24,16},{28,20},{1,9},{5... | collective-permute-start | bytes 1843208 | tf_op jit(solution)/shard_map/ppermute | solution.py:120
  150.1 24.3 %collective-permute-start.21 = (bf16[2,200,1024]{2,1,0:T(8,128)(2,1)}, bf16[2,200,1024]{2,1,0:T(8,128)(2,1)S(1)}, u32[]{:S(2)}, u32[]{:S(2)}) collective-permute-start(bf16[2,200,1024]{2,1,0:T(8,128)(2,1)} %tie.5), channel_id=1, source_target_pairs={{0,1},{1,0},{2,3},{3,2},{4,5},{5,4},{6,7},{7,6},{8,9},{9,8},{10,11... | collective-permute-start | bytes 2457608 | tf_op jit(solution)/shard_map/ppermute | solution.py:120
  161.7 30.0 %collective-permute-start.38 = (bf16[4,128,1024]{2,1,0:T(8,128)(2,1)}, bf16[4,128,1024]{2,1,0:T(8,128)(2,1)S(1)}, u32[]{:S(2)}, u32[]{:S(2)}) collective-permute-start(bf16[4,128,1024]{2,1,0:T(8,128)(2,1)} %get-tuple-element.168), channel_id=1, source_target_pairs={{0,4},{4,0},{8,12},{12,8},{16,20},{20,16},{24,28},{28,24},{1,5},{5... | collective-permute-start | bytes 3145736 | tf_op jit(solution)/shard_map/ppermute | solution.py:120
  163.5 17.2 %collective-permute-start.27 = (bf16[2,200,768]{2,1,0:T(8,128)(2,1)S(1)}, bf16[2,200,768]{2,1,0:T(8,128)(2,1)S(1)}, u32[]{:S(2)}, u32[]{:S(2)}) collective-permute-start(bf16[2,200,768]{2,1,0:T(8,128)(2,1)S(1)} %pad_maximum_fusion.2.refs_2_.refs_4_), channel_id=1, source_target_pairs={{0,16},{4,20},{8,24},{12,28},{16,0},{20,4},{24,8},{28,12},{1,17},{... | collective-permute-start | bytes 1843208 | tf_op jit(solution)/shard_map/ppermute | solution.py:120
  169.7 17.1 %collective-permute-start.34 = (bf16[2,200,1024]{2,1,0:T(8,128)(2,1)S(1)}, bf16[2,200,1024]{2,1,0:T(8,128)(2,1)S(1)}, u32[]{:S(2)}, u32[]{:S(2)}) collective-permute-start(bf16[2,200,1024]{2,1,0:T(8,128)(2,1)S(1)} %pad_maximum_fusion.1.refs_3_.refs_5_), channel_id=1, source_target_pairs={{0,8},{4,12},{8,0},{12,4},{16,24},{20,28},{24,16},{28,20},{1,9},{5... | collective-permute-start | bytes 2457608 | tf_op jit(solution)/shard_map/ppermute | solution.py:120
  194.1 34.8 %collective-permute-start.39 = (bf16[8,32,1024]{2,1,0:T(8,128)(2,1)}, bf16[8,32,1024]{2,1,0:T(8,128)(2,1)S(1)}, u32[]{:S(2)}, u32[]{:S(2)}) collective-permute-start(bf16[8,32,1024]{2,1,0:T(8,128)(2,1)} %get-tuple-element.170), channel_id=1, source_target_pairs={{0,8},{4,12},{8,0},{12,4},{16,24},{20,28},{24,16},{28,20},{1,9},{5... | collective-permute-start | bytes 1572872 | tf_op jit(solution)/shard_map/ppermute | solution.py:120
  197.2 24.0 %collective-permute-start.29 = (bf16[11,32,768]{2,1,0:T(8,128)(2,1)S(1)}, bf16[11,32,768]{2,1,0:T(8,128)(2,1)S(1)}, u32[]{:S(2)}, u32[]{:S(2)}) collective-permute-start(bf16[11,32,768]{2,1,0:T(8,128)(2,1)S(1)} %get-tuple-element.146.refs_2_), channel_id=1, source_target_pairs={{0,1},{1,0},{2,3},{3,2},{4,5},{5,4},{6,7},{7,6},{8,9},{9,8},{10,11... | collective-permute-start | bytes 1622024 | tf_op jit(solution)/shard_map/ppermute | solution.py:120
  200.3 29.9 %collective-permute-start.26 = (bf16[1,200,1024]{2,1,0:T(8,128)(2,1)S(1)}, bf16[1,200,1024]{2,1,0:T(8,128)(2,1)}, u32[]{:S(2)}, u32[]{:S(2)}) collective-permute-start(bf16[1,200,1024]{2,1,0:T(8,128)(2,1)S(1)} %copy-done.48), channel_id=1, source_target_pairs={{0,2},{1,3},{2,0},{3,1},{4,6},{5,7},{6,4},{7,5},{8,10},{9,11},{10,... | collective-permute-start | bytes 1228808 | tf_op jit(solution)/shard_map/ppermute | solution.py:120
  204.1 21.4 %collective-permute-start.36 = (bf16[2,64,1024]{2,1,0:T(8,128)(2,1)S(1)}, bf16[2,64,1024]{2,1,0:T(8,128)(2,1)S(1)}, u32[]{:S(2)}, u32[]{:S(2)}) collective-permute-start(bf16[2,64,1024]{2,1,0:T(8,128)(2,1)S(1)} %get-tuple-element.162), channel_id=1, source_target_pairs={{0,1},{1,0},{2,3},{3,2},{4,5},{5,4},{6,7},{7,6},{8,9},{9,8},{10,11... | collective-permute-start | bytes 786440 | tf_op jit(solution)/shard_map/ppermute | solution.py:120
  232.1 18.7 %collective-permute-start.30 = (bf16[7,32,768]{2,1,0:T(8,128)(2,1)S(1)}, bf16[7,32,768]{2,1,0:T(8,128)(2,1)S(1)}, u32[]{:S(2)}, u32[]{:S(2)}) collective-permute-start(bf16[7,32,768]{2,1,0:T(8,128)(2,1)S(1)} %get-tuple-element.149.refs_2_), channel_id=1, source_target_pairs={{0,2},{1,3},{2,0},{3,1},{4,6},{5,7},{6,4},{7,5},{8,10},{9,11},{10,... | collective-permute-start | bytes 1032200 | tf_op jit(solution)/shard_map/ppermute | solution.py:120
  (99 other events, 957.0 us)

commit v2 on v1

--- a/solution.py
+++ b/solution.py
@@ -15,13 +15,10 @@
 MEBI = 1024 * 1024
 PROBS_ROOM = 52
 WAIT_US = 100.0
-WEIGHT_US = {
-    "attend_back": 7.2, "back1": 4.1, "proj_grad": 3.1, "back0": 3.3, "qkv_grad": 5.0, "merge_grad": 4.2,
-    "second_join": 2.0, "qkv_join": 1.5,
-}
+WEIGHT_US = {"back1": 20, "proj_grad": 20, "back0": 20, "second_join": 20, "proj_join": 20}
 WEIGHT_US |= dict.fromkeys(
     ("pack", "front", "cut", "pieces", "spread", "attend", "mine", "after", "slope", "feed", "second", "fc1_grad",
-     "fc2_grad", "fc1_join", "fc2_join", "fc1_join2", "fc2_join2", "back2"), WAIT_US
+     "fc2_grad", "fc1_join", "fc2_join", "fc1_join2", "fc2_join2"), WAIT_US
 )
 FLOPS_PER_US = 10**9
 BF = jnp.bfloat16
@@ -78,27 +75,32 @@
     return jax.ShapeDtypeStruct(shape, dtype)
 
 
-def whole(kernel, place, outs, *operands, leave=(), scratch=(), after=(), room=20, name=None):
+def whole(
+    kernel, place, outs, *operands, leave=(), scratch=(), after=(), through=(), room=20, name=None
+):
     arrays = [a for a, _ in operands]
-    count, skip = len(arrays), len(after)
+    count, skip, given = len(arrays), len(after) + len(through), len(outs)
 
     def body(place_ref, *refs):
-        kernel(place_ref, *refs[:count], *refs[count + skip :])
+        own_outs = refs[count + skip : count + skip + given]
+        kernel(place_ref, *refs[:count], *own_outs, *refs[count + skip + given + len(through) :])
 
     return pl.pallas_call(
         body,
         in_specs=[pl.BlockSpec(memory_space=pltpu.SMEM)]
         + [{True: held, False: outside, None: stays}[inside]() for _, inside in operands]
         + [stays()] * skip,
-        out_specs=[outside() if k in leave else held() for k in range(len(outs))],
-        out_shape=list(outs),
+        out_specs=[outside() if k in leave else held() for k in range(given)]
+        + [stays()] * len(through),
+        out_shape=list(outs) + [shape_of(a.shape, a.dtype) for a in through],
+        input_output_aliases={1 + count + len(after) + k: given + k for k in range(len(through))},
         scratch_shapes=list(scratch),
         compiler_params=pltpu.CompilerParams(vmem_limit_bytes=room * MEBI),
         cost_estimate=pl.CostEstimate(
-            flops=int(WEIGHT_US.get(name, 0.7) * FLOPS_PER_US), bytes_accessed=0, transcendentals=0
+            flops=int(WEIGHT_US.get(name, 5) * FLOPS_PER_US), bytes_accessed=0, transcendentals=0
         ),
         name=name,
-    )(place, *arrays, *after)
+    )(place, *arrays, *after, *through)
 
 
 def tie(array, *after):
@@ -198,12 +200,12 @@
     return total
 
 
-def join_call(place, groups, outs, name, after=(), sums=None):
+def join_call(place, groups, outs, name, after=(), through=(), sums=None):
     width = groups[0][0].shape[2]
     counts = [len(sources) for sources in groups]
     count = sum(counts)
     rows_of = [pieces[0]((0, 0, 0))[3] for _, pieces in outs]
-    more = 2 * sums[0].shape[0] // rows_of[1] if sums else 0
+    more = -(-sums[0].shape[0] // rows_of[1]) if sums else 0
     shapes = [
         shape_of((len(pieces) + (more if k else 0), rows, width), dtype)
         for k, ((dtype, pieces), rows) in enumerate(zip(outs, rows_of))
@@ -231,13 +233,12 @@
 
     arrays = [s for sources in groups for s in sources] + ([sums[0]] if sums else [])
     return whole(
-        kernel, place, shapes, *((s, True) for s in arrays), after=after, name=name
+        kernel, place, shapes, *((s, True) for s in arrays), after=after, through=through, name=name
     )
 
 
 def give_sums(ref, first, values):
-    high = low(values)
-    parts = jnp.concatenate([high, low(values - high.astype(F32))], 0)
+    parts = low(values)
     size = ref.shape[1]
     for k in range(parts.shape[0] // size):
         ref[first + k] = parts[k * size : (k + 1) * size]
@@ -248,9 +249,8 @@
 
 def take_sums(ref, first, rows):
     size = ref.shape[1]
-    blocks = [ref[first + k].astype(F32) for k in range(-(-2 * rows // size))]
-    parts = jnp.concatenate(blocks, 0) if len(blocks) > 1 else blocks[0]
-    return parts[:rows] + parts[rows : 2 * rows]
+    blocks = [ref[first + k].astype(F32) for k in range(-(-rows // size))]
+    return (jnp.concatenate(blocks, 0) if len(blocks) > 1 else blocks[0])[:rows]
 
 
 def cut_kernel(place_ref, merged_ref, own_ref, sent_ref, onward_ref):
@@ -458,7 +458,7 @@
 
 
 def back1_kernel(
-    place_ref, even_ref, odd_ref, dresid1_ref, resid0_ref, n1g_ref, qw_any,
+    place_ref, d0_ref, d1_ref, d2_ref, d3_ref, dresid1_ref, resid0_ref, n1g_ref, qw_any,
     dresid0_ref, sums_ref, qw_ref, sems,
 ):
     rows, width = resid0_ref.shape
@@ -474,8 +474,8 @@
     d_norm1 = jnp.zeros((rows, width), F32)
     for i in range(3):
         copies[i].wait()
-        for j in range(4):
-            part = (odd_ref if j % 2 else even_ref)[j // 2, :, i * lanes : (i + 1) * lanes]
+        for j, d_ref in enumerate((d0_ref, d1_ref, d2_ref, d3_ref)):
+            part = d_ref[:, i * lanes : (i + 1) * lanes]
             at = pl.ds(pl.multiple_of((quad ^ j) * lanes, lanes), lanes)
             d_norm1 = d_norm1 + contract(part, qw_ref[i, :, at], 1, 1)
             sums_ref[2 + i : 3 + i, at] = jnp.sum(part.astype(F32), 0, keepdims=True)
@@ -625,7 +625,7 @@
 
 
 def attend_back_kernel(
-    place_ref, qkv_ref, grad_ref, probs_any, even_ref, odd_ref, table_ref, dbias_ref, probs_ref, sems,
+    place_ref, qkv_ref, grad_ref, probs_any, d0_ref, d1_ref, d2_ref, d3_ref, table_ref, dbias_ref, probs_ref, sems,
     *, windows, head_dim
 ):
     width = grad_ref.shape[1]
@@ -642,7 +642,7 @@
     def _(step):
         fetch(step).wait()
         attend_back_group(
-            place_ref[2] ^ step, step, qkv_ref, grad_ref, probs_ref, even_ref, odd_ref, dbias_ref,
+            place_ref[2] ^ step, step, qkv_ref, grad_ref, probs_ref, (d0_ref, d1_ref, d2_ref, d3_ref), dbias_ref,
             windows, head_dim, width, width // 4,
         )
 
@@ -650,7 +650,7 @@
 
 
 def attend_back_group(
-    group, step, qkv_ref, grad_ref, probs_ref, even_ref, odd_ref, dbias_ref,
+    group, step, qkv_ref, grad_ref, probs_ref, d_refs, dbias_ref,
     windows, head_dim, width, lanes,
 ):
     heads, all_heads = lanes // head_dim, width // head_dim
@@ -692,13 +692,11 @@
         [low(jnp.concatenate(parts, 0)) for parts in (all_q, all_k, all_v)], 1
     )
 
-    @pl.when(step % 2 == 0)
-    def _():
-        even_ref[step // 2] = result
-
-    @pl.when(step % 2 == 1)
-    def _():
-        odd_ref[step // 2] = result
+    for k, d_ref in enumerate(d_refs):
+
+        @pl.when(step == k)
+        def _(d_ref=d_ref):
+            d_ref[...] = result
 
 
 def spots(heads, lines, vectors):
@@ -731,15 +729,17 @@
         out_ref[pl.ds(first, own), 128:256] = block
 
 
-def deliver_kernel(place_ref, all_ref, sums_ref, rel_ref, b_ref):
-    heads = rel_ref.shape[0]
-    vectors, width = sums_ref.shape
-    lines = width // 128
-    rel_ref[...] = all_ref[:heads, :OFFSETS]
-    for k, (at, lane) in enumerate(spots(heads, lines, vectors)):
-        sums_ref[k // lines : k // lines + 1, 128 * (k % lines) : 128 * (k % lines + 1)] = all_ref[
-            at : at + 1, lane : lane + 128
-        ]
+def deliver_kernel(place_ref, all_ref, *refs, heads):
+    *vector_refs, rel_ref, b_ref = refs
+    offsets = rel_ref.shape[0]
+    rel = jnp.concatenate([all_ref[:heads, :OFFSETS], jnp.zeros((128 - heads, OFFSETS), F32)], 0)
+    rel_ref[...] = jnp.transpose(rel)[:offsets, :heads]
+    lines = [ref.shape[0] // 128 for ref in vector_refs]
+    places = iter(spots(heads, 1, sum(lines)))
+    for ref, count in zip(vector_refs, lines):
+        for k in range(count):
+            at, lane = next(places)
+            ref[128 * k : 128 * (k + 1)] = all_ref[at, lane : lane + 128]
     own = b_ref.shape[0]
     first = heads + pl.multiple_of((place_ref[0] // 2) * own, own)
     side = place_ref[0] % 2
@@ -984,9 +984,6 @@
         "fc2_join2",
     )
     fc1_come, fc2_come = swap(fc1_sent, "wide", 4), swap(fc2_sent, "wide", 2)
-    fc1_out = settle(fc1_kept + fc1_come.astype(F32))
-    fc2_out = settle(fc2_kept + fc2_come.astype(F32))
-
     second_kept, second_sent = whole(
         functools.partial(second_kernel, pad=pad, groups=groups),
         place,
@@ -995,7 +992,7 @@
         (fc2_weight, True),
         name="second",
     )
-    d_resid1, d_heads = whole(
+    d_resid1, d_heads, second_sent = whole(
         functools.partial(back2_kernel, groups=groups),
         place,
         [shape_of((tokens + 8, width), F32), shape_of((tokens, width), BF)],
@@ -1003,85 +1000,56 @@
         (resid1, True), (dy_own, True), (row(norm2_gain), True),
         (proj_weight, None), (mine, None), (theirs, None),
         scratch=[pltpu.VMEM((width, width), BF), pltpu.SemaphoreType.DMA((1 + 8 * (groups - 1),))],
-        after=(fc1_sent, fc2_sent, second_sent),
+        after=(fc1_sent, fc2_sent),
+        through=(second_sent,),
         name="back2",
     )
-    second_come = swap(tie(second_sent, d_heads), "narrow", 1)
-    d_even, d_odd, rel_part = whole(
+    second_come = swap(second_sent, "narrow", 1)
+    *d_parts, rel_part = whole(
         functools.partial(attend_back_kernel, windows=windows, head_dim=head_dim),
         place,
-        [shape_of((2, tokens, 3 * width // 4), BF)] * 2 + [shape_of((heads, OFFSETS), F32)],
+        [shape_of((tokens, 3 * width // 4), BF)] * 4 + [shape_of((heads, OFFSETS), F32)],
         (qkv, True), (d_heads, True), (probs, False),
         scratch=[
             pltpu.VMEM((QUERY_ROWS * heads, KEY_ROWS), F32),
             pltpu.VMEM((4, *probs.shape[1:]), F32),
             pltpu.SemaphoreType.DMA((4,)),
         ],
+        after=(fc1_come, fc2_come),
         name="attend_back",
     )
-    d_near = swap(d_odd, "wide", 2)
+    d_come = [swap(d_parts[j], "wide", 2 * j) for j in (1, 2, 3)]
 
     d_resid0, sums1 = whole(
         back1_kernel,
         place,
         [shape_of((tokens, width), BF), shape_of((5, width), F32)],
-        (d_even, True), (d_odd, True), (d_resid1, True), (resid0, True),
+        *((d, True) for d in d_parts), (d_resid1, True), (resid0, True),
         (row(norm1_gain), True), (qkv_weight, False),
         room=56,
         scratch=[pltpu.VMEM((3, width, width), BF), pltpu.SemaphoreType.DMA((3,))],
-        after=(fc1_come, fc2_come),
         name="back1",
     )
-    r_near = swap(d_resid0, "wide", 4)
-    proj_kept, proj_sent = grad_call(
-        place, [arrange(heads_out, "nhqc")], [d_resid1], 256, 32, "proj_grad", after=(d_resid0,)
-    )
-    proj_come = swap(proj_sent, "wide", 1)
-    d_onward = jnp.stack([d_even[1], d_near[1]])
-    d_far = swap(d_onward, "wide", 4)
-    r_both = jnp.stack([d_resid0, r_near])
-    r_far = swap(r_both, "wide", 2)
-
     d_flat, sums0 = whole(
         back0_kernel,
         place,
         [shape_of(flat.shape, BF), shape_of((2 * flat.shape[1] // width, width), F32)],
         (d_resid0, True), (flat, True), (row(merge_gain), True), (merge_weight, False),
         scratch=[pltpu.VMEM(merge_weight.shape, BF), pltpu.SemaphoreType.DMA((1,))],
-        after=(d_onward, r_both),
         name="back0",
     )
-    patches_grad = d_flat.reshape(patches.shape)
 
     second_own, second_sent = join_call(
         place, [(second_kept, second_come)],
         [(F32, [lambda p: (0, 0, 0, tokens)]), (BF, [lambda p: (0, 1, 0, tokens)])],
         "second_join",
-        after=(d_onward, r_both),
     )
     second_come = swap(second_sent, "narrow", 2)
 
-    own_sums = whole(
-        collect_kernel,
-        place,
-        [shape_of((48, 3 * width // 4), F32)],
-        (sums0, True), (sums1, True), (d_resid1, True), (rel_part, True), (fc1_b_grad, True),
-        name="collect",
-    )[0]
-    qkv_kept, qkv_sent = grad_call(
-        place,
-        [normed1_cut, (normed1_both, 1), (normed1_far, 0), (normed1_far, 1)],
-        [(d_even, 0), (d_near, 0), (d_far, 0), (d_far, 1)],
-        256, 128, "qkv_grad", sums=own_sums, after=(second_sent,),
-    )
-    qkv_come = swap(qkv_sent, "wide", 1)
-    merge_kept, merge_sent = grad_call(
-        place,
-        [merged_own, (merged_near, 0), (merged_far, 0), (merged_far, 1)],
-        [d_resid0, (r_both, 1), (r_far, 0), (r_far, 1)],
-        merged_own.shape[1], merged_own.shape[1] // 2, "merge_grad", after=(qkv_sent,),
-    )
-    merge_come = swap(merge_sent, "wide", 1)
+    proj_kept, proj_sent = grad_call(
+        place, [arrange(heads_out, "nhqc")], [d_resid1], 256, 32, "proj_grad", after=(d_resid0,)
+    )
+    proj_come = swap(proj_sent, "wide", 1)
 
     side = lambda pick_x: [
         lambda p, n=n, y=y: (0, n, (2 * y + pick_x(p[2] % 2)) * 32, 32)
@@ -1091,10 +1059,26 @@
         place, [(proj_kept, proj_come)],
         [(F32, side(lambda x: x)), (BF, side(lambda x: 1 - x))],
         "proj_join",
-        after=(qkv_sent,),
     )
     proj_come = swap(proj_sent, "wide", 2)
 
+    own_sums, d_resid0 = whole(
+        collect_kernel,
+        place,
+        [shape_of((48, 3 * width // 4), F32)],
+        (sums0, True), (sums1, True), (d_resid1, True), (rel_part, True), (fc1_b_grad, True),
+        after=(*d_come, second_sent, proj_sent),
+        through=(d_resid0,),
+        name="collect",
+    )
+    r_come = [swap(d_resid0, "wide", 2 * j) for j in (1, 2, 3)]
+    qkv_kept, qkv_sent = grad_call(
+        place,
+        [normed1_cut, (normed1_both, 1), (normed1_far, 0), (normed1_far, 1)],
+        [d_parts[0], *d_come],
+        256, 128, "qkv_grad", sums=own_sums, after=(second_sent,),
+    )
+    qkv_come = swap(qkv_sent, "wide", 1)
     rows = 128 // groups
     qkv_pieces = lambda flip: [
         lambda p, g=g, k=k: (0, g, (2 * k + (p[0] + flip) % 2) * rows, rows)
@@ -1106,18 +1090,13 @@
     )
     qkv_come = swap(qkv_sent, "narrow", 1)
 
-    merge_rows = merged_own.shape[1] // 2 // groups
-    merge_pieces = lambda flip: [
-        lambda p, k=k: (0, 0, (2 * k + (p[0] + flip) % 2) * merge_rows, merge_rows)
-        for k in range(2)
-    ]
-    merge_kept, merge_sent = join_call(
-        place, [(merge_kept, merge_come)],
-        [(F32, merge_pieces(0)), (BF, merge_pieces(1))],
-        "merge_join",
-        after=(qkv_sent,),
-    )
-    merge_come = swap(merge_sent, "narrow", 1)
+    merge_kept, merge_sent = grad_call(
+        place,
+        [merged_own, (merged_far, 0), (merged_near, 0), (merged_far, 1)],
+        [d_resid0, *r_come],
+        merged_own.shape[1], merged_own.shape[1] // 2, "merge_grad", after=(qkv_sent,),
+    )
+    merge_come = swap(merge_sent, "wide", 1)
 
     second_pieces = lambda flip: [
         lambda p, g=g: (0, ((p[0] // 2 + flip) % 2) * 4 + g, 0, rows) for g in range(4)
@@ -1127,8 +1106,24 @@
         [(F32, second_pieces(0)), (BF, second_pieces(1))],
         "qkv_join2",
         sums=(own_sums, 8),
+        after=(merge_sent,),
     )
     qkv_come = swap(qkv_sent, "narrow", 2)
+    merge_rows = merged_own.shape[1] // 2 // groups
+    merge_pieces = lambda flip: [
+        lambda p, k=k: (0, 0, (2 * k + (p[0] + flip) % 2) * merge_rows, merge_rows)
+        for k in range(2)
+    ]
+    merge_kept, merge_sent, fc1_come, fc2_come, d_flat = join_call(
+        place, [(merge_kept, merge_come)],
+        [(F32, merge_pieces(0)), (BF, merge_pieces(1))],
+        "merge_join",
+        after=(qkv_sent,),
+        through=(fc1_come, fc2_come, d_flat),
+    )
+    merge_first = merge_sent
+    merge_come = swap(merge_sent, "narrow", 1)
+
     last_pieces = lambda flip, size: [lambda p: (0, (p[0] // 2 + flip) % 2, 0, size)]
     merge_kept, merge_sent = join_call(
         place, [(merge_kept, merge_come)],
@@ -1136,6 +1131,7 @@
         "merge_join2",
         after=(qkv_sent,),
     )
+    merge_last = merge_sent
     merge_come = swap(merge_sent, "narrow", 2)
 
     proj_kept, proj_sent = join_call(
@@ -1145,7 +1141,7 @@
             (BF, [lambda p, n=n: (0, 2 * n + 1 - p[2] // 2, 0, 32) for n in range(groups)]),
         ],
         "proj_join2",
-        after=(qkv_sent,),
+        after=(merge_first,),
     )
     proj_come = swap(proj_sent, "wide", 4)
     proj_pieces = lambda flip: [
@@ -1154,6 +1150,7 @@
     proj_kept, proj_sent = join_call(
         place, [(proj_kept, proj_come)], [(F32, proj_pieces(0)), (BF, proj_pieces(1))],
         "proj_join3",
+        after=(merge_sent,),
     )
     proj_come = swap(proj_sent, "narrow", 1)
     proj_kept, proj_sent = join_call(
@@ -1168,6 +1165,7 @@
         [(BF, [lambda p, j=j: (0, p[2] ^ j, 0, rows)]) for j in range(4)],
         "qkv_join3",
         sums=(own_sums, 4),
+        after=(merge_last,),
     )
     cuts = [cuts[0]] + [swap(cuts[j], "wide", 2 * j) for j in (1, 2, 3)]
     qkv_out, all_sums = whole(
@@ -1185,20 +1183,23 @@
     merge_out = settle(merge_kept + merge_come.astype(F32))
     proj_out = settle(proj_kept + proj_come.astype(F32))
 
+    fc1_out = settle(fc1_kept + fc1_come.astype(F32))
+    fc2_out = settle(fc2_kept + fc2_come.astype(F32))
+    patches_grad = d_flat.reshape(patches.shape)
     output = low(resid1 + row(fc2_bias) + second_own[0] + second_come[0].astype(F32))
 
-    sums, rel_sum, fc1_b_mine = whole(
-        deliver_kernel,
+    deep = merged.shape[1]
+    *vectors, rel_grad, fc1_b_mine = whole(
+        functools.partial(deliver_kernel, heads=heads),
         place,
         [
-            shape_of((13, width), F32),
-            shape_of((heads, OFFSETS), F32),
-            shape_of((units // 128, 128), F32),
-        ],
+            shape_of((size,), F32)
+            for size in (deep, deep, width, width, 3 * width, width, width, width, width)
+        ]
+        + [shape_of((rel_table.shape[0], heads), F32), shape_of((units // 128, 128), F32)],
         (all_sums, True),
         name="deliver",
     )
-    rel_grad = jnp.transpose(rel_sum[:, : rel_table.shape[0]])
     fc1_b_out = lax.dynamic_index_in_dim(
         fc1_b_mine.reshape(wide, -1), wide_at, 0, keepdims=False
     )
@@ -1206,22 +1207,22 @@
     return (
         output,
         patches_grad,
-        sums[0:2].reshape(-1),
-        sums[2:4].reshape(-1),
+        vectors[0],
+        vectors[1],
         merge_out,
-        sums[4],
-        sums[5],
+        vectors[2],
+        vectors[3],
         qkv_out,
-        sums[6:9].reshape(-1),
+        vectors[4],
         rel_grad,
         proj_out,
-        sums[9],
-        sums[10],
-        sums[11],
+        vectors[5],
+        vectors[6],
+        vectors[7],
         fc1_out,
         fc1_b_out,
         fc2_out,
-        sums[12],
+        vectors[8],
     )
 
 

time: 269 us -> 249 us (0.926)
  waiting for transfers between devices: 88.1 us -> 66 us
  starting transfers between devices: 47.4 us -> 53.1 us
  other arithmetic: 10.3 us -> 7.24 us
    ppermute x34 -> x36, waiting for transfers between devices: 62.7 us -> 40.7 us  [swap(): return lax.ppermute(array, axis, [(i, i ^ mask) for i in range(size)])]
    ppermute x34 -> x36, starting transfers between devices: 33.5 us -> 39.2 us  [swap(): return lax.ppermute(array, axis, [(i, i ^ mask) for i in range(size)])]
    unnamed x165 -> x145, local copies, waits for them, and re-layouts: 17.5 us -> 20 us
  transfers between devices with their start and end apart: 43 -> 45, of which waited for: 19 -> 16; matrix products, arithmetic and copies ran while one was open for 5% -> 5% of each run, Pallas kernels for 30% -> 30%
where the time goes in v2:
time: 249 us; the launch traced here: 248 us
  Pallas kernels  95.8 us (38%)
  waiting for transfers between devices  66 us (27%)
  starting transfers between devices  53.1 us (21%)
  local copies, waits for them, and re-layouts  23.9 us (10%)
  other arithmetic  7.24 us (3%)
    pallas_call x37, Pallas kernels, whole(): pl.pallas_call(body, in_specs=[pl.BlockSpec(memory_space=pltpu.SMEM)] + [...  95.8 us
    ppermute x36, waiting for transfers between devices, swap(): return lax.ppermute(array, axis, [(i, i ^ mask) for i in range(size)])  40.7 us
    ppermute x36, starting transfers between devices, swap(): return lax.ppermute(array, axis, [(i, i ^ mask) for i in range(size)])  39.2 us
    ppermute x9, waiting for transfers between devices, turn(): lax.ppermute(array, axis, [(i, (i + step) % size) for i in range(size)])  25.3 us
    unnamed x145, local copies, waits for them, and re-layouts  20 us
    ppermute x9, starting transfers between devices, turn(): lax.ppermute(array, axis, [(i, (i + step) % size) for i in range(size)])  13.9 us
  transfers between devices with their start and end apart: 45, of which 16 were waited for; matrix products, arithmetic and copies ran while one was open for 5% of the time, Pallas kernels for 30%

profile of v2, /device:TPU:0, one launch (start us, length us, event | category | flops | bytes accessed | tf_op | source)
XLA Modules:
  0.0 247.7 jit_solution(5559205763218761004)
XLA Ops:
  4.0 5.0 %collective-permute-start.2 = (bf16[48,1024]{1,0:T(8,128)(2,1)}, bf16[48,1024]{1,0:T(8,128)(2,1)}, u32[]{:S(2)}, u32[]{:S(2)}) collective-permute-start(bf16[48,1024]{1,0:T(8,128)(2,1)} %pack.1.refs_0_), channel_id=1, source_target_pairs={{0,3},{1,0},{2,1},{3,2},{4,7},{5,4},{6,5},{7,6},{8,11},{9,8},{10,9... | collective-permute-start | bytes 294920 | tf_op jit(solution)/shard_map/ppermute | solution.py:127
  10.4 4.8 %front.1 = (bf16[200,2048]{1,0:T(8,128)(2,1)S(1)}, f32[200,1024]{1,0:T(8,128)S(1)}, bf16[200,1024]{1,0:T(8,128)(2,1)}, bf16[200,3072]{1,0:T(8,128)(2,1)S(1)}) custom-call(s32[3]{0:T(128)S(1)} %pad_add_fusion.place_ref, bf16[200,2048]{1,0:T(8,128)(2,1)S(1)} %bitcast.38, f32[1,2048]{1,0:T(1,128)S(1)} %bitcast.43, f32[1,2048]{1,0:T(1,128)S(1)} %bitcast.42, ...), custom_call_target="tpu_custom_call" | custom-call | flops 99999997952 | tf_op jit(solution)/shard_map/front/pallas_call | solution.py:88
  28.4 6.8 %attend.1 = (bf16[200,1024]{1,0:T(8,128)(2,1)S(1)}, f32[52,2,8,112,128]{4,3,2,1,0:T(8,128)}) custom-call(s32[3]{0:T(128)S(1)} %pad_add_fusion.place_ref, bf16[200,3072]{1,0:T(8,128)(2,1)S(1)} %get-tuple-element.115.refs_0_, f32[3584,128]{1,0:T(8,128)S(1)} %spread.1.refs_1_, f32[2,1,128]{2,1,0:T(1,128)S(1)} %and_select_fusion.refs_2_), custom_call_target="tpu_custom_call" | custom-call | flops 99999997952 | tf_op jit(solution)/shard_map/attend/pallas_call | solution.py:88
  42.0 4.6 %after.1 = (f32[200,1024]{1,0:T(8,128)S(1)}, bf16[200,1024]{1,0:T(8,128)(2,1)}) custom-call(s32[3]{0:T(128)S(1)} %pad_add_fusion.place_ref, bf16[200,1024]{1,0:T(8,128)(2,1)S(1)} %get-tuple-element.116.refs_4_.refs_0_, f32[200,1024]{1,0:T(8,128)S(1)} %get-tuple-element.117.refs_1_.refs_5_, f32[1,1024]{1,0:T(1,128)S(1)} %bitcast.46, f32[1,1024]{1,0:T(1,128)S(1)} %bitcast.49, ...), custom_call_target="tpu_custom_call" | custom-call | flops 99999997952 | tf_op jit(solution)/shard_map/after/pallas_call | solution.py:88
  46.6 3.1 %collective-permute-start.11 = (bf16[200,1024]{1,0:T(8,128)(2,1)}, bf16[200,1024]{1,0:T(8,128)(2,1)}, u32[]{:S(2)}, u32[]{:S(2)}) collective-permute-start(bf16[200,1024]{1,0:T(8,128)(2,1)} %get-tuple-element.122.refs_2_.refs_1_.refs_0_), channel_id=1, source_target_pairs={{0,3},{1,0},{2,1},{3,2},{4,7},{5,4},{6,5},{7,6},{8,11},{9,8},{10,9... | collective-permute-start | bytes 1228808 | tf_op jit(solution)/shard_map/ppermute | solution.py:127
  59.4 3.5 %slope.1 = (bf16[832,1024]{1,0:T(8,128)(2,1)S(1)}, bf16[200,1024]{1,0:T(8,128)(2,1)S(1)}, f32[832,1024]{1,0:T(8,128)S(1)}) custom-call(s32[3]{0:T(128)S(1)} %pad_add_fusion.place_ref, bf16[800,1024]{1,0:T(8,128)(2,1)S(1)} %copy-done.19, bf16[1024,1024]{1,0:T(8,128)(2,1)S(1)} %copy-done.17, bf16[200,1024]{1,0:T(8,128)(2,1)} %get-tuple-element.122.refs_2_.refs_1_.refs_0_), custom_call_target="tpu_custom_call" | custom-call | flops 99999997952 | tf_op jit(solution)/shard_map/slope/pallas_call | solution.py:88
  63.6 23.1 %collective-permute-done.10.refs_2_ = bf16[200,1024]{1,0:T(8,128)(2,1)} collective-permute-done((bf16[200,1024]{1,0:T(8,128)(2,1)}, bf16[200,1024]{1,0:T(8,128)(2,1)}, u32[]{:S(2)}, u32[]{:S(2)}) %collective-permute-start.10) | collective-permute-done | bytes 409632 | tf_op jit(solution)/shard_map/ppermute | solution.py:127
  86.8 9.2 %feed.1 = (bf16[832,1024]{1,0:T(8,128)(2,1)S(1)}, bf16[832,1024]{1,0:T(8,128)(2,1)S(1)}, bf16[832,1024]{1,0:T(8,128)(2,1)S(1)}, f32[1,1024]{1,0:T(1,128)S(1)}, b...) custom-call(s32[3]{0:T(128)S(1)} %pad_add_fusion.place_ref, ...), custom_call_target="tpu_custom_call" | custom-call | flops 99999997952 | tf_op jit(solution)/shard_map/feed/pallas_call | solution.py:88
  99.6 2.5 %second.1 = (bf16[2,200,1024]{2,1,0:T(8,128)(2,1)S(1)}, bf16[2,200,1024]{2,1,0:T(8,128)(2,1)S(1)}) custom-call(s32[3]{0:T(128)S(1)} %pad_add_fusion.place_ref, bf16[832,1024]{1,0:T(8,128)(2,1)S(1)} %get-tuple-element.125.refs_0_, bf16[1024,1024]{1,0:T(8,128)(2,1)S(1)} %copy-done.18), custom_call_target="tpu_custom_call" | custom-call | flops 99999997952 | tf_op jit(solution)/shard_map/second/pallas_call | solution.py:88
  103.0 4.0 %fc2_grad.1 = (f32[4,128,1024]{2,1,0:T(8,128)S(1)}, bf16[4,128,1024]{2,1,0:T(8,128)(2,1)S(1)}) custom-call(s32[3]{0:T(128)S(1)} %pad_add_fusion.place_ref, bf16[832,1024]{1,0:T(8,128)(2,1)S(1)} %get-tuple-element.125.refs_0_, bf16[832,1024]{1,0:T(8,128)(2,1)S(1)} %get-tuple-element.139.refs_1_), custom_call_target="tpu_custom_call" | custom-call | flops 99999997952 | tf_op jit(solution)/shard_map/fc2_grad/pallas_call | solution.py:88
  107.1 3.8 %fc1_grad.1 = (f32[4,128,1024]{2,1,0:T(8,128)S(1)}, bf16[4,128,1024]{2,1,0:T(8,128)(2,1)S(1)}) custom-call(s32[3]{0:T(128)S(1)} %pad_add_fusion.place_ref, bf16[832,1024]{1,0:T(8,128)(2,1)S(1)} %get-tuple-element.132.refs_0_, bf16[832,1024]{1,0:T(8,128)(2,1)S(1)} %get-tuple-element.133.refs_1_), custom_call_target="tpu_custom_call" | custom-call | flops 99999997952 | tf_op jit(solution)/shard_map/fc1_grad/pallas_call | solution.py:88
  116.1 10.1 %collective-permute-done.20.refs_1_ = bf16[2,128,1024]{2,1,0:T(8,128)(2,1)S(1)} collective-permute-done((bf16[2,128,1024]{2,1,0:T(8,128)(2,1)S(1)}, bf16[2,128,1024]{2,1,0:T(8,128)(2,1)S(1)}, u32[]{:S(2)}, u32[]{:S(2)}) %collective-permute-start.20) | collective-permute-done | bytes 524320 | tf_op jit(solution)/shard_map/ppermute | solution.py:122
  133.3 5.4 %back2.1 = (f32[208,1024]{1,0:T(8,128)S(1)}, bf16[200,1024]{1,0:T(8,128)(2,1)S(1)}, bf16[2,200,1024]{2,1,0:T(8,128)(2,1)S(1)}) custom-call(s32[3]{0:T(128)S(1)} %pad_add_fusion.place_ref, bf16[200,1024]{1,0:T(8,128)(2,1)S(1)} %get-tuple-element.127.refs_0_, bf16[200,1024]{1,0:T(8,128)(2,1)} %collective-permute-done.14.refs_1_, ...), custom_call_target="tpu_custom_call", output_to_operand_aliasing={{2}: (13, {})} | custom-call | flops 5000000000 | tf_op jit(solution)/shard_map/back2/pallas_call | solution.py:88
  138.8 9.4 %attend_back.1 = (bf16[200,768]{1,0:T(8,128)(2,1)S(1)}, bf16[200,768]{1,0:T(8,128)(2,1)S(1)}, bf16[200,768]{1,0:T(8,128)(2,1)S(1)}, bf16[200,768]{1,0:T(8,128)(2,1)S(1)}, f32[32,384]{1,0:T(8,128)S(1)}) custom-call(s32[3]{0:T(128)S(1)} %pad_add_fusion.place_ref, bf16[200,3072]{1,0:T(8,128)(2,1)S(1)} %get-tuple-element.115.refs_0_, ...), custom_call_target="tpu_custom_call" | custom-call | flops 5000000000 | tf_op jit(solution)/shard_map/attend_back/pallas_call | solution.py:88
  152.4 6.7 %back1.1 = (bf16[200,1024]{1,0:T(8,128)(2,1)}, f32[5,1024]{1,0:T(8,128)}) custom-call(s32[3]{0:T(128)} %copy-done.11, bf16[200,768]{1,0:T(8,128)(2,1)} %copy-done.33, bf16[200,768]{1,0:T(8,128)(2,1)} %copy-done.37, bf16[200,768]{1,0:T(8,128)(2,1)} %copy-done.36, bf16[200,768]{1,0:T(8,128)(2,1)} %copy-done.35, f32[208,1024]{1,0:T(8,128)} %copy-done.51, ...), custom_call_target="tpu_custom_call" | custom-call | flops 20000000000 | tf_op jit(solution)/shard_map/back1/pallas_call | solution.py:88
  161.4 3.9 %back0.1 = (bf16[200,2048]{1,0:T(8,128)(2,1)S(1)}, f32[4,1024]{1,0:T(4,128)S(1)}) custom-call(s32[3]{0:T(128)S(1)} %copy-done.12, bf16[200,1024]{1,0:T(8,128)(2,1)} %get-tuple-element.157.refs_0_.refs_2_.refs_10_, bf16[200,2048]{1,0:T(8,128)(2,1)S(1)} %bitcast.39, f32[1,2048]{1,0:T(1,128)S(1)} %bitcast.44, bf16[2048,1024]{1,0:T(8,128)(2,1)S(1)} %copy-done.15), custom_call_target="tpu_custom_call" | custom-call | flops 20000000000 | tf_op jit(solution)/shard_map/back0/pallas_call | solution.py:88
  173.0 4.9 %qkv_grad.1 = (f32[4,128,768]{2,1,0:T(8,128)S(1)}, bf16[5,128,768]{2,1,0:T(8,128)(2,1)}) custom-call(s32[3]{0:T(128)S(1)} %copy-done.12, bf16[200,1024]{1,0:T(8,128)(2,1)} %get-tuple-element.120.refs_0_, bf16[2,200,1024]{2,1,0:T(8,128)(2,1)S(1)} %copy-done.5, bf16[2,200,1024]{2,1,0:T(8,128)(2,1)S(1)} %copy-done.21, bf16[2,200,1024]{2,1,0:T(8,128)(2,1)S(1)} %copy-done.21, ...), custom_call_target="tpu_custom_call" | custom-call | flops 5000000000 | tf_op jit(solution)/shard_map/qkv_grad/pallas_call | solution.py:88
  189.0 5.0 %collective-permute-done.31.refs_7_ = bf16[200,1024]{1,0:T(8,128)(2,1)S(1)} collective-permute-done((bf16[200,1024]{1,0:T(8,128)(2,1)}, bf16[200,1024]{1,0:T(8,128)(2,1)S(1)}, u32[]{:S(2)}, u32[]{:S(2)}) %collective-permute-start.31) | collective-permute-done | bytes 409632 | tf_op jit(solution)/shard_map/ppermute | solution.py:122
  194.0 7.9 %collective-permute-done.30.refs_6_ = bf16[200,1024]{1,0:T(8,128)(2,1)S(1)} collective-permute-done((bf16[200,1024]{1,0:T(8,128)(2,1)}, bf16[200,1024]{1,0:T(8,128)(2,1)S(1)}, u32[]{:S(2)}, u32[]{:S(2)}) %collective-permute-start.30) | collective-permute-done | bytes 409632 | tf_op jit(solution)/shard_map/ppermute | solution.py:122
  201.9 2.5 %merge_grad.1 = (f32[1,256,1024]{2,1,0:T(8,128)S(1)}, bf16[1,256,1024]{2,1,0:T(8,128)(2,1)S(1)}) custom-call(s32[3]{0:T(128)S(1)} %copy-done.12, bf16[200,512]{1,0:T(8,128)(2,1)S(1)} %copy-done.62, bf16[2,200,512]{2,1,0:T(8,128)(2,1)S(1)} %copy-done.32, bf16[2,200,512]{2,1,0:T(8,128)(2,1)} %collective-permute-done.6.refs_5_.refs_2_, ...), custom_call_target="tpu_custom_call" | custom-call | flops 5000000000 | tf_op jit(solution)/shard_map/merge_grad/pallas_call | solution.py:88
  208.2 2.3 collective-permute-start.35
  211.9 2.5 %collective-permute-start.36 = (bf16[2,64,1024]{2,1,0:T(8,128)(2,1)S(1)}, bf16[2,64,1024]{2,1,0:T(8,128)(2,1)S(1)}, u32[]{:S(2)}, u32[]{:S(2)}) collective-permute-start(bf16[2,64,1024]{2,1,0:T(8,128)(2,1)S(1)} %get-tuple-element.180.refs_2_), channel_id=1, source_target_pairs={{0,1},{1,0},{2,3},{3,2},{4,5},{5,4},{6,7},{7,6},{8,9},{9,8},{10,11... | collective-permute-start | bytes 786440 | tf_op jit(solution)/shard_map/ppermute | solution.py:122
  214.4 5.4 %collective-permute-done.41.refs_1_ = bf16[8,32,1024]{2,1,0:T(8,128)(2,1)S(1)} collective-permute-done((bf16[8,32,1024]{2,1,0:T(8,128)(2,1)S(1)}, bf16[8,32,1024]{2,1,0:T(8,128)(2,1)S(1)}, u32[]{:S(2)}, u32[]{:S(2)}) %collective-permute-start.41) | collective-permute-done | bytes 524320 | tf_op jit(solution)/shard_map/ppermute | solution.py:122
  228.0 3.2 %collective-permute-done.42.refs_1_ = bf16[4,32,1024]{2,1,0:T(8,128)(2,1)S(1)} collective-permute-done((bf16[4,32,1024]{2,1,0:T(8,128)(2,1)S(1)}, bf16[4,32,1024]{2,1,0:T(8,128)(2,1)S(1)}, u32[]{:S(2)}, u32[]{:S(2)}) %collective-permute-start.42) | collective-permute-done | bytes 262176 | tf_op jit(solution)/shard_map/ppermute | solution.py:122
  (266 shorter events, 106.3 us)
Async XLA Ops:
  4.0 17.0 %collective-permute-start.2 = (bf16[48,1024]{1,0:T(8,128)(2,1)}, bf16[48,1024]{1,0:T(8,128)(2,1)}, u32[]{:S(2)}, u32[]{:S(2)}) collective-permute-start(bf16[48,1024]{1,0:T(8,128)(2,1)} %pack.1.refs_0_), channel_id=1, source_target_pairs={{0,3},{1,0},{2,1},{3,2},{4,7},{5,4},{6,5},{7,6},{8,11},{9,8},{10,9... | collective-permute-start | bytes 294920 | tf_op jit(solution)/shard_map/ppermute | solution.py:127
  17.9 20.4 %collective-permute-start.6 = (bf16[2,200,512]{2,1,0:T(8,128)(2,1)}, bf16[2,200,512]{2,1,0:T(8,128)(2,1)}, u32[]{:S(2)}, u32[]{:S(2)}) collective-permute-start(bf16[2,200,512]{2,1,0:T(8,128)(2,1)} %get-tuple-element.119), channel_id=1, source_target_pairs={{0,16},{4,20},{8,24},{12,28},{16,0},{20,4},{24,8},{28,12},{1,17},{... | collective-permute-start | bytes 1228808 | tf_op jit(solution)/shard_map/ppermute | solution.py:122
  19.4 18.8 %collective-permute-start.7 = (bf16[200,1024]{1,0:T(8,128)(2,1)}, bf16[200,1024]{1,0:T(8,128)(2,1)}, u32[]{:S(2)}, u32[]{:S(2)}) collective-permute-start(bf16[200,1024]{1,0:T(8,128)(2,1)} %get-tuple-element.120.refs_0_), channel_id=1, source_target_pairs={{0,8},{4,12},{8,0},{12,4},{16,24},{20,28},{24,16},{28,20},{1,9},{5... | collective-permute-start | bytes 1228808 | tf_op jit(solution)/shard_map/ppermute | solution.py:122
  23.3 13.7 %collective-permute-start.4 = (bf16[96,1024]{1,0:T(8,128)(2,1)}, bf16[96,1024]{1,0:T(8,128)(2,1)}, u32[]{:S(2)}, u32[]{:S(2)}) collective-permute-start(bf16[96,1024]{1,0:T(8,128)(2,1)} %pieces.1.refs_0_), channel_id=1, source_target_pairs={{0,16},{4,20},{8,24},{12,28},{16,0},{20,4},{24,8},{28,12},{1,17},{... | collective-permute-start | bytes 589832 | tf_op jit(solution)/shard_map/ppermute | solution.py:122
  46.6 17.0 %collective-permute-start.11 = (bf16[200,1024]{1,0:T(8,128)(2,1)}, bf16[200,1024]{1,0:T(8,128)(2,1)}, u32[]{:S(2)}, u32[]{:S(2)}) collective-permute-start(bf16[200,1024]{1,0:T(8,128)(2,1)} %get-tuple-element.122.refs_2_.refs_1_.refs_0_), channel_id=1, source_target_pairs={{0,3},{1,0},{2,1},{3,2},{4,7},{5,4},{6,5},{7,6},{8,11},{9,8},{10,9... | collective-permute-start | bytes 1228808 | tf_op jit(solution)/shard_map/ppermute | solution.py:127
  49.7 37.0 %collective-permute-start.10 = (bf16[200,1024]{1,0:T(8,128)(2,1)}, bf16[200,1024]{1,0:T(8,128)(2,1)}, u32[]{:S(2)}, u32[]{:S(2)}) collective-permute-start(bf16[200,1024]{1,0:T(8,128)(2,1)} %get-tuple-element.122.refs_2_.refs_1_.refs_0_), channel_id=1, source_target_pairs={{0,2},{1,3},{2,0},{3,1},{4,6},{5,7},{6,4},{7,5},{8,10},{9,11},{10,... | collective-permute-start | bytes 1228808 | tf_op jit(solution)/shard_map/ppermute | solution.py:127
  50.6 36.1 %collective-permute-start.9 = (bf16[200,1024]{1,0:T(8,128)(2,1)}, bf16[200,1024]{1,0:T(8,128)(2,1)}, u32[]{:S(2)}, u32[]{:S(2)}) collective-permute-start(bf16[200,1024]{1,0:T(8,128)(2,1)} %get-tuple-element.122.refs_2_.refs_1_.refs_0_), channel_id=1, source_target_pairs={{0,1},{1,2},{2,3},{3,0},{4,5},{5,6},{6,7},{7,4},{8,9},{9,10},{10,1... | collective-permute-start | bytes 1228808 | tf_op jit(solution)/shard_map/ppermute | solution.py:127
  55.4 31.3 %collective-permute-start.12 = (bf16[2,200,1024]{2,1,0:T(8,128)(2,1)S(1)}, bf16[2,200,1024]{2,1,0:T(8,128)(2,1)S(1)}, u32[]{:S(2)}, u32[]{:S(2)}) collective-permute-start(bf16[2,200,1024]{2,1,0:T(8,128)(2,1)S(1)} %pad_maximum_fusion.refs_1_), channel_id=1, source_target_pairs={{0,16},{4,20},{8,24},{12,28},{16,0},{20,4},{24,8},{28,12},{1,17},{... | collective-permute-start | bytes 2457608 | tf_op jit(solution)/shard_map/ppermute | solution.py:122
  96.0 35.1 %collective-permute-start.14 = (bf16[200,1024]{1,0:T(8,128)(2,1)}, bf16[200,1024]{1,0:T(8,128)(2,1)}, u32[]{:S(2)}, u32[]{:S(2)}) collective-permute-start(bf16[200,1024]{1,0:T(8,128)(2,1)} %get-tuple-element.128), channel_id=1, source_target_pairs={{0,3},{1,0},{2,1},{3,2},{4,7},{5,4},{6,5},{7,6},{8,11},{9,8},{10,9... | collective-permute-start | bytes 1228808 | tf_op jit(solution)/shard_map/ppermute | solution.py:127
  96.1 37.2 %collective-permute-start.15 = (bf16[200,1024]{1,0:T(8,128)(2,1)}, bf16[200,1024]{1,0:T(8,128)(2,1)}, u32[]{:S(2)}, u32[]{:S(2)}) collective-permute-start(bf16[200,1024]{1,0:T(8,128)(2,1)} %get-tuple-element.129), channel_id=1, source_target_pairs={{0,2},{1,3},{2,0},{3,1},{4,6},{5,7},{6,4},{7,5},{8,10},{9,11},{10,... | collective-permute-start | bytes 1228808 | tf_op jit(solution)/shard_map/ppermute | solution.py:127
  97.6 35.6 %collective-permute-start.16 = (bf16[200,1024]{1,0:T(8,128)(2,1)}, bf16[200,1024]{1,0:T(8,128)(2,1)}, u32[]{:S(2)}, u32[]{:S(2)}) collective-permute-start(bf16[200,1024]{1,0:T(8,128)(2,1)} %get-tuple-element.130), channel_id=1, source_target_pairs={{0,1},{1,2},{2,3},{3,0},{4,5},{5,6},{6,7},{7,4},{8,9},{9,10},{10,1... | collective-permute-start | bytes 1228808 | tf_op jit(solution)/shard_map/ppermute | solution.py:127
  112.3 13.9 %collective-permute-start.20 = (bf16[2,128,1024]{2,1,0:T(8,128)(2,1)S(1)}, bf16[2,128,1024]{2,1,0:T(8,128)(2,1)S(1)}, u32[]{:S(2)}, u32[]{:S(2)}) collective-permute-start(bf16[2,128,1024]{2,1,0:T(8,128)(2,1)S(1)} %get-tuple-element.143), channel_id=1, source_target_pairs={{0,16},{4,20},{8,24},{12,28},{16,0},{20,4},{24,8},{28,12},{1,17},{... | collective-permute-start | bytes 1572872 | tf_op jit(solution)/shard_map/ppermute | solution.py:122
  114.6 14.6 %collective-permute-start.18 = (bf16[2,128,1024]{2,1,0:T(8,128)(2,1)S(1)}, bf16[2,128,1024]{2,1,0:T(8,128)(2,1)S(1)}, u32[]{:S(2)}, u32[]{:S(2)}) collective-permute-start(bf16[2,128,1024]{2,1,0:T(8,128)(2,1)S(1)} %get-tuple-element.137), channel_id=1, source_target_pairs={{0,8},{4,12},{8,0},{12,4},{16,24},{20,28},{24,16},{28,20},{1,9},{5... | collective-permute-start | bytes 1572872 | tf_op jit(solution)/shard_map/ppermute | solution.py:122
  138.7 28.9 %collective-permute-start.21 = (bf16[2,200,1024]{2,1,0:T(8,128)(2,1)S(1)}, bf16[2,200,1024]{2,1,0:T(8,128)(2,1)S(1)}, u32[]{:S(2)}, u32[]{:S(2)}) collective-permute-start(bf16[2,200,1024]{2,1,0:T(8,128)(2,1)S(1)} %get-tuple-element.146), channel_id=1, source_target_pairs={{0,1},{1,0},{2,3},{3,2},{4,5},{5,4},{6,7},{7,6},{8,9},{9,8},{10,11... | collective-permute-start | bytes 2457608 | tf_op jit(solution)/shard_map/ppermute | solution.py:122
  148.9 22.0 %collective-permute-start.25 = (bf16[200,768]{1,0:T(8,128)(2,1)S(1)}, bf16[200,768]{1,0:T(8,128)(2,1)S(1)}, u32[]{:S(2)}, u32[]{:S(2)}) collective-permute-start(bf16[200,768]{1,0:T(8,128)(2,1)S(1)} %get-tuple-element.153.refs_1_), channel_id=1, source_target_pairs={{0,8},{4,12},{8,0},{12,4},{16,24},{20,28},{24,16},{28,20},{1,9},{5... | collective-permute-start | bytes 921608 | tf_op jit(solution)/shard_map/ppermute | solution.py:122
  150.4 20.6 %collective-permute-start.26 = (bf16[200,768]{1,0:T(8,128)(2,1)S(1)}, bf16[200,768]{1,0:T(8,128)(2,1)S(1)}, u32[]{:S(2)}, u32[]{:S(2)}) collective-permute-start(bf16[200,768]{1,0:T(8,128)(2,1)S(1)} %get-tuple-element.154.refs_2_), channel_id=1, source_target_pairs={{0,16},{4,20},{8,24},{12,28},{16,0},{20,4},{24,8},{28,12},{1,17},{... | collective-permute-start | bytes 921608 | tf_op jit(solution)/shard_map/ppermute | solution.py:122
  150.9 20.1 %collective-permute-start.27 = (bf16[200,768]{1,0:T(8,128)(2,1)S(1)}, bf16[200,768]{1,0:T(8,128)(2,1)S(1)}, u32[]{:S(2)}, u32[]{:S(2)}) collective-permute-start(bf16[200,768]{1,0:T(8,128)(2,1)S(1)} %get-tuple-element.155.refs_3_), channel_id=1, source_target_pairs={{0,24},{4,28},{8,16},{12,20},{16,8},{20,12},{24,0},{28,4},{1,25},{... | collective-permute-start | bytes 921608 | tf_op jit(solution)/shard_map/ppermute | solution.py:122
  179.2 25.4 %collective-permute-start.22 = (bf16[1,200,1024]{2,1,0:T(8,128)(2,1)}, bf16[1,200,1024]{2,1,0:T(8,128)(2,1)S(1)}, u32[]{:S(2)}, u32[]{:S(2)}) collective-permute-start(bf16[1,200,1024]{2,1,0:T(8,128)(2,1)} %get-tuple-element.148.refs_8_.refs_9_), channel_id=1, source_target_pairs={{0,2},{1,3},{2,0},{3,1},{4,6},{5,7},{6,4},{7,5},{8,10},{9,11},{10,... | collective-permute-start | bytes 1228808 | tf_op jit(solution)/shard_map/ppermute | solution.py:122
  182.0 19.9 %collective-permute-start.30 = (bf16[200,1024]{1,0:T(8,128)(2,1)}, bf16[200,1024]{1,0:T(8,128)(2,1)S(1)}, u32[]{:S(2)}, u32[]{:S(2)}) collective-permute-start(bf16[200,1024]{1,0:T(8,128)(2,1)} %get-tuple-element.165.refs_4_), channel_id=1, source_target_pairs={{0,16},{4,20},{8,24},{12,28},{16,0},{20,4},{24,8},{28,12},{1,17},{... | collective-permute-start | bytes 1228808 | tf_op jit(solution)/shard_map/ppermute | solution.py:122
  183.5 18.4 %collective-permute-start.29 = (bf16[200,1024]{1,0:T(8,128)(2,1)}, bf16[200,1024]{1,0:T(8,128)(2,1)S(1)}, u32[]{:S(2)}, u32[]{:S(2)}) collective-permute-start(bf16[200,1024]{1,0:T(8,128)(2,1)} %get-tuple-element.165.refs_4_), channel_id=1, source_target_pairs={{0,8},{4,12},{8,0},{12,4},{16,24},{20,28},{24,16},{28,20},{1,9},{5... | collective-permute-start | bytes 1228808 | tf_op jit(solution)/shard_map/ppermute | solution.py:122
  186.9 19.9 %collective-permute-start.34 = (bf16[10,32,768]{2,1,0:T(8,128)(2,1)S(1)}, bf16[10,32,768]{2,1,0:T(8,128)(2,1)S(1)}, u32[]{:S(2)}, u32[]{:S(2)}) collective-permute-start(bf16[10,32,768]{2,1,0:T(8,128)(2,1)S(1)} %get-tuple-element.169.refs_8_), channel_id=1, source_target_pairs={{0,1},{1,0},{2,3},{3,2},{4,5},{5,4},{6,7},{7,6},{8,9},{9,8},{10,11... | collective-permute-start | bytes 1474568 | tf_op jit(solution)/shard_map/ppermute | solution.py:122
  205.5 14.3 %collective-permute-start.41 = (bf16[8,32,1024]{2,1,0:T(8,128)(2,1)S(1)}, bf16[8,32,1024]{2,1,0:T(8,128)(2,1)S(1)}, u32[]{:S(2)}, u32[]{:S(2)}) collective-permute-start(bf16[8,32,1024]{2,1,0:T(8,128)(2,1)S(1)} %copy-done.30), channel_id=1, source_target_pairs={{0,8},{4,12},{8,0},{12,4},{16,24},{20,28},{24,16},{28,20},{1,9},{5... | collective-permute-start | bytes 1572872 | tf_op jit(solution)/shard_map/ppermute | solution.py:122
  208.2 25.6 %collective-permute-start.35 = (bf16[6,32,768]{2,1,0:T(8,128)(2,1)S(1)}, bf16[6,32,768]{2,1,0:T(8,128)(2,1)S(1)}, u32[]{:S(2)}, u32[]{:S(2)}) collective-permute-start(bf16[6,32,768]{2,1,0:T(8,128)(2,1)S(1)} %get-tuple-element.174.refs_2_), channel_id=1, source_target_pairs={{0,2},{1,3},{2,0},{3,1},{4,6},{5,7},{6,4},{7,5},{8,10},{9,11},{10,... | collective-permute-start | bytes 884744 | tf_op jit(solution)/shard_map/ppermute | solution.py:122
  226.3 13.8 %collective-permute-start.40 = (bf16[1,64,1024]{2,1,0:T(8,128)(2,1)S(1)}, bf16[1,64,1024]{2,1,0:T(8,128)(2,1)S(1)}, u32[]{:S(2)}, u32[]{:S(2)}) collective-permute-start(bf16[1,64,1024]{2,1,0:T(8,128)(2,1)S(1)} %get-tuple-element.181.refs_3_.refs_2_), channel_id=1, source_target_pairs={{0,2},{1,3},{2,0},{3,1},{4,6},{5,7},{6,4},{7,5},{8,10},{9,11},{10,... | collective-permute-start | bytes 393224 | tf_op jit(solution)/shard_map/ppermute | solution.py:122
  (92 other events, 731.4 us)

commit v3 on v2

--- a/solution.py
+++ b/solution.py
@@ -339,33 +339,24 @@
         refs[-1][q * rows : (q + 1) * rows] = ref[...]
 
 
-def bring_proj(place_ref, own_any, mine_any, theirs_any, proj_ref, sems, groups):
+def whole_proj(place_ref, own_ref, mine_ref, theirs_ref, proj_ref, groups):
     rank, core, quad = place_ref[0], place_ref[1], place_ref[2]
-    shard = own_any.shape[0]
+    shard = own_ref.shape[0]
     part = shard // 8
-
-    def bring(source, start, rows, sem):
-        at = pl.ds(pl.multiple_of(start, rows), rows)
-        copy = pltpu.make_async_copy(source, proj_ref.at[at], sems.at[sem])
-        copy.start()
-        return copy
-
-    copies = [bring(own_any, rank * shard, shard, 0)]
+    proj_ref[pl.ds(pl.multiple_of(rank * shard, shard), shard), :] = own_ref[...]
     for k in range(4 * (groups - 1)):
         q, j = k // (groups - 1), k % (groups - 1)
         base = lax.rem(rank + groups - 1 - j, groups) * shard + (quad ^ q) * 2 * part
-        rows = pl.ds(k * part, part)
-        copies.append(bring(mine_any.at[rows], base + core * part, part, 1 + 2 * k))
-        copies.append(bring(theirs_any.at[rows], base + (1 - core) * part, part, 2 + 2 * k))
-    return copies
+        rows = slice(k * part, (k + 1) * part)
+        proj_ref[pl.ds(pl.multiple_of(base + core * part, part), part), :] = mine_ref[rows]
+        proj_ref[pl.ds(pl.multiple_of(base + (1 - core) * part, part), part), :] = theirs_ref[rows]
 
 
 def after_kernel(
-    place_ref, heads_ref, resid0_ref, pb_ref, n2g_ref, n2s_ref, own_any, mine_any, theirs_any,
-    resid1_ref, normed2_ref, proj_ref, sems, *, groups,
-):
-    for copy in bring_proj(place_ref, own_any, mine_any, theirs_any, proj_ref, sems, groups):
-        copy.wait()
+    place_ref, heads_ref, resid0_ref, pb_ref, n2g_ref, n2s_ref, own_ref, mine_ref, theirs_ref,
+    resid1_ref, normed2_ref, proj_ref, *, groups,
+):
+    whole_proj(place_ref, own_ref, mine_ref, theirs_ref, proj_ref, groups)
     resid1 = resid0_ref[...] + matmul(heads_ref[...], proj_ref[...]) + pb_ref[...]
     resid1_ref[...] = resid1
     hat2, _ = normalise(resid1)
@@ -436,10 +427,10 @@
 
 
 def back2_kernel(
-    place_ref, c0_ref, c1_ref, c2_ref, c3_ref, resid1_ref, dy_ref, n2g_ref, own_any, mine_any, theirs_any,
-    dresid1_ref, dheads_ref, proj_ref, sems, *, groups,
-):
-    copies = bring_proj(place_ref, own_any, mine_any, theirs_any, proj_ref, sems, groups)
+    place_ref, c0_ref, c1_ref, c2_ref, c3_ref, resid1_ref, dy_ref, n2g_ref, own_ref, mine_ref, theirs_ref,
+    dresid1_ref, dheads_ref, proj_ref, *, groups,
+):
+    whole_proj(place_ref, own_ref, mine_ref, theirs_ref, proj_ref, groups)
     rows = dheads_ref.shape[0]
     d_norm2 = (
         c0_ref[...].astype(F32) + c1_ref[...].astype(F32)
@@ -452,8 +443,6 @@
     sums = (d_resid1, d_norm2 * hat2, d_norm2, dy)
     for k, part in enumerate(sums):
         dresid1_ref[rows + k : rows + k + 1] = jnp.sum(part, 0, keepdims=True)
-    for copy in copies:
-        copy.wait()
     dheads_ref[...] = low(contract(low(d_resid1), proj_ref[...], 1, 1))
 
 
@@ -731,9 +720,7 @@
 
 def deliver_kernel(place_ref, all_ref, *refs, heads):
     *vector_refs, rel_ref, b_ref = refs
-    offsets = rel_ref.shape[0]
-    rel = jnp.concatenate([all_ref[:heads, :OFFSETS], jnp.zeros((128 - heads, OFFSETS), F32)], 0)
-    rel_ref[...] = jnp.transpose(rel)[:offsets, :heads]
+    rel_ref[...] = all_ref[:heads, : rel_ref.shape[1]]
     lines = [ref.shape[0] // 128 for ref in vector_refs]
     places = iter(spots(heads, 1, sum(lines)))
     for ref, count in zip(vector_refs, lines):
@@ -906,8 +893,8 @@
         [shape_of((tokens, width), F32), shape_of((tokens, width), BF)],
         (heads_out, True), (resid0, True),
         (row(proj_bias), True), (row(norm2_gain), True), (row(norm2_shift), True),
-        (proj_weight, None), (mine, None), (theirs, None),
-        scratch=[pltpu.VMEM((width, width), BF), pltpu.SemaphoreType.DMA((1 + 8 * (groups - 1),))],
+        (proj_weight, True), (mine, True), (theirs, True),
+        scratch=[pltpu.VMEM((width, width), BF)],
         name="after",
     )
     blocks = [normed2] + [turn(normed2, "narrow", step) for step in range(1, groups)]
@@ -998,8 +985,8 @@
         [shape_of((tokens + 8, width), F32), shape_of((tokens, width), BF)],
         *((a, True) for a in arrived),
         (resid1, True), (dy_own, True), (row(norm2_gain), True),
-        (proj_weight, None), (mine, None), (theirs, None),
-        scratch=[pltpu.VMEM((width, width), BF), pltpu.SemaphoreType.DMA((1 + 8 * (groups - 1),))],
+        (proj_weight, True), (mine, True), (theirs, True),
+        scratch=[pltpu.VMEM((width, width), BF)],
         after=(fc1_sent, fc2_sent),
         through=(second_sent,),
         name="back2",
@@ -1026,8 +1013,10 @@
         [shape_of((tokens, width), BF), shape_of((5, width), F32)],
         *((d, True) for d in d_parts), (d_resid1, True), (resid0, True),
         (row(norm1_gain), True), (qkv_weight, False),
-        room=56,
-        scratch=[pltpu.VMEM((3, width, width), BF), pltpu.SemaphoreType.DMA((3,))],
+        scratch=[
+            pltpu.VMEM((3, width, width), BF),
+            pltpu.SemaphoreType.DMA((3,)),
+        ],
         name="back1",
     )
     d_flat, sums0 = whole(
@@ -1196,7 +1185,7 @@
             shape_of((size,), F32)
             for size in (deep, deep, width, width, 3 * width, width, width, width, width)
         ]
-        + [shape_of((rel_table.shape[0], heads), F32), shape_of((units // 128, 128), F32)],
+        + [shape_of((heads, rel_table.shape[0]), F32), shape_of((units // 128, 128), F32)],
         (all_sums, True),
         name="deliver",
     )
@@ -1214,7 +1203,7 @@
         vectors[3],
         qkv_out,
         vectors[4],
-        rel_grad,
+        jnp.transpose(rel_grad),
         proj_out,
         vectors[5],
         vectors[6],

time: 249 us -> 239 us (0.960)
  Pallas kernels: 95.8 us -> 89.8 us
  waiting for transfers between devices: 66 us -> 71.1 us
  local copies, waits for them, and re-layouts: 23.9 us -> 19.3 us
  starting transfers between devices: 53.1 us -> 48.9 us
    pallas_call x37, Pallas kernels: 95.8 us -> 89.8 us  [whole(): pl.pallas_call(body, in_specs=[pl.BlockSpec(memory_space=pltpu.SMEM)] + [...]
    unnamed x145 -> x128, local copies, waits for them, and re-layouts: 20 us -> 15.4 us
    ppermute x36, waiting for transfers between devices: 40.7 us -> 44.9 us  [swap(): return lax.ppermute(array, axis, [(i, i ^ mask) for i in range(size)])]
    ppermute x36, starting transfers between devices: 39.2 us -> 35 us  [swap(): return lax.ppermute(array, axis, [(i, i ^ mask) for i in range(size)])]
  transfers between devices with their start and end apart: 45 -> 45, of which waited for: 16 -> 18; matrix products, arithmetic and copies ran while one was open for 5% -> 4% of each run, Pallas kernels for 30% -> 29%
where the time goes in v3:
time: 239 us; the launch traced here: 238 us
  Pallas kernels  89.8 us (38%)
  waiting for transfers between devices  71.1 us (30%)
  starting transfers between devices  48.9 us (20%)
  local copies, waits for them, and re-layouts  19.3 us (8%)
  other arithmetic  7.24 us (3%)
    pallas_call x37, Pallas kernels, whole(): pl.pallas_call(body, in_specs=[pl.BlockSpec(memory_space=pltpu.SMEM)] + [...  89.8 us
    ppermute x36, waiting for transfers between devices, swap(): return lax.ppermute(array, axis, [(i, i ^ mask) for i in range(size)])  44.9 us
    ppermute x36, starting transfers between devices, swap(): return lax.ppermute(array, axis, [(i, i ^ mask) for i in range(size)])  35 us
    ppermute x9, waiting for transfers between devices, turn(): lax.ppermute(array, axis, [(i, (i + step) % size) for i in range(size)])  26.2 us
    unnamed x128, local copies, waits for them, and re-layouts  15.4 us
    ppermute x9, starting transfers between devices, turn(): lax.ppermute(array, axis, [(i, (i + step) % size) for i in range(size)])  13.9 us
  transfers between devices with their start and end apart: 45, of which 18 were waited for; matrix products, arithmetic and copies ran while one was open for 4% of the time, Pallas kernels for 29%

profile of v3, /device:TPU:0, one launch (start us, length us, event | category | flops | bytes accessed | tf_op | source)
XLA Modules:
  0.0 237.9 jit_solution(7177986620058223450)
XLA Ops:
  4.0 5.0 %collective-permute-start.2 = (bf16[48,1024]{1,0:T(8,128)(2,1)}, bf16[48,1024]{1,0:T(8,128)(2,1)}, u32[]{:S(2)}, u32[]{:S(2)}) collective-permute-start(bf16[48,1024]{1,0:T(8,128)(2,1)} %pack.1.refs_0_), channel_id=1, source_target_pairs={{0,3},{1,0},{2,1},{3,2},{4,7},{5,4},{6,5},{7,6},{8,11},{9,8},{10,9... | collective-permute-start | bytes 294920 | tf_op jit(solution)/shard_map/ppermute | solution.py:127
  10.4 4.8 %front.1 = (bf16[200,2048]{1,0:T(8,128)(2,1)S(1)}, f32[200,1024]{1,0:T(8,128)S(1)}, bf16[200,1024]{1,0:T(8,128)(2,1)}, bf16[200,3072]{1,0:T(8,128)(2,1)S(1)}) custom-call(s32[3]{0:T(128)S(1)} %pad_add_fusion.place_ref, bf16[200,2048]{1,0:T(8,128)(2,1)S(1)} %bitcast.39, f32[1,2048]{1,0:T(1,128)S(1)} %bitcast.46, f32[1,2048]{1,0:T(1,128)S(1)} %bitcast.45, ...), custom_call_target="tpu_custom_call" | custom-call | flops 99999997952 | tf_op jit(solution)/shard_map/front/pallas_call | solution.py:88
  28.4 6.7 %attend.1 = (bf16[200,1024]{1,0:T(8,128)(2,1)S(1)}, f32[52,2,8,112,128]{4,3,2,1,0:T(8,128)}) custom-call(s32[3]{0:T(128)S(1)} %pad_add_fusion.place_ref, bf16[200,3072]{1,0:T(8,128)(2,1)S(1)} %get-tuple-element.115.refs_0_, f32[3584,128]{1,0:T(8,128)S(1)} %spread.1.refs_1_, f32[2,1,128]{2,1,0:T(1,128)S(1)} %and_select_fusion.refs_2_), custom_call_target="tpu_custom_call" | custom-call | flops 99999997952 | tf_op jit(solution)/shard_map/attend/pallas_call | solution.py:88
  42.0 2.3 after.1
  44.3 3.1 %collective-permute-start.11 = (bf16[200,1024]{1,0:T(8,128)(2,1)}, bf16[200,1024]{1,0:T(8,128)(2,1)}, u32[]{:S(2)}, u32[]{:S(2)}) collective-permute-start(bf16[200,1024]{1,0:T(8,128)(2,1)} %get-tuple-element.122.refs_2_.refs_1_.refs_0_), channel_id=1, source_target_pairs={{0,3},{1,0},{2,1},{3,2},{4,7},{5,4},{6,5},{7,6},{8,11},{9,8},{10,9... | collective-permute-start | bytes 1228808 | tf_op jit(solution)/shard_map/ppermute | solution.py:127
  57.0 3.5 %slope.1 = (bf16[832,1024]{1,0:T(8,128)(2,1)S(1)}, bf16[200,1024]{1,0:T(8,128)(2,1)S(1)}, f32[832,1024]{1,0:T(8,128)S(1)}) custom-call(s32[3]{0:T(128)S(1)} %pad_add_fusion.place_ref, bf16[800,1024]{1,0:T(8,128)(2,1)S(1)} %copy-done.17, bf16[1024,1024]{1,0:T(8,128)(2,1)S(1)} %copy-done.15, bf16[200,1024]{1,0:T(8,128)(2,1)} %get-tuple-element.122.refs_2_.refs_1_.refs_0_), custom_call_target="tpu_custom_call" | custom-call | flops 99999997952 | tf_op jit(solution)/shard_map/slope/pallas_call | solution.py:88
  61.2 23.1 %collective-permute-done.10.refs_2_ = bf16[200,1024]{1,0:T(8,128)(2,1)} collective-permute-done((bf16[200,1024]{1,0:T(8,128)(2,1)}, bf16[200,1024]{1,0:T(8,128)(2,1)}, u32[]{:S(2)}, u32[]{:S(2)}) %collective-permute-start.10) | collective-permute-done | bytes 409632 | tf_op jit(solution)/shard_map/ppermute | solution.py:127
  84.4 9.2 %feed.1 = (bf16[832,1024]{1,0:T(8,128)(2,1)S(1)}, bf16[832,1024]{1,0:T(8,128)(2,1)S(1)}, bf16[832,1024]{1,0:T(8,128)(2,1)S(1)}, f32[1,1024]{1,0:T(1,128)S(1)}, b...) custom-call(s32[3]{0:T(128)S(1)} %pad_add_fusion.place_ref, ...), custom_call_target="tpu_custom_call" | custom-call | flops 99999997952 | tf_op jit(solution)/shard_map/feed/pallas_call | solution.py:88
  97.2 2.5 %second.1 = (bf16[2,200,1024]{2,1,0:T(8,128)(2,1)S(1)}, bf16[2,200,1024]{2,1,0:T(8,128)(2,1)S(1)}) custom-call(s32[3]{0:T(128)S(1)} %pad_add_fusion.place_ref, bf16[832,1024]{1,0:T(8,128)(2,1)S(1)} %get-tuple-element.125.refs_0_, bf16[1024,1024]{1,0:T(8,128)(2,1)S(1)} %copy-done.16), custom_call_target="tpu_custom_call" | custom-call | flops 99999997952 | tf_op jit(solution)/shard_map/second/pallas_call | solution.py:88
  99.7 4.0 %fc2_grad.1 = (f32[4,128,1024]{2,1,0:T(8,128)S(1)}, bf16[4,128,1024]{2,1,0:T(8,128)(2,1)S(1)}) custom-call(s32[3]{0:T(128)S(1)} %pad_add_fusion.place_ref, bf16[832,1024]{1,0:T(8,128)(2,1)S(1)} %get-tuple-element.125.refs_0_, bf16[832,1024]{1,0:T(8,128)(2,1)S(1)} %get-tuple-element.139.refs_1_), custom_call_target="tpu_custom_call" | custom-call | flops 99999997952 | tf_op jit(solution)/shard_map/fc2_grad/pallas_call | solution.py:88
  103.9 3.8 %fc1_grad.1 = (f32[4,128,1024]{2,1,0:T(8,128)S(1)}, bf16[4,128,1024]{2,1,0:T(8,128)(2,1)S(1)}) custom-call(s32[3]{0:T(128)S(1)} %pad_add_fusion.place_ref, bf16[832,1024]{1,0:T(8,128)(2,1)S(1)} %get-tuple-element.132.refs_0_, bf16[832,1024]{1,0:T(8,128)(2,1)S(1)} %get-tuple-element.133.refs_1_), custom_call_target="tpu_custom_call" | custom-call | flops 99999997952 | tf_op jit(solution)/shard_map/fc1_grad/pallas_call | solution.py:88
  112.9 10.0 %collective-permute-done.20.refs_1_ = bf16[2,128,1024]{2,1,0:T(8,128)(2,1)S(1)} collective-permute-done((bf16[2,128,1024]{2,1,0:T(8,128)(2,1)S(1)}, bf16[2,128,1024]{2,1,0:T(8,128)(2,1)S(1)}, u32[]{:S(2)}, u32[]{:S(2)}) %collective-permute-start.20) | collective-permute-done | bytes 524320 | tf_op jit(solution)/shard_map/ppermute | solution.py:122
  127.8 3.0 %collective-permute-done.15.refs_2_ = bf16[200,1024]{1,0:T(8,128)(2,1)} collective-permute-done((bf16[200,1024]{1,0:T(8,128)(2,1)}, bf16[200,1024]{1,0:T(8,128)(2,1)}, u32[]{:S(2)}, u32[]{:S(2)}) %collective-permute-start.15) | collective-permute-done | bytes 409632 | tf_op jit(solution)/shard_map/ppermute | solution.py:127
  130.9 3.1 %back2.1 = (f32[208,1024]{1,0:T(8,128)S(1)}, bf16[200,1024]{1,0:T(8,128)(2,1)S(1)}, bf16[2,200,1024]{2,1,0:T(8,128)(2,1)S(1)}) custom-call(s32[3]{0:T(128)S(1)} %pad_add_fusion.place_ref, bf16[200,1024]{1,0:T(8,128)(2,1)S(1)} %get-tuple-element.127.refs_0_, bf16[200,1024]{1,0:T(8,128)(2,1)} %collective-permute-done.14.refs_1_, ...), custom_call_target="tpu_custom_call", output_to_operand_aliasing={{2}: (13, {})} | custom-call | flops 5000000000 | tf_op jit(solution)/shard_map/back2/pallas_call | solution.py:88
  135.0 9.7 %attend_back.1 = (bf16[200,768]{1,0:T(8,128)(2,1)S(1)}, bf16[200,768]{1,0:T(8,128)(2,1)S(1)}, bf16[200,768]{1,0:T(8,128)(2,1)S(1)}, bf16[200,768]{1,0:T(8,128)(2,1)S(1)}, f32[32,384]{1,0:T(8,128)S(1)}) custom-call(s32[3]{0:T(128)S(1)} %pad_add_fusion.place_ref, bf16[200,3072]{1,0:T(8,128)(2,1)S(1)} %get-tuple-element.115.refs_0_, ...), custom_call_target="tpu_custom_call" | custom-call | flops 5000000000 | tf_op jit(solution)/shard_map/attend_back/pallas_call | solution.py:88
  148.2 5.0 %back1.1 = (bf16[200,1024]{1,0:T(8,128)(2,1)}, f32[5,1024]{1,0:T(8,128)S(1)}) custom-call(s32[3]{0:T(128)S(1)} %pad_add_fusion.place_ref, bf16[200,768]{1,0:T(8,128)(2,1)S(1)} %get-tuple-element.152.refs_0_.refs_4_, bf16[200,768]{1,0:T(8,128)(2,1)S(1)} %get-tuple-element.153.refs_1_, bf16[200,768]{1,0:T(8,128)(2,1)S(1)} %get-tuple-element.154.refs_2_, ...), custom_call_target="tpu_custom_call" | custom-call | flops 20000000000 | tf_op jit(solution)/shard_map/back1/pallas_call | solution.py:88
  153.2 3.9 %back0.1 = (bf16[200,2048]{1,0:T(8,128)(2,1)S(1)}, f32[4,1024]{1,0:T(4,128)S(1)}) custom-call(s32[3]{0:T(128)S(1)} %pad_add_fusion.place_ref, bf16[200,1024]{1,0:T(8,128)(2,1)} %get-tuple-element.157.refs_0_.refs_2_.refs_10_, bf16[200,2048]{1,0:T(8,128)(2,1)S(1)} %bitcast.40, f32[1,2048]{1,0:T(1,128)S(1)} %bitcast.47, bf16[2048,1024]{1,0:T(8,128)(2,1)S(1)} %copy-done.13), custom_call_target="tpu_custom_call" | custom-call | flops 20000000000 | tf_op jit(solution)/shard_map/back0/pallas_call | solution.py:88
  164.7 4.9 %qkv_grad.1 = (f32[4,128,768]{2,1,0:T(8,128)S(1)}, bf16[5,128,768]{2,1,0:T(8,128)(2,1)}) custom-call(s32[3]{0:T(128)S(1)} %pad_add_fusion.place_ref, bf16[200,1024]{1,0:T(8,128)(2,1)} %get-tuple-element.120.refs_0_, bf16[2,200,1024]{2,1,0:T(8,128)(2,1)S(1)} %copy-done.5, bf16[2,200,1024]{2,1,0:T(8,128)(2,1)S(1)} %copy-done.19, ...), custom_call_target="tpu_custom_call" | custom-call | flops 5000000000 | tf_op jit(solution)/shard_map/qkv_grad/pallas_call | solution.py:88
  180.0 5.9 %collective-permute-done.31.refs_7_ = bf16[200,1024]{1,0:T(8,128)(2,1)S(1)} collective-permute-done((bf16[200,1024]{1,0:T(8,128)(2,1)}, bf16[200,1024]{1,0:T(8,128)(2,1)S(1)}, u32[]{:S(2)}, u32[]{:S(2)}) %collective-permute-start.31) | collective-permute-done | bytes 409632 | tf_op jit(solution)/shard_map/ppermute | solution.py:122
  185.9 7.9 %collective-permute-done.30.refs_6_ = bf16[200,1024]{1,0:T(8,128)(2,1)S(1)} collective-permute-done((bf16[200,1024]{1,0:T(8,128)(2,1)}, bf16[200,1024]{1,0:T(8,128)(2,1)S(1)}, u32[]{:S(2)}, u32[]{:S(2)}) %collective-permute-start.30) | collective-permute-done | bytes 409632 | tf_op jit(solution)/shard_map/ppermute | solution.py:122
  193.8 2.6 %merge_grad.1 = (f32[1,256,1024]{2,1,0:T(8,128)S(1)}, bf16[1,256,1024]{2,1,0:T(8,128)(2,1)S(1)}) custom-call(s32[3]{0:T(128)S(1)} %pad_add_fusion.place_ref, bf16[200,512]{1,0:T(8,128)(2,1)S(1)} %copy-done.54, bf16[2,200,512]{2,1,0:T(8,128)(2,1)S(1)} %copy-done.30, bf16[2,200,512]{2,1,0:T(8,128)(2,1)} %collective-permute-done.6.refs_5_.refs_2_, ...), custom_call_target="tpu_custom_call" | custom-call | flops 5000000000 | tf_op jit(solution)/shard_map/merge_grad/pallas_call | solution.py:88
  202.6 2.5 %collective-permute-start.36 = (bf16[2,64,1024]{2,1,0:T(8,128)(2,1)S(1)}, bf16[2,64,1024]{2,1,0:T(8,128)(2,1)S(1)}, u32[]{:S(2)}, u32[]{:S(2)}) collective-permute-start(bf16[2,64,1024]{2,1,0:T(8,128)(2,1)S(1)} %get-tuple-element.180.refs_2_), channel_id=1, source_target_pairs={{0,1},{1,0},{2,3},{3,2},{4,5},{5,4},{6,7},{7,6},{8,9},{9,8},{10,11... | collective-permute-start | bytes 786440 | tf_op jit(solution)/shard_map/ppermute | solution.py:122
  205.1 6.6 %collective-permute-done.41.refs_1_ = bf16[8,32,1024]{2,1,0:T(8,128)(2,1)S(1)} collective-permute-done((bf16[8,32,1024]{2,1,0:T(8,128)(2,1)S(1)}, bf16[8,32,1024]{2,1,0:T(8,128)(2,1)S(1)}, u32[]{:S(2)}, u32[]{:S(2)}) %collective-permute-start.41) | collective-permute-done | bytes 524320 | tf_op jit(solution)/shard_map/ppermute | solution.py:122
  219.8 3.2 %collective-permute-done.42.refs_1_ = bf16[4,32,1024]{2,1,0:T(8,128)(2,1)S(1)} collective-permute-done((bf16[4,32,1024]{2,1,0:T(8,128)(2,1)S(1)}, bf16[4,32,1024]{2,1,0:T(8,128)(2,1)S(1)}, u32[]{:S(2)}, u32[]{:S(2)}) %collective-permute-start.42) | collective-permute-done | bytes 262176 | tf_op jit(solution)/shard_map/ppermute | solution.py:122
  (250 shorter events, 100.0 us)
Async XLA Ops:
  4.0 17.0 %collective-permute-start.2 = (bf16[48,1024]{1,0:T(8,128)(2,1)}, bf16[48,1024]{1,0:T(8,128)(2,1)}, u32[]{:S(2)}, u32[]{:S(2)}) collective-permute-start(bf16[48,1024]{1,0:T(8,128)(2,1)} %pack.1.refs_0_), channel_id=1, source_target_pairs={{0,3},{1,0},{2,1},{3,2},{4,7},{5,4},{6,5},{7,6},{8,11},{9,8},{10,9... | collective-permute-start | bytes 294920 | tf_op jit(solution)/shard_map/ppermute | solution.py:127
  17.9 20.4 %collective-permute-start.6 = (bf16[2,200,512]{2,1,0:T(8,128)(2,1)}, bf16[2,200,512]{2,1,0:T(8,128)(2,1)}, u32[]{:S(2)}, u32[]{:S(2)}) collective-permute-start(bf16[2,200,512]{2,1,0:T(8,128)(2,1)} %get-tuple-element.119), channel_id=1, source_target_pairs={{0,16},{4,20},{8,24},{12,28},{16,0},{20,4},{24,8},{28,12},{1,17},{... | collective-permute-start | bytes 1228808 | tf_op jit(solution)/shard_map/ppermute | solution.py:122
  19.4 18.8 %collective-permute-start.7 = (bf16[200,1024]{1,0:T(8,128)(2,1)}, bf16[200,1024]{1,0:T(8,128)(2,1)}, u32[]{:S(2)}, u32[]{:S(2)}) collective-permute-start(bf16[200,1024]{1,0:T(8,128)(2,1)} %get-tuple-element.120.refs_0_), channel_id=1, source_target_pairs={{0,8},{4,12},{8,0},{12,4},{16,24},{20,28},{24,16},{28,20},{1,9},{5... | collective-permute-start | bytes 1228808 | tf_op jit(solution)/shard_map/ppermute | solution.py:122
  23.2 13.7 %collective-permute-start.4 = (bf16[96,1024]{1,0:T(8,128)(2,1)}, bf16[96,1024]{1,0:T(8,128)(2,1)}, u32[]{:S(2)}, u32[]{:S(2)}) collective-permute-start(bf16[96,1024]{1,0:T(8,128)(2,1)} %pieces.1.refs_0_), channel_id=1, source_target_pairs={{0,16},{4,20},{8,24},{12,28},{16,0},{20,4},{24,8},{28,12},{1,17},{... | collective-permute-start | bytes 589832 | tf_op jit(solution)/shard_map/ppermute | solution.py:122
  44.3 16.9 %collective-permute-start.11 = (bf16[200,1024]{1,0:T(8,128)(2,1)}, bf16[200,1024]{1,0:T(8,128)(2,1)}, u32[]{:S(2)}, u32[]{:S(2)}) collective-permute-start(bf16[200,1024]{1,0:T(8,128)(2,1)} %get-tuple-element.122.refs_2_.refs_1_.refs_0_), channel_id=1, source_target_pairs={{0,3},{1,0},{2,1},{3,2},{4,7},{5,4},{6,5},{7,6},{8,11},{9,8},{10,9... | collective-permute-start | bytes 1228808 | tf_op jit(solution)/shard_map/ppermute | solution.py:127
  47.4 37.0 %collective-permute-start.10 = (bf16[200,1024]{1,0:T(8,128)(2,1)}, bf16[200,1024]{1,0:T(8,128)(2,1)}, u32[]{:S(2)}, u32[]{:S(2)}) collective-permute-start(bf16[200,1024]{1,0:T(8,128)(2,1)} %get-tuple-element.122.refs_2_.refs_1_.refs_0_), channel_id=1, source_target_pairs={{0,2},{1,3},{2,0},{3,1},{4,6},{5,7},{6,4},{7,5},{8,10},{9,11},{10,... | collective-permute-start | bytes 1228808 | tf_op jit(solution)/shard_map/ppermute | solution.py:127
  48.3 36.1 %collective-permute-start.9 = (bf16[200,1024]{1,0:T(8,128)(2,1)}, bf16[200,1024]{1,0:T(8,128)(2,1)}, u32[]{:S(2)}, u32[]{:S(2)}) collective-permute-start(bf16[200,1024]{1,0:T(8,128)(2,1)} %get-tuple-element.122.refs_2_.refs_1_.refs_0_), channel_id=1, source_target_pairs={{0,1},{1,2},{2,3},{3,0},{4,5},{5,6},{6,7},{7,4},{8,9},{9,10},{10,1... | collective-permute-start | bytes 1228808 | tf_op jit(solution)/shard_map/ppermute | solution.py:127
  53.1 31.3 %collective-permute-start.12 = (bf16[2,200,1024]{2,1,0:T(8,128)(2,1)S(1)}, bf16[2,200,1024]{2,1,0:T(8,128)(2,1)S(1)}, u32[]{:S(2)}, u32[]{:S(2)}) collective-permute-start(bf16[2,200,1024]{2,1,0:T(8,128)(2,1)S(1)} %pad_maximum_fusion.refs_1_), channel_id=1, source_target_pairs={{0,16},{4,20},{8,24},{12,28},{16,0},{20,4},{24,8},{28,12},{1,17},{... | collective-permute-start | bytes 2457608 | tf_op jit(solution)/shard_map/ppermute | solution.py:122
  93.6 34.2 %collective-permute-start.14 = (bf16[200,1024]{1,0:T(8,128)(2,1)}, bf16[200,1024]{1,0:T(8,128)(2,1)}, u32[]{:S(2)}, u32[]{:S(2)}) collective-permute-start(bf16[200,1024]{1,0:T(8,128)(2,1)} %get-tuple-element.128), channel_id=1, source_target_pairs={{0,3},{1,0},{2,1},{3,2},{4,7},{5,4},{6,5},{7,6},{8,11},{9,8},{10,9... | collective-permute-start | bytes 1228808 | tf_op jit(solution)/shard_map/ppermute | solution.py:127
  93.7 37.2 %collective-permute-start.15 = (bf16[200,1024]{1,0:T(8,128)(2,1)}, bf16[200,1024]{1,0:T(8,128)(2,1)}, u32[]{:S(2)}, u32[]{:S(2)}) collective-permute-start(bf16[200,1024]{1,0:T(8,128)(2,1)} %get-tuple-element.129), channel_id=1, source_target_pairs={{0,2},{1,3},{2,0},{3,1},{4,6},{5,7},{6,4},{7,5},{8,10},{9,11},{10,... | collective-permute-start | bytes 1228808 | tf_op jit(solution)/shard_map/ppermute | solution.py:127
  95.3 35.6 %collective-permute-start.16 = (bf16[200,1024]{1,0:T(8,128)(2,1)}, bf16[200,1024]{1,0:T(8,128)(2,1)}, u32[]{:S(2)}, u32[]{:S(2)}) collective-permute-start(bf16[200,1024]{1,0:T(8,128)(2,1)} %get-tuple-element.130), channel_id=1, source_target_pairs={{0,1},{1,2},{2,3},{3,0},{4,5},{5,6},{6,7},{7,4},{8,9},{9,10},{10,1... | collective-permute-start | bytes 1228808 | tf_op jit(solution)/shard_map/ppermute | solution.py:127
  109.0 13.9 %collective-permute-start.20 = (bf16[2,128,1024]{2,1,0:T(8,128)(2,1)S(1)}, bf16[2,128,1024]{2,1,0:T(8,128)(2,1)S(1)}, u32[]{:S(2)}, u32[]{:S(2)}) collective-permute-start(bf16[2,128,1024]{2,1,0:T(8,128)(2,1)S(1)} %get-tuple-element.143), channel_id=1, source_target_pairs={{0,16},{4,20},{8,24},{12,28},{16,0},{20,4},{24,8},{28,12},{1,17},{... | collective-permute-start | bytes 1572872 | tf_op jit(solution)/shard_map/ppermute | solution.py:122
  111.4 14.5 %collective-permute-start.18 = (bf16[2,128,1024]{2,1,0:T(8,128)(2,1)S(1)}, bf16[2,128,1024]{2,1,0:T(8,128)(2,1)S(1)}, u32[]{:S(2)}, u32[]{:S(2)}) collective-permute-start(bf16[2,128,1024]{2,1,0:T(8,128)(2,1)S(1)} %get-tuple-element.137), channel_id=1, source_target_pairs={{0,8},{4,12},{8,0},{12,4},{16,24},{20,28},{24,16},{28,20},{1,9},{5... | collective-permute-start | bytes 1572872 | tf_op jit(solution)/shard_map/ppermute | solution.py:122
  134.0 25.4 %collective-permute-start.21 = (bf16[2,200,1024]{2,1,0:T(8,128)(2,1)S(1)}, bf16[2,200,1024]{2,1,0:T(8,128)(2,1)S(1)}, u32[]{:S(2)}, u32[]{:S(2)}) collective-permute-start(bf16[2,200,1024]{2,1,0:T(8,128)(2,1)S(1)} %get-tuple-element.146), channel_id=1, source_target_pairs={{0,1},{1,0},{2,3},{3,2},{4,5},{5,4},{6,7},{7,6},{8,9},{9,8},{10,11... | collective-permute-start | bytes 2457608 | tf_op jit(solution)/shard_map/ppermute | solution.py:122
  144.6 18.2 %collective-permute-start.25 = (bf16[200,768]{1,0:T(8,128)(2,1)S(1)}, bf16[200,768]{1,0:T(8,128)(2,1)S(1)}, u32[]{:S(2)}, u32[]{:S(2)}) collective-permute-start(bf16[200,768]{1,0:T(8,128)(2,1)S(1)} %get-tuple-element.153.refs_1_), channel_id=1, source_target_pairs={{0,8},{4,12},{8,0},{12,4},{16,24},{20,28},{24,16},{28,20},{1,9},{5... | collective-permute-start | bytes 921608 | tf_op jit(solution)/shard_map/ppermute | solution.py:122
  146.2 16.6 %collective-permute-start.26 = (bf16[200,768]{1,0:T(8,128)(2,1)S(1)}, bf16[200,768]{1,0:T(8,128)(2,1)S(1)}, u32[]{:S(2)}, u32[]{:S(2)}) collective-permute-start(bf16[200,768]{1,0:T(8,128)(2,1)S(1)} %get-tuple-element.154.refs_2_), channel_id=1, source_target_pairs={{0,16},{4,20},{8,24},{12,28},{16,0},{20,4},{24,8},{28,12},{1,17},{... | collective-permute-start | bytes 921608 | tf_op jit(solution)/shard_map/ppermute | solution.py:122
  146.6 16.2 %collective-permute-start.27 = (bf16[200,768]{1,0:T(8,128)(2,1)S(1)}, bf16[200,768]{1,0:T(8,128)(2,1)S(1)}, u32[]{:S(2)}, u32[]{:S(2)}) collective-permute-start(bf16[200,768]{1,0:T(8,128)(2,1)S(1)} %get-tuple-element.155.refs_3_), channel_id=1, source_target_pairs={{0,24},{4,28},{8,16},{12,20},{16,8},{20,12},{24,0},{28,4},{1,25},{... | collective-permute-start | bytes 921608 | tf_op jit(solution)/shard_map/ppermute | solution.py:122
  171.0 25.4 %collective-permute-start.22 = (bf16[1,200,1024]{2,1,0:T(8,128)(2,1)}, bf16[1,200,1024]{2,1,0:T(8,128)(2,1)S(1)}, u32[]{:S(2)}, u32[]{:S(2)}) collective-permute-start(bf16[1,200,1024]{2,1,0:T(8,128)(2,1)} %get-tuple-element.148.refs_8_.refs_9_), channel_id=1, source_target_pairs={{0,2},{1,3},{2,0},{3,1},{4,6},{5,7},{6,4},{7,5},{8,10},{9,11},{10,... | collective-permute-start | bytes 1228808 | tf_op jit(solution)/shard_map/ppermute | solution.py:122
  173.8 19.9 %collective-permute-start.30 = (bf16[200,1024]{1,0:T(8,128)(2,1)}, bf16[200,1024]{1,0:T(8,128)(2,1)S(1)}, u32[]{:S(2)}, u32[]{:S(2)}) collective-permute-start(bf16[200,1024]{1,0:T(8,128)(2,1)} %get-tuple-element.165.refs_4_), channel_id=1, source_target_pairs={{0,16},{4,20},{8,24},{12,28},{16,0},{20,4},{24,8},{28,12},{1,17},{... | collective-permute-start | bytes 1228808 | tf_op jit(solution)/shard_map/ppermute | solution.py:122
  175.4 18.4 %collective-permute-start.29 = (bf16[200,1024]{1,0:T(8,128)(2,1)}, bf16[200,1024]{1,0:T(8,128)(2,1)S(1)}, u32[]{:S(2)}, u32[]{:S(2)}) collective-permute-start(bf16[200,1024]{1,0:T(8,128)(2,1)} %get-tuple-element.165.refs_4_), channel_id=1, source_target_pairs={{0,8},{4,12},{8,0},{12,4},{16,24},{20,28},{24,16},{28,20},{1,9},{5... | collective-permute-start | bytes 1228808 | tf_op jit(solution)/shard_map/ppermute | solution.py:122
  178.8 20.5 %collective-permute-start.34 = (bf16[10,32,768]{2,1,0:T(8,128)(2,1)S(1)}, bf16[10,32,768]{2,1,0:T(8,128)(2,1)S(1)}, u32[]{:S(2)}, u32[]{:S(2)}) collective-permute-start(bf16[10,32,768]{2,1,0:T(8,128)(2,1)S(1)} %get-tuple-element.169.refs_8_), channel_id=1, source_target_pairs={{0,1},{1,0},{2,3},{3,2},{4,5},{5,4},{6,7},{7,6},{8,9},{9,8},{10,11... | collective-permute-start | bytes 1474568 | tf_op jit(solution)/shard_map/ppermute | solution.py:122
  197.4 14.3 %collective-permute-start.41 = (bf16[8,32,1024]{2,1,0:T(8,128)(2,1)S(1)}, bf16[8,32,1024]{2,1,0:T(8,128)(2,1)S(1)}, u32[]{:S(2)}, u32[]{:S(2)}) collective-permute-start(bf16[8,32,1024]{2,1,0:T(8,128)(2,1)S(1)} %copy-done.28), channel_id=1, source_target_pairs={{0,8},{4,12},{8,0},{12,4},{16,24},{20,28},{24,16},{28,20},{1,9},{5... | collective-permute-start | bytes 1572872 | tf_op jit(solution)/shard_map/ppermute | solution.py:122
  200.7 24.1 %collective-permute-start.35 = (bf16[6,32,768]{2,1,0:T(8,128)(2,1)S(1)}, bf16[6,32,768]{2,1,0:T(8,128)(2,1)S(1)}, u32[]{:S(2)}, u32[]{:S(2)}) collective-permute-start(bf16[6,32,768]{2,1,0:T(8,128)(2,1)S(1)} %get-tuple-element.174.refs_2_), channel_id=1, source_target_pairs={{0,2},{1,3},{2,0},{3,1},{4,6},{5,7},{6,4},{7,5},{8,10},{9,11},{10,... | collective-permute-start | bytes 884744 | tf_op jit(solution)/shard_map/ppermute | solution.py:122
  202.6 13.9 %collective-permute-start.36 = (bf16[2,64,1024]{2,1,0:T(8,128)(2,1)S(1)}, bf16[2,64,1024]{2,1,0:T(8,128)(2,1)S(1)}, u32[]{:S(2)}, u32[]{:S(2)}) collective-permute-start(bf16[2,64,1024]{2,1,0:T(8,128)(2,1)S(1)} %get-tuple-element.180.refs_2_), channel_id=1, source_target_pairs={{0,1},{1,0},{2,3},{3,2},{4,5},{5,4},{6,7},{7,6},{8,9},{9,8},{10,11... | collective-permute-start | bytes 786440 | tf_op jit(solution)/shard_map/ppermute | solution.py:122
  (84 other events, 608.3 us)
